TPU v7x, 256 devices: a whole 4x4x8 slice. The times are simulated.
256 devices in a mesh: tm: 8 (over z), space: 32 (over y, x, core).
Axes of the slice: x: 4, y: 4, z: 8, core: 2. Of those that a mesh axis runs over, the one named last changes fastest.
Arguments:
- features: bfloat16 [32, 256, 128, 128], P('tm', 'space'), may hold values from -45 to 45
- gain_one: float32 [128], replicated, may hold values from 0.1 to 1.9
- shift_one: float32 [128], replicated, may hold values from -3 to 3
- kernel_one: bfloat16 [3, 3, 3, 128, 128], replicated, may hold values from -0.109375 to 0.109375
- bias_one: float32 [128], replicated, may hold values from -3 to 3
- gain_two: float32 [128], replicated, may hold values from 0.1 to 1.9
- shift_two: float32 [128], replicated, may hold values from -3 to 3
- kernel_two: bfloat16 [3, 3, 3, 128, 128], replicated, may hold values from -0.109375 to 0.109375
- bias_two: float32 [128], replicated, may hold values from -3 to 3
Outputs:
- decoded: float32 [32, 256, 128, 128], P('tm', 'space')
All inputs are finite; a program needn't handle non-finite values.
Results may differ from a plain program's by a relative error of at most 0.0014.
Values may be sent and summed in bfloat16 or wider, within the bound.
No kernel may reach another device: no remote copies, remote signals or barrier semaphores. Data moves between devices by JAX's collectives and lax.ppermute only.
A program may use at most 128 MiB of HBM per device.

v0:
```python
import jax
import jax.numpy as jnp
from jax import lax
from jax.sharding import PartitionSpec as P

GROUPS = 32


EPS = 1e-06


def shifted(value, axis, by):
    devices = lax.axis_size(axis)
    pairs = [(i, i + by) for i in range(devices) if 0 <= i + by < devices]
    return lax.ppermute(value, axis, pairs)


def padded_2(cells, sides, width):
    for axis, dim in sides:
        count = lax.axis_size(axis)
        ends = count - 1
        head = lax.slice_in_dim(cells, 0, width, axis=dim)
        tail = lax.slice_in_dim(cells, cells.shape[dim] - width, cells.shape[dim], axis=dim)
        cells = jnp.concatenate(
            [
                lax.ppermute(tail, axis, [(i, (i + 1) % count) for i in range(ends)]),
                cells,
                lax.ppermute(head, axis, [((i + 1) % count, i) for i in range(ends)]),
            ],
            axis=dim,
        )
    return cells


def group_stats(part, groups):
    values = part.astype(jnp.float32)
    width = values.shape[-1]
    members = width // groups
    count = (
        values.shape[0]
        * values.shape[1]
        * values.shape[2]
        * members
        * lax.axis_size("tm")
        * lax.axis_size("space")
    )
    grouped = values.reshape(values.shape[:-1] + (groups, members))
    local_sum = jnp.sum(grouped, axis=(0, 1, 2, 4))
    mean = lax.psum(local_sum, ("tm", "space")) / count
    deviation = grouped - mean[:, None]
    local_spread = jnp.sum(deviation * deviation, axis=(0, 1, 2, 4))
    var = lax.psum(local_spread, ("tm", "space")) / count
    return (mean, lax.rsqrt(var + EPS))


def apply_norm(field, mean, scale, gain, shift):
    values = field.astype(jnp.float32)
    width = values.shape[-1]
    groups = mean.shape[0]
    grouped = values.reshape(values.shape[:-1] + (groups, width // groups))
    normed = ((grouped - mean[:, None]) * scale[:, None]).reshape(values.shape)
    return jax.nn.silu(normed * gain + shift).astype(jnp.bfloat16)


def earlier_frames(field, count):
    tail = field[field.shape[0] - count :]
    carried = shifted(tail, "tm", 1)
    repeated = jnp.broadcast_to(field[:1], carried.shape)
    return jnp.where(lax.axis_index("tm") == 0, repeated, carried)


def causal_conv(extended, kernel, bias):
    frames = extended.shape[0] - 2
    rows = extended.shape[1]
    cols = extended.shape[2]
    width = extended.shape[3]
    rimmed = padded_2(extended, (("space", 1),), 1)
    padded = jnp.pad(rimmed, ((0, 0), (0, 0), (1, 1), (0, 0)))
    total = jnp.zeros((frames * rows * cols, width), jnp.float32)
    for step_t in range(3):
        slab = padded[step_t : step_t + frames]
        pieces = []
        for step_r in range(3):
            for step_c in range(3):
                pieces.append(slab[:, step_r : step_r + rows, step_c : step_c + cols, :])
        patches = jnp.concatenate(pieces, axis=-1).reshape(frames * rows * cols, 9 * width)
        taps = kernel[step_t].reshape(9 * width, width)
        total = total + jnp.dot(patches, taps, preferred_element_type=jnp.float32)
    return total.reshape(frames, rows, cols, width) + bias


def shards(
    features, gain_one, shift_one, kernel_one, bias_one, gain_two, shift_two, kernel_two, bias_two
):
    mean_one, scale_one = group_stats(features, GROUPS)
    first = apply_norm(features, mean_one, scale_one, gain_one, shift_one)
    inner = causal_conv(
        jnp.concatenate([earlier_frames(first, 2), first], axis=0), kernel_one, bias_one
    )
    mean_two, scale_two = group_stats(inner, GROUPS)
    second = apply_norm(inner, mean_two, scale_two, gain_two, shift_two)
    carried = earlier_frames(second, 2)
    outer = causal_conv(jnp.concatenate([carried, second], axis=0), kernel_two, bias_two)
    return features.astype(jnp.float32) + outer


def solution(mesh):
    placed = (P("tm", "space", None, None), P(), P(), P(), P(), P(), P(), P(), P())
    return jax.shard_map(
        shards, mesh=mesh, in_specs=placed, out_specs=P("tm", "space", None, None), check_vma=False
    )
```

profile of v0, /device:TPU:1, one launch (start us, length us, event | category | flops | bytes accessed | tf_op | source)
XLA Modules:
  0.0 409.0 jit_solution(588084766954603079)
XLA Ops:
  0.0 1.9 convert_reduce_fusion
  2.1 81.4 %psum.28 = f32[32]{0:T(128)S(1)} all-reduce(f32[32]{0:T(128)S(1)} %reduce_sum.51), channel_id=1, replica_groups=mesh['tm'=8,'space'=32] {'tm','space'}, use_global_device_ids=true, to_apply=%region_2.0 | all-reduce | flops 32 | bytes 256 | tf_op jit(solution)/shard_map/psum | solution.py:49
  83.7 1.8 fusion.3
  85.7 72.4 %psum.29 = f32[32]{0:T(128)S(1)} all-reduce(f32[32]{0:T(128)S(1)} %reduce_sum.54), channel_id=1, replica_groups=mesh['tm'=8,'space'=32] {'tm','space'}, use_global_device_ids=true, to_apply=%region_5.6 | all-reduce | flops 32 | bytes 256 | tf_op jit(solution)/shard_map/psum | solution.py:52
  158.3 2.0 fusion.11
  160.3 3.7 collective-permute-start
  164.1 10.5 %collective-permute-done = bf16[2,8,128,128]{3,2,1,0:T(8,128)(2,1)S(1)} collective-permute-done((bf16[2,8,128,128]{3,2,1,0:T(8,128)(2,1)S(1)}, bf16[2,8,128,128]{3,2,1,0:T(8,128)(2,1)S(1)}, u32[]{:S(2)}, u32[]{:S(2)}) %collective-permute-start) | collective-permute-done | bytes 524320 | tf_op jit(solution)/shard_map/ppermute | solution.py:15
  174.7 3.7 collective-permute-start.1
  178.4 1.9 collective-permute-start.2
  181.0 4.4 %collective-permute-done.2 = bf16[6,1,128,128]{3,2,1,0:T(8,128)(2,1)S(1)} collective-permute-done((bf16[6,1,128,128]{3,2,1,0:T(8,128)(2,1)S(1)}, bf16[6,1,128,128]{3,2,1,0:T(8,128)(2,1)S(1)}, u32[]{:S(2)}, u32[]{:S(2)}) %collective-permute-start.2) | collective-permute-done | bytes 196640 | tf_op jit(solution)/shard_map/ppermute | solution.py:28
  185.4 1.3 fusion.19
  189.4 1.3 slice_dynamic-update-slice_fusion.29
  193.3 1.3 slice_dynamic-update-slice_fusion.27
  197.2 1.3 slice_dynamic-update-slice_fusion.24
  198.5 2.7 fusion.30
  201.2 3.0 convolution_add_fusion.3
  204.2 2.7 add_reduce_fusion
  207.2 77.0 %psum.30 = f32[32]{0:T(128)S(1)} all-reduce(f32[32]{0:T(128)S(1)} %reduce_sum.72), channel_id=1, replica_groups=mesh['tm'=8,'space'=32] {'tm','space'}, use_global_device_ids=true, to_apply=%region_8.9 | all-reduce | flops 32 | bytes 256 | tf_op jit(solution)/shard_map/psum | solution.py:49
  285.1 74.3 %psum.31 = f32[32]{0:T(128)S(1)} all-reduce(f32[32]{0:T(128)S(1)} %reduce_sum.75), channel_id=1, replica_groups=mesh['tm'=8,'space'=32] {'tm','space'}, use_global_device_ids=true, to_apply=%region_11.12 | all-reduce | flops 32 | bytes 256 | tf_op jit(solution)/shard_map/psum | solution.py:52
  360.5 2.8 collective-permute-start.3
  363.3 10.5 %collective-permute-done.3 = bf16[2,8,128,128]{3,2,1,0:T(8,128)(2,1)S(1)} collective-permute-done((bf16[2,8,128,128]{3,2,1,0:T(8,128)(2,1)S(1)}, bf16[2,8,128,128]{3,2,1,0:T(8,128)(2,1)S(1)}, u32[]{:S(2)}, u32[]{:S(2)}) %collective-permute-start.3) | collective-permute-done | bytes 524320 | tf_op jit(solution)/shard_map/ppermute | solution.py:15
  373.9 4.3 %collective-permute-start.4 = (bf16[6,1,128,128]{3,2,1,0:T(8,128)(2,1)S(1)}, bf16[6,1,128,128]{3,2,1,0:T(8,128)(2,1)S(1)}, u32[]{:S(2)}, u32[]{:S(2)}) collective-permute-start(bf16[6,1,128,128]{3,2,1,0:T(8,128)(2,1)S(1)} %get-tuple-element.57), channel_id=1, source_target_pairs={{0,1},{1,2},{2,3},{3,4},{4,5},{5,6},{6,7},{7,8},{8,9},{9,10},{10,1... | collective-permute-start | bytes 589832 | tf_op jit(solution)/shard_map/ppermute | solution.py:26
  378.2 1.9 collective-permute-start.5
  380.8 4.4 %collective-permute-done.5 = bf16[6,1,128,128]{3,2,1,0:T(8,128)(2,1)S(1)} collective-permute-done((bf16[6,1,128,128]{3,2,1,0:T(8,128)(2,1)S(1)}, bf16[6,1,128,128]{3,2,1,0:T(8,128)(2,1)S(1)}, u32[]{:S(2)}, u32[]{:S(2)}) %collective-permute-start.5) | collective-permute-done | bytes 196640 | tf_op jit(solution)/shard_map/ppermute | solution.py:28
  385.2 1.3 select_maximum_fusion
  389.5 1.3 slice_dynamic-update-slice_fusion.5
  393.3 1.3 slice_dynamic-update-slice_fusion.3
  397.2 1.3 slice_dynamic-update-slice_fusion
  398.6 2.7 fusion.31
  401.3 3.1 convolution_add_fusion.1
  404.4 2.7 convolution_add_fusion
  407.2 1.6 convert_add_fusion
  (62 shorter events, 20.1 us)
Async XLA Ops:
  0.0 180.3 %copy-start.1 = (bf16[3,3,3,128,128]{4,3,2,1,0:T(8,128)(2,1)S(1)}, bf16[3,3,3,128,128]{4,3,2,1,0:T(8,128)(2,1)}, u32[]{:S(2)}) copy-start(bf16[3,3,3,128,128]{4,3,2,1,0:T(8,128)(2,1)} %param.12) | copy-start | bytes 2654212
  160.3 14.3 %collective-permute-start = (bf16[2,8,128,128]{3,2,1,0:T(8,128)(2,1)S(1)}, bf16[2,8,128,128]{3,2,1,0:T(8,128)(2,1)S(1)}, u32[]{:S(2)}, u32[]{:S(2)}) collective-permute-start(bf16[2,8,128,128]{3,2,1,0:T(8,128)(2,1)S(1)} %slice.363), channel_id=1, source_target_pairs={{0,32},{32,64},{64,96},{96,128},{128,160},{160,192},{192,224},{1,3... | collective-permute-start | bytes 1572872 | tf_op jit(solution)/shard_map/ppermute | solution.py:15
  174.7 6.3 %collective-permute-start.1 = (bf16[6,1,128,128]{3,2,1,0:T(8,128)(2,1)S(1)}, bf16[6,1,128,128]{3,2,1,0:T(8,128)(2,1)S(1)}, u32[]{:S(2)}, u32[]{:S(2)}) collective-permute-start(bf16[6,1,128,128]{3,2,1,0:T(8,128)(2,1)S(1)} %get-tuple-element.63), channel_id=1, source_target_pairs={{0,1},{1,2},{2,3},{3,4},{4,5},{5,6},{6,7},{7,8},{8,9},{9,10},{10,1... | collective-permute-start | bytes 589832 | tf_op jit(solution)/shard_map/ppermute | solution.py:26
  178.4 7.0 %collective-permute-start.2 = (bf16[6,1,128,128]{3,2,1,0:T(8,128)(2,1)S(1)}, bf16[6,1,128,128]{3,2,1,0:T(8,128)(2,1)S(1)}, u32[]{:S(2)}, u32[]{:S(2)}) collective-permute-start(bf16[6,1,128,128]{3,2,1,0:T(8,128)(2,1)S(1)} %get-tuple-element.64), channel_id=1, source_target_pairs={{1,0},{2,1},{3,2},{4,3},{5,4},{6,5},{7,6},{8,7},{9,8},{10,9},{11,1... | collective-permute-start | bytes 589832 | tf_op jit(solution)/shard_map/ppermute | solution.py:28
  201.2 3.0 copy-start.3
  204.2 155.5 %copy-start.4 = (f32[128]{0:T(128)S(1)}, f32[128]{0:T(128)}, u32[]{:S(2)}) copy-start(f32[128]{0:T(128)} %param.15) | copy-start | bytes 1540
  204.2 155.5 %copy-start.5 = (f32[128]{0:T(128)S(1)}, f32[128]{0:T(128)}, u32[]{:S(2)}) copy-start(f32[128]{0:T(128)} %param.14) | copy-start | bytes 1540
  207.0 173.2 %copy-start.2 = (bf16[3,3,3,128,128]{4,3,2,1,0:T(8,128)(2,1)S(1)}, bf16[3,3,3,128,128]{4,3,2,1,0:T(8,128)(2,1)}, u32[]{:S(2)}) copy-start(bf16[3,3,3,128,128]{4,3,2,1,0:T(8,128)(2,1)} %param.16) | copy-start | bytes 2654212
  360.5 13.3 %collective-permute-start.3 = (bf16[2,8,128,128]{3,2,1,0:T(8,128)(2,1)S(1)}, bf16[2,8,128,128]{3,2,1,0:T(8,128)(2,1)S(1)}, u32[]{:S(2)}, u32[]{:S(2)}) collective-permute-start(bf16[2,8,128,128]{3,2,1,0:T(8,128)(2,1)S(1)} %slice.391), channel_id=1, source_target_pairs={{0,32},{32,64},{64,96},{96,128},{128,160},{160,192},{192,224},{1,3... | collective-permute-start | bytes 1572872 | tf_op jit(solution)/shard_map/ppermute | solution.py:15
  373.9 6.9 %collective-permute-start.4 = (bf16[6,1,128,128]{3,2,1,0:T(8,128)(2,1)S(1)}, bf16[6,1,128,128]{3,2,1,0:T(8,128)(2,1)S(1)}, u32[]{:S(2)}, u32[]{:S(2)}) collective-permute-start(bf16[6,1,128,128]{3,2,1,0:T(8,128)(2,1)S(1)} %get-tuple-element.57), channel_id=1, source_target_pairs={{0,1},{1,2},{2,3},{3,4},{4,5},{5,6},{6,7},{7,8},{8,9},{9,10},{10,1... | collective-permute-start | bytes 589832 | tf_op jit(solution)/shard_map/ppermute | solution.py:26
  378.2 7.0 %collective-permute-start.5 = (bf16[6,1,128,128]{3,2,1,0:T(8,128)(2,1)S(1)}, bf16[6,1,128,128]{3,2,1,0:T(8,128)(2,1)S(1)}, u32[]{:S(2)}, u32[]{:S(2)}) collective-permute-start(bf16[6,1,128,128]{3,2,1,0:T(8,128)(2,1)S(1)} %get-tuple-element.58), channel_id=1, source_target_pairs={{1,0},{2,1},{3,2},{4,3},{5,4},{6,5},{7,6},{8,7},{9,8},{10,9},{11,1... | collective-permute-start | bytes 589832 | tf_op jit(solution)/shard_map/ppermute | solution.py:28
  404.4 2.8 copy-start
  404.4 2.8 copy-start.6
where the time goes:
time: 416 us; the launch traced here: 409 us
  blocking collectives  305 us (73%)
  waiting for transfers between devices  31 us (7%)
  local copies, waits for them, and re-layouts  21 us (5%)
  starting transfers between devices  18.3 us (4%)
  matrix products  16.9 us (4%)
  other arithmetic  16 us (4%)
    psum x2, blocking collectives, group_stats(): mean = lax.psum(local_sum, ('tm', 'space')) / count  158 us
    psum x2, blocking collectives, group_stats(): var = lax.psum(local_spread, ('tm', 'space')) / count  147 us
    ppermute x2, waiting for transfers between devices, shifted(): return lax.ppermute(value, axis, pairs)  21 us
    unnamed x28, local copies, waits for them, and re-layouts  17 us
    dot_general x6, matrix products, causal_conv(): total = total + jnp.dot(patches, taps, preferred_element_type=jnp.float32)  16.9 us
    ppermute x2, waiting for transfers between devices, padded_2(): lax.ppermute(head, axis, [((i + 1) % count, i) for i in range(ends)])  8.79 us
  transfers between devices with their start and end apart: 6, of which 6 were waited for; matrix products, arithmetic and copies ran while one was open for 0% of the time, Pallas kernels for 0%

commit v1 on v0

v1 whole, which is shorter than its diff:
```python
import functools

import jax
import jax.numpy as jnp
from jax import lax
from jax.experimental import pallas as pl
from jax.experimental.pallas import tpu as pltpu
from jax.sharding import PartitionSpec as P

EPS = 1e-06
MEMBERS = 4
BOTH = ("tm", "space")
F32 = jnp.float32
BF16 = jnp.bfloat16


def lane_of(shape):
    return lax.broadcasted_iota(jnp.int32, shape, len(shape) - 1)


def group_sum(v):
    lane = lane_of(v.shape)
    width = v.shape[-1]
    axis = v.ndim - 1
    v = v + jnp.where((lane & 1) == 1, pltpu.roll(v, 1, axis), pltpu.roll(v, width - 1, axis))
    return v + jnp.where((lane & 2) == 2, pltpu.roll(v, 2, axis), pltpu.roll(v, width - 2, axis))


def column_sum(v):
    return jnp.broadcast_to(jnp.sum(v, axis=0, keepdims=True), (8, v.shape[1]))


def local_stats(load, rows, cells):
    def add(i, total):
        return total + load(i)

    zero = jnp.zeros((128, 128), F32)
    mean = group_sum(column_sum(lax.fori_loop(0, rows, add, zero, unroll=4))) / cells

    def spread(i, total):
        d = load(i) - mean[:1]
        return total + d * d

    return mean, group_sum(column_sum(lax.fori_loop(0, rows, spread, zero, unroll=4)))


def payload(mean, spread, extra):
    place = lane_of(mean.shape) & 3
    return jnp.where(place == 0, mean, jnp.where(place == 1, spread, jnp.where(place == 2, extra, 0.0)))


def pick(rows, place):
    return group_sum(jnp.where((lane_of(rows.shape) & 3) == place, rows, 0.0))


def whole_stats(got_ref, cells):
    got = got_ref[...]
    devices = got.shape[0]
    place = lane_of(got.shape) & 3
    means = jnp.where(place == 0, got, 0.0)
    mean = group_sum(column_sum(means)) / devices
    spread = group_sum(column_sum(jnp.where(place == 1, got, 0.0)))
    off = jnp.where(place == 0, got - mean[:1], 0.0)
    between = group_sum(column_sum(off * off))
    var = (spread + between * cells) / (cells * devices)
    return mean, lax.rsqrt(var + EPS)


def put_act(x, mean, slope, half_shift, keep, out, f, r):
    h = (x - mean) * slope + half_shift
    y = h + h * jnp.tanh(h)
    if keep is not None:
        y = y * keep
    row = lax.broadcasted_iota(jnp.int32, y.shape, 0)
    out[0, f, r] = jnp.where(row == 0, 0.0, pltpu.roll(y, 1, 0)).astype(BF16)
    out[1, f, r] = y.astype(BF16)
    out[2, f, r] = jnp.where(row == 127, 0.0, pltpu.roll(y, 127, 0)).astype(BF16)


def build_taps(kernel_ref, taps):
    zero = jnp.zeros((9 * 128, 128), BF16)
    for f in range(4):
        at = pl.ds(f * 9 * 128, 9 * 128)
        taps[at, :128] = kernel_ref[f] if f < 3 else zero
        taps[at, 128:] = kernel_ref[f - 1] if f > 0 else zero


def conv_rows(acts, taps, r, count):
    pieces = []
    for f in range(4):
        for i in range(3):
            for j in range(3):
                pieces.append(acts[j, f, pl.ds(r + i, count)].reshape(count * 128, 128))
    return jnp.dot(jnp.concatenate(pieces, axis=-1), taps[...], preferred_element_type=F32)


def stats_kernel(x_ref, out_ref):
    rows = x_ref.shape[0] * x_ref.shape[1]
    per = x_ref.shape[1]
    load = lambda i: x_ref[i // per, i % per].astype(F32)
    mean, spread = local_stats(load, rows, float(rows * 128 * MEMBERS))
    out_ref[...] = jnp.broadcast_to(payload(mean, spread, mean)[:1], out_ref.shape)


def norm_constants(got_ref, gain_ref, shift_ref, cells):
    mean, scale = whole_stats(got_ref, cells)
    return mean[:1], scale[:1] * gain_ref[...] * 0.5, shift_ref[...] * 0.5


def first_kernel(early, cells, rc, place_ref, got_ref, gain_ref, shift_ref, kernel_ref, bias_ref, *refs):
    if early:
        x_ref, up_ref, down_ref, z_ref, zup_ref, zdown_ref, prev_ref, inner_ref, pay_ref, acts, taps = refs
    else:
        x_ref, up_ref, down_ref, inner_ref, part_ref, send_ref, acts, taps = refs
    mean, slope, half = norm_constants(got_ref, gain_ref, shift_ref, cells)
    build_taps(kernel_ref, taps)
    top = jnp.where(place_ref[1] == 0, 0.0, 1.0)
    bottom = jnp.where(place_ref[2] == 0, 0.0, 1.0)

    def frame(src, up, down, f_src, f):
        for r in range(2):
            put_act(up[f_src, r].astype(F32), mean, slope, half, top, acts, f, r)
            put_act(down[f_src, r].astype(F32), mean, slope, half, bottom, acts, f, 10 + r)

        def own(r, c):
            put_act(src[f_src, r].astype(F32), mean, slope, half, None, acts, f, 2 + r)
            return c

        lax.fori_loop(0, 8, own, 0, unroll=4)

    if early:
        for f in range(2):
            frame(x_ref, up_ref, down_ref, f, 2 + f)

        @pl.when(place_ref[0] == 0)
        def _():
            for f in range(2):
                for j in range(3):
                    acts[j, f] = acts[j, 2]

        @pl.when(place_ref[0] != 0)
        def _():
            for f in range(2):
                frame(z_ref, zup_ref, zdown_ref, f, f)
    else:
        for f in range(4):
            frame(x_ref, up_ref, down_ref, f, f)

    def rows(i, c):
        r = i * rc
        got = conv_rows(acts, taps, r, rc)
        for o in range(2):
            inner_ref[o, pl.ds(r, rc)] = (got[:, o * 128 : (o + 1) * 128] + bias_ref[...]).reshape(rc, 128, 128)
        return c

    lax.fori_loop(0, 10 // rc, rows, 0)
    half_cells = cells / 2
    load = lambda i: inner_ref[i // 8, 1 + i % 8]
    m, s = local_stats(load, 16, half_cells)
    if early:
        m_late, s_late = prev_ref[0], prev_ref[1]
        both = (m + m_late) * 0.5
        gap = m - m_late
        pay = payload(both, s + s_late + gap * gap * (half_cells / 2), m_late)
        pay_ref[...] = jnp.broadcast_to(pay[:1], pay_ref.shape)
    else:
        part_ref[0] = m
        part_ref[1] = s
        for o in range(2):
            send_ref[o] = (inner_ref[o] - m[:1]).astype(BF16)


def second_kernel(early, cells, rc, place_ref, got_ref, gain_ref, shift_ref, kernel_ref, bias_ref, *refs):
    if early:
        b_ref, z_ref, feat_ref, _, out_ref, acts, taps = refs
    else:
        b_ref, a_ref, feat_ref, out_ref, acts, taps = refs
    mean, slope, half = norm_constants(got_ref, gain_ref, shift_ref, cells)
    build_taps(kernel_ref, taps)
    top = jnp.where(place_ref[1] == 0, 0.0, 1.0)
    bottom = jnp.where(place_ref[2] == 0, 0.0, 1.0)

    def frame(src, f_src, f, base):
        put_act(src[f_src, 0].astype(F32), base, slope, half, top, acts, f, 0)
        put_act(src[f_src, 9].astype(F32), base, slope, half, bottom, acts, f, 9)

        def own(r, c):
            put_act(src[f_src, r].astype(F32), base, slope, half, None, acts, f, r)
            return c

        lax.fori_loop(1, 9, own, 0, unroll=4)

    if early:
        for f in range(2):
            frame(b_ref, f, 2 + f, mean)

        @pl.when(place_ref[0] == 0)
        def _():
            for f in range(2):
                for j in range(3):
                    acts[j, f] = acts[j, 2]

        @pl.when(place_ref[0] != 0)
        def _():
            sender = got_ref[pl.ds(place_ref[3], 1)]
            base = mean - pick(jnp.broadcast_to(sender, (8, 128)), 2)[:1]
            for f in range(2):
                frame(z_ref, f, f, base)
    else:
        for f in range(2):
            frame(b_ref, f, f, mean)
            frame(a_ref, f, 2 + f, mean)

    def rows(i, c):
        r = i * rc
        got = conv_rows(acts, taps, r, rc)
        for o in range(2):
            add = feat_ref[o, pl.ds(r, rc)].astype(F32)
            out_ref[o, pl.ds(r, rc)] = add + (got[:, o * 128 : (o + 1) * 128] + bias_ref[...]).reshape(rc, 128, 128)
        return c

    lax.fori_loop(0, 8 // rc, rows, 0)


VMEM = pl.BlockSpec(memory_space=pltpu.VMEM)
SMEM = pl.BlockSpec(memory_space=pltpu.SMEM)
PARAMS = pltpu.CompilerParams(vmem_limit_bytes=48 * 1024 * 1024)


def scratch(rows):
    return [pltpu.VMEM((3, 4, rows, 128, 128), BF16), pltpu.VMEM((36 * 128, 256), BF16)]


def cost(rows):
    return pl.CostEstimate(flops=2 * 2 * rows * 128 * 36 * 128 * 128, bytes_accessed=4 << 20, transcendentals=4 * rows * 128 * 128)


def shape(dims, dtype):
    return jax.ShapeDtypeStruct(dims, dtype)


def shards(features, gain_one, shift_one, kernel_one, bias_one, gain_two, shift_two, kernel_two, bias_two):
    slabs = lax.axis_size("tm")
    strips = lax.axis_size("space")
    tm = lax.axis_index("tm")
    space = lax.axis_index("space")
    devices = slabs * strips
    cells = float(4 * 8 * 128 * MEMBERS)
    before = jnp.maximum(tm - 1, 0) * strips + space
    place = jnp.stack([tm, space, strips - 1 - space, before]).astype(jnp.int32)
    down_pairs = [(i, i + 1) for i in range(strips - 1)]
    up_pairs = [(i + 1, i) for i in range(strips - 1)]
    later = [(i, i + 1) for i in range(slabs - 1)]
    row = lambda v: v.reshape(1, 128)
    taps_one = kernel_one.reshape(3, 9 * 128, 128)
    taps_two = kernel_two.reshape(3, 9 * 128, 128)

    z_one = lax.ppermute(features[2:], "tm", later)
    up = lax.ppermute(features[:, 6:], "space", down_pairs)
    down = lax.ppermute(features[:, :2], "space", up_pairs)
    pay = pl.pallas_call(
        stats_kernel, out_shape=shape((devices, 128), F32), in_specs=[VMEM], out_specs=VMEM,
        cost_estimate=pl.CostEstimate(flops=1 << 22, bytes_accessed=1 << 20, transcendentals=0), name="stats",
    )(features)
    got = lax.all_to_all(pay, BOTH, 0, 0)
    z_up = lax.ppermute(z_one[:, 6:], "space", down_pairs)
    z_down = lax.ppermute(z_one[:, :2], "space", up_pairs)
    head = (place, got, row(gain_one), row(shift_one), taps_one, row(bias_one))
    inner_a, part, send = pl.pallas_call(
        functools.partial(first_kernel, False, cells, 2),
        out_shape=[shape((2, 10, 128, 128), F32), shape((2, 8, 128), F32), shape((2, 10, 128, 128), BF16)],
        in_specs=[SMEM] + [VMEM] * 8, out_specs=[VMEM] * 3, scratch_shapes=scratch(12),
        compiler_params=PARAMS, cost_estimate=cost(10), name="first_late",
    )(*head, features, up, down)
    z_two = lax.ppermute(send, "tm", later)
    inner_b, pay = pl.pallas_call(
        functools.partial(first_kernel, True, cells, 2),
        out_shape=[shape((2, 10, 128, 128), F32), shape((devices, 128), F32)],
        in_specs=[SMEM] + [VMEM] * 12, out_specs=[VMEM] * 2, scratch_shapes=scratch(12),
        compiler_params=PARAMS, cost_estimate=cost(10), name="first_early",
    )(*head, features, up, down, z_one, z_up, z_down, part)
    got = lax.all_to_all(pay, BOTH, 0, 0)
    head = (place, got, row(gain_two), row(shift_two), taps_two, row(bias_two))
    block = lambda k: pl.BlockSpec((2, 8, 128, 128), lambda *_: (k, 0, 0, 0))
    out = pl.pallas_call(
        functools.partial(second_kernel, False, cells, 2), grid=(1,),
        out_shape=shape((4, 8, 128, 128), F32),
        in_specs=[SMEM] + [VMEM] * 7 + [block(1)], out_specs=block(1), scratch_shapes=scratch(10),
        compiler_params=PARAMS, cost_estimate=cost(8), name="second_late",
    )(*head, inner_b, inner_a, features)
    return pl.pallas_call(
        functools.partial(second_kernel, True, cells, 2), grid=(1,),
        out_shape=shape((4, 8, 128, 128), F32),
        in_specs=[SMEM] + [VMEM] * 7 + [block(0), pl.BlockSpec(memory_space=pl.ANY)], out_specs=block(0),
        scratch_shapes=scratch(10), input_output_aliases={9: 0},
        compiler_params=PARAMS, cost_estimate=cost(8), name="second_early",
    )(*head, inner_b, z_two, features, out)


def solution(mesh):
    placed = (P("tm", "space", None, None), P(), P(), P(), P(), P(), P(), P(), P())
    return jax.shard_map(
        shards, mesh=mesh, in_specs=placed, out_specs=P("tm", "space", None, None), check_vma=False
    )
```

time: 416 us -> 95.8 us (0.23); the launches traced: 409 us -> 95.4 us
  blocking collectives: 305 us -> 29.8 us
  waiting for transfers between devices: 31 us -> 0.02 us
  Pallas kernels: 0 us -> 28.6 us
  local copies, waits for them, and re-layouts: 21 us -> 3.57 us
  matrix products: 16.9 us -> 0 us
  other arithmetic: 16 us -> 0.08 us
  starting transfers between devices: 18.3 us -> 33.1 us
    psum x4 -> x0, blocking collectives: 305 us -> none  [the longest x2 158 us: group_stats(): mean = lax.psum(local_sum, ('tm', 'space')) / count]
    ppermute x6, waiting for transfers between devices: 31 us -> 0.02 us  [the longest x1 0.01 us: shards(): down = lax.ppermute(features[:, :2], 'space', up_pairs)]
    all_to_all x0 -> x1, blocking collectives: none -> 29.8 us  [shards(): got = lax.all_to_all(pay, BOTH, 0, 0)]
    pallas_call x0 -> x5, Pallas kernels: none -> 28.6 us  [the longest x1 7.06 us: shards(): pl.pallas_call(functools.partial(first_kernel, False, cells, 2), out_shap...]
    unnamed x28 -> x18, local copies, waits for them, and re-layouts: 17 us -> 0.04 us
    dot_general x6 -> x0, matrix products: 16.9 us -> none  [causal_conv(): total = total + jnp.dot(patches, taps, preferred_element_type=jnp.float32)]
    all_to_all x0 -> x1, starting transfers between devices: none -> 14.2 us  [shards(): got = lax.all_to_all(pay, BOTH, 0, 0)]
    reduce_sum x7 -> x0, other arithmetic: 4.66 us -> none  [the longest x4 2.57 us: group_stats(): local_spread = jnp.sum(deviation * deviation, axis=(0, 1, 2, 4))]
  transfers between devices with their start and end apart: 6 -> 7, of which waited for: 6 -> 0; matrix products, arithmetic and copies ran while one was open for 0% -> 2% of each run, Pallas kernels for 0% -> 24%
where the time goes in v1:
time: 95.8 us; the launch traced here: 95.4 us
  starting transfers between devices  33.1 us (35%)
  blocking collectives  29.8 us (31%)
  Pallas kernels  28.6 us (30%)
  local copies, waits for them, and re-layouts  3.57 us (4%)
    all_to_all x1, blocking collectives, shards(): got = lax.all_to_all(pay, BOTH, 0, 0)  29.8 us
    all_to_all x1, starting transfers between devices, shards(): got = lax.all_to_all(pay, BOTH, 0, 0)  14.2 us
    pallas_call x1, Pallas kernels, shards(): pl.pallas_call(functools.partial(first_kernel, False, cells, 2), out_shap...  7.06 us
    pallas_call x1, Pallas kernels, shards(): pl.pallas_call(functools.partial(first_kernel, True, cells, 2), out_shape...  6.52 us
    pallas_call x1, Pallas kernels, shards(): pl.pallas_call(functools.partial(second_kernel, False, cells, 2), grid=(1...  6.3 us
    pallas_call x1, Pallas kernels, shards(): pl.pallas_call(functools.partial(second_kernel, True, cells, 2), grid=(1,...  5.93 us
    ppermute x1, starting transfers between devices, shards(): z_one = lax.ppermute(features[2:], 'tm', later)  4.39 us
    ppermute x1, starting transfers between devices, shards(): down = lax.ppermute(features[:, :2], 'space', up_pairs)  4.04 us
  transfers between devices with their start and end apart: 7, of which 0 were waited for; matrix products, arithmetic and copies ran while one was open for 2% of the time, Pallas kernels for 24%

profile of v1, /device:TPU:1, one launch (start us, length us, event | category | flops | bytes accessed | tf_op | source)
XLA Modules:
  0.0 95.4 jit_solution(5813118972295537716)
XLA Ops:
  0.0 0.0 copy-start.4
  0.0 0.0 copy-start.3
  0.0 2.0 %slice.17 = bf16[2,8,128,128]{3,2,1,0:T(8,128)(2,1)} slice(bf16[4,8,128,128]{3,2,1,0:T(8,128)(2,1)} %refs_2_.3), slice={[2:4], [0:8], [0:128], [0:128]} | slice | bytes 1048576 | tf_op jit(solution)/shard_map/slice | solution.py:258
  2.0 4.4 %collective-permute-start.2 = (bf16[2,8,128,128]{3,2,1,0:T(8,128)(2,1)}, bf16[2,8,128,128]{3,2,1,0:T(8,128)(2,1)S(1)}, u32[]{:S(2)}, u32[]{:S(2)}) collective-permute-start(bf16[2,8,128,128]{3,2,1,0:T(8,128)(2,1)} %slice.17), channel_id=1, source_target_pairs={{0,32},{32,64},{64,96},{96,128},{128,160},{160,192},{192,224},{1,3... | collective-permute-start | bytes 1572872 | tf_op jit(solution)/shard_map/ppermute | solution.py:258
  6.4 2.8 %stats.1 = f32[256,128]{1,0:T(8,128)} custom-call(bf16[4,8,128,128]{3,2,1,0:T(8,128)(2,1)} %refs_2_.3), custom_call_target="tpu_custom_call" | custom-call | flops 4194304 | bytes 1048576 | tf_op jit(solution)/shard_map/stats/pallas_call | solution.py:261
  9.3 14.2 %all-to-all-start = ((f32[256,1,128]{2,1,0:T(1,128)}), f32[256,1,128]{2,1,0:T(1,128)S(1)}, u32[]{:S(2)}, u32[]{:S(2)}) async-start(f32[256,1,128]{2,1,0:T(1,128)} %bitcast.41), calls=%async_computation | async-start | bytes 262144 | tf_op jit(solution)/shard_map/all_to_all | solution.py:265
  23.5 0.8 fusion
  24.3 4.0 %collective-permute-start.1 = (bf16[4,2,128,128]{3,2,1,0:T(8,128)(2,1)}, bf16[4,2,128,128]{3,2,1,0:T(8,128)(2,1)S(1)}, u32[]{:S(2)}, u32[]{:S(2)}) collective-permute-start(bf16[4,2,128,128]{3,2,1,0:T(8,128)(2,1)} %get-tuple-element.15), channel_id=1, source_target_pairs={{1,0},{2,1},{3,2},{4,3},{5,4},{6,5},{7,6},{8,7},{9,8},{10,9},{11,1... | collective-permute-start | bytes 786440 | tf_op jit(solution)/shard_map/ppermute | solution.py:260
  28.4 1.9 %collective-permute-start = (bf16[4,2,128,128]{3,2,1,0:T(8,128)(2,1)}, bf16[4,2,128,128]{3,2,1,0:T(8,128)(2,1)S(1)}, u32[]{:S(2)}, u32[]{:S(2)}) collective-permute-start(bf16[4,2,128,128]{3,2,1,0:T(8,128)(2,1)} %get-tuple-element.16), channel_id=1, source_target_pairs={{0,1},{1,2},{2,3},{3,4},{4,5},{5,6},{6,7},{7,8},{8,9},{9,10},{10,1... | collective-permute-start | bytes 786440 | tf_op jit(solution)/shard_map/ppermute | solution.py:259
  30.3 0.1 pad_add_fusion.place_ref
  30.4 0.0 collective-permute-done.2.refs_3_
  30.4 0.7 fusion.1
  31.1 2.4 %collective-permute-start.4 = (bf16[2,2,128,128]{3,2,1,0:T(8,128)(2,1)}, bf16[2,2,128,128]{3,2,1,0:T(8,128)(2,1)S(1)}, u32[]{:S(2)}, u32[]{:S(2)}) collective-permute-start(bf16[2,2,128,128]{3,2,1,0:T(8,128)(2,1)} %get-tuple-element.17), channel_id=1, source_target_pairs={{1,0},{2,1},{3,2},{4,3},{5,4},{6,5},{7,6},{8,7},{9,8},{10,9},{11,1... | collective-permute-start | bytes 393224 | tf_op jit(solution)/shard_map/ppermute | solution.py:267
  33.5 3.1 %collective-permute-start.3 = (bf16[2,2,128,128]{3,2,1,0:T(8,128)(2,1)S(1)}, bf16[2,2,128,128]{3,2,1,0:T(8,128)(2,1)S(1)}, u32[]{:S(2)}, u32[]{:S(2)}) collective-permute-start(bf16[2,2,128,128]{3,2,1,0:T(8,128)(2,1)S(1)} %get-tuple-element.18), channel_id=1, source_target_pairs={{0,1},{1,2},{2,3},{3,4},{4,5},{5,6},{6,7},{7,8},{8,9},{9,10},{10,1... | collective-permute-start | bytes 393224 | tf_op jit(solution)/shard_map/ppermute | solution.py:266
  36.6 0.0 all-to-all-done
  36.6 0.0 collective-permute-done.1.refs_2_
  36.6 0.0 collective-permute-done.refs_1_
  36.7 7.1 %first_late.1 = (f32[2,10,128,128]{3,2,1,0:T(8,128)S(1)}, f32[2,8,128]{2,1,0:T(8,128)S(1)}, bf16[2,10,128,128]{3,2,1,0:T(8,128)(2,1)S(1)}) custom-call(s32[4]{0:T(128)S(1)} %pad_add_fusion.place_ref, f32[256,128]{1,0:T(8,128)S(1)} %bitcast.20, f32[1,128]{1,0:T(1,128)S(1)} %bitcast.29, f32[1,128]{1,0:T(1,128)S(1)} %bitcast.31, ...), custom_call_target="tpu_custom_call" | custom-call | flops 3019898880 | bytes 4194304 | tf_op jit(solution)/shard_map/first_late/pallas_call | solution.py:269
  43.8 3.0 %collective-permute-start.5 = (bf16[2,10,128,128]{3,2,1,0:T(8,128)(2,1)S(1)}, bf16[2,10,128,128]{3,2,1,0:T(8,128)(2,1)S(1)}, u32[]{:S(2)}, u32[]{:S(2)}) collective-permute-start(bf16[2,10,128,128]{3,2,1,0:T(8,128)(2,1)S(1)} %get-tuple-element.13), channel_id=1, source_target_pairs={{0,32},{32,64},{64,96},{96,128},{128,160},{160,192},{192,224},{1,3... | collective-permute-start | bytes 1966088 | tf_op jit(solution)/shard_map/ppermute | solution.py:275
  46.8 0.0 collective-permute-done.4.refs_5_
  46.8 0.0 collective-permute-done.3.refs_4_
  46.8 0.0 copy-start.2
  46.8 0.0 copy-start.6
  46.9 0.0 copy-start.7
  46.9 0.0 copy-start.8
  46.9 6.5 %first_early.1 = (f32[2,10,128,128]{3,2,1,0:T(8,128)S(1)}, f32[256,128]{1,0:T(8,128)S(1)}) custom-call(s32[4]{0:T(128)S(1)} %pad_add_fusion.place_ref, f32[256,128]{1,0:T(8,128)S(1)} %bitcast.21, f32[1,128]{1,0:T(1,128)S(1)} %bitcast.30, f32[1,128]{1,0:T(1,128)S(1)} %bitcast.32, bf16[3,1152,128]{2,1,0:T(8,128)(2,1)S(1)} %bitcast.26, f32[1,128]{1,0:T(1,128)S(1)} %bitcast.34, ...), custom_call_target="tpu_custom_call" | custom-call | flops 3019898880 | bytes 4194304 | tf_op jit(solution)/shard_map/first_early/pallas_call | solution.py:276
  53.4 29.8 %all_to_all.22 = f32[256,1,128]{2,1,0:T(1,128)S(1)} all-to-all(f32[256,1,128]{2,1,0:T(1,128)S(1)} %bitcast.24), channel_id=1, replica_groups=mesh['tm'=8,'space'=32] {'tm','space'}, dimensions={0} | all-to-all | bytes 262144 | tf_op jit(solution)/shard_map/all_to_all | solution.py:282
  83.2 0.0 copy-done.7
  83.2 0.0 copy-done.8
  83.2 6.3 %second_late.1.refs_3_ = f32[4,8,128,128]{3,2,1,0:T(8,128)} custom-call(s32[4]{0:T(128)S(1)} %pad_add_fusion.place_ref, f32[256,128]{1,0:T(8,128)S(1)} %bitcast.22, f32[1,128]{1,0:T(1,128)S(1)} %bitcast.35, f32[1,128]{1,0:T(1,128)S(1)} %bitcast.37, bf16[3,1152,128]{2,1,0:T(8,128)(2,1)S(1)} %bitcast.27, f32[1,128]{1,0:T(1,128)S(1)} %bitcast.39, ...), custom_call_target="tpu_custom_call" | custom-call | flops 2415919104 | bytes 4194304 | tf_op jit(solution)/shard_map/second_late/pallas_call | solution.py:285
  89.5 0.0 collective-permute-done.5.refs_1_
  89.5 5.9 %second_early.1 = f32[4,8,128,128]{3,2,1,0:T(8,128)} custom-call(s32[4]{0:T(128)S(1)} %pad_add_fusion.place_ref, f32[256,128]{1,0:T(8,128)S(1)} %bitcast.23, f32[1,128]{1,0:T(1,128)S(1)} %bitcast.36, f32[1,128]{1,0:T(1,128)S(1)} %bitcast.38, bf16[3,1152,128]{2,1,0:T(8,128)(2,1)S(1)} %bitcast.28, ...), custom_call_target="tpu_custom_call", output_to_operand_aliasing={{}: (9, {})} | custom-call | flops 2415919104 | bytes 4194304 | tf_op jit(solution)/shard_map/second_early/pallas_call | solution.py:291
  (10 shorter events, 0.0 us)
Async XLA Ops:
  0.0 23.5 %copy-start = (bf16[4,8,128,128]{3,2,1,0:T(8,128)(2,1)S(1)}, bf16[4,8,128,128]{3,2,1,0:T(8,128)(2,1)}, u32[]{:S(2)}) copy-start(bf16[4,8,128,128]{3,2,1,0:T(8,128)(2,1)} %refs_2_.3) | copy-start | bytes 3145732
  0.0 36.7 %copy-start.5 = (f32[128]{0:T(128)S(1)}, f32[128]{0:T(128)}, u32[]{:S(2)}) copy-start(f32[128]{0:T(128)} %param.13) | copy-start | bytes 1540
  0.0 36.7 %copy-start.1 = (bf16[3,3,3,128,128]{4,3,2,1,0:T(8,128)(2,1)S(1)}, bf16[3,3,3,128,128]{4,3,2,1,0:T(8,128)(2,1)}, u32[]{:S(2)}) copy-start(bf16[3,3,3,128,128]{4,3,2,1,0:T(8,128)(2,1)} %param.12) | copy-start | bytes 2654212
  0.0 36.7 %copy-start.4 = (f32[128]{0:T(128)S(1)}, f32[128]{0:T(128)}, u32[]{:S(2)}) copy-start(f32[128]{0:T(128)} %param.11) | copy-start | bytes 1540
  0.0 36.7 %copy-start.3 = (f32[128]{0:T(128)S(1)}, f32[128]{0:T(128)}, u32[]{:S(2)}) copy-start(f32[128]{0:T(128)} %param.10) | copy-start | bytes 1540
  2.0 28.3 %collective-permute-start.2 = (bf16[2,8,128,128]{3,2,1,0:T(8,128)(2,1)}, bf16[2,8,128,128]{3,2,1,0:T(8,128)(2,1)S(1)}, u32[]{:S(2)}, u32[]{:S(2)}) collective-permute-start(bf16[2,8,128,128]{3,2,1,0:T(8,128)(2,1)} %slice.17), channel_id=1, source_target_pairs={{0,32},{32,64},{64,96},{96,128},{128,160},{160,192},{192,224},{1,3... | collective-permute-start | bytes 1572872 | tf_op jit(solution)/shard_map/ppermute | solution.py:258
  9.3 27.3 %all-to-all-start = ((f32[256,1,128]{2,1,0:T(1,128)}), f32[256,1,128]{2,1,0:T(1,128)S(1)}, u32[]{:S(2)}, u32[]{:S(2)}) async-start(f32[256,1,128]{2,1,0:T(1,128)} %bitcast.41), calls=%async_computation | async-start | bytes 262144 | tf_op jit(solution)/shard_map/all_to_all | solution.py:265
  24.3 12.3 %collective-permute-start.1 = (bf16[4,2,128,128]{3,2,1,0:T(8,128)(2,1)}, bf16[4,2,128,128]{3,2,1,0:T(8,128)(2,1)S(1)}, u32[]{:S(2)}, u32[]{:S(2)}) collective-permute-start(bf16[4,2,128,128]{3,2,1,0:T(8,128)(2,1)} %get-tuple-element.15), channel_id=1, source_target_pairs={{1,0},{2,1},{3,2},{4,3},{5,4},{6,5},{7,6},{8,7},{9,8},{10,9},{11,1... | collective-permute-start | bytes 786440 | tf_op jit(solution)/shard_map/ppermute | solution.py:260
  28.4 8.3 %collective-permute-start = (bf16[4,2,128,128]{3,2,1,0:T(8,128)(2,1)}, bf16[4,2,128,128]{3,2,1,0:T(8,128)(2,1)S(1)}, u32[]{:S(2)}, u32[]{:S(2)}) collective-permute-start(bf16[4,2,128,128]{3,2,1,0:T(8,128)(2,1)} %get-tuple-element.16), channel_id=1, source_target_pairs={{0,1},{1,2},{2,3},{3,4},{4,5},{5,6},{6,7},{7,8},{8,9},{9,10},{10,1... | collective-permute-start | bytes 786440 | tf_op jit(solution)/shard_map/ppermute | solution.py:259
  31.1 15.8 %collective-permute-start.4 = (bf16[2,2,128,128]{3,2,1,0:T(8,128)(2,1)}, bf16[2,2,128,128]{3,2,1,0:T(8,128)(2,1)S(1)}, u32[]{:S(2)}, u32[]{:S(2)}) collective-permute-start(bf16[2,2,128,128]{3,2,1,0:T(8,128)(2,1)} %get-tuple-element.17), channel_id=1, source_target_pairs={{1,0},{2,1},{3,2},{4,3},{5,4},{6,5},{7,6},{8,7},{9,8},{10,9},{11,1... | collective-permute-start | bytes 393224 | tf_op jit(solution)/shard_map/ppermute | solution.py:267
  33.5 13.4 %collective-permute-start.3 = (bf16[2,2,128,128]{3,2,1,0:T(8,128)(2,1)S(1)}, bf16[2,2,128,128]{3,2,1,0:T(8,128)(2,1)S(1)}, u32[]{:S(2)}, u32[]{:S(2)}) collective-permute-start(bf16[2,2,128,128]{3,2,1,0:T(8,128)(2,1)S(1)} %get-tuple-element.18), channel_id=1, source_target_pairs={{0,1},{1,2},{2,3},{3,4},{4,5},{5,6},{6,7},{7,8},{8,9},{9,10},{10,1... | collective-permute-start | bytes 393224 | tf_op jit(solution)/shard_map/ppermute | solution.py:266
  43.8 45.7 %collective-permute-start.5 = (bf16[2,10,128,128]{3,2,1,0:T(8,128)(2,1)S(1)}, bf16[2,10,128,128]{3,2,1,0:T(8,128)(2,1)S(1)}, u32[]{:S(2)}, u32[]{:S(2)}) collective-permute-start(bf16[2,10,128,128]{3,2,1,0:T(8,128)(2,1)S(1)} %get-tuple-element.13), channel_id=1, source_target_pairs={{0,32},{32,64},{64,96},{96,128},{128,160},{160,192},{192,224},{1,3... | collective-permute-start | bytes 1966088 | tf_op jit(solution)/shard_map/ppermute | solution.py:275
  46.8 36.3 %copy-start.2 = (bf16[3,3,3,128,128]{4,3,2,1,0:T(8,128)(2,1)S(1)}, bf16[3,3,3,128,128]{4,3,2,1,0:T(8,128)(2,1)}, u32[]{:S(2)}) copy-start(bf16[3,3,3,128,128]{4,3,2,1,0:T(8,128)(2,1)} %param.16) | copy-start | bytes 2654212
  46.8 36.3 %copy-start.6 = (f32[128]{0:T(128)S(1)}, f32[128]{0:T(128)}, u32[]{:S(2)}) copy-start(f32[128]{0:T(128)} %param.14) | copy-start | bytes 1540
  46.9 36.3 %copy-start.7 = (f32[128]{0:T(128)S(1)}, f32[128]{0:T(128)}, u32[]{:S(2)}) copy-start(f32[128]{0:T(128)} %param.15) | copy-start | bytes 1540
  46.9 36.3 %copy-start.8 = (f32[128]{0:T(128)S(1)}, f32[128]{0:T(128)}, u32[]{:S(2)}) copy-start(f32[128]{0:T(128)} %param.17) | copy-start | bytes 1540

commit v2 on v0

v2 whole, which is shorter than its diff:
```python
import functools

import jax
import jax.numpy as jnp
from jax import lax
from jax.experimental import pallas as pl
from jax.experimental.pallas import tpu as pltpu
from jax.sharding import PartitionSpec as P

EPS = 1e-06
MEMBERS = 4
LATE = 1
BOTH = ("tm", "space")
F32 = jnp.float32
BF16 = jnp.bfloat16


def lane_of(shape):
    return lax.broadcasted_iota(jnp.int32, shape, len(shape) - 1)


def group_sum(v):
    lane = lane_of(v.shape)
    width = v.shape[-1]
    axis = v.ndim - 1
    v = v + jnp.where((lane & 1) == 1, pltpu.roll(v, 1, axis), pltpu.roll(v, width - 1, axis))
    return v + jnp.where((lane & 2) == 2, pltpu.roll(v, 2, axis), pltpu.roll(v, width - 2, axis))


def column_sum(v):
    return jnp.broadcast_to(jnp.sum(v, axis=0, keepdims=True), (8, v.shape[1]))


def local_stats(load, rows, cells):
    total = load(0)
    for i in range(1, rows):
        total = total + load(i)
    mean = group_sum(column_sum(total)) / cells
    spread = jnp.zeros((128, 128), F32)
    for i in range(rows):
        d = load(i) - mean[:1]
        spread = spread + d * d
    return mean, group_sum(column_sum(spread))


def payload(mean, spread):
    place = lane_of(mean.shape) & 3
    return jnp.where(place == 0, mean, jnp.where(place == 1, spread, 0.0))


def pick(rows, place):
    return group_sum(jnp.where((lane_of(rows.shape) & 3) == place, rows, 0.0))


def whole_stats(got_ref, cells):
    got = got_ref[...]
    devices = got.shape[0]
    place = lane_of(got.shape) & 3
    means = jnp.where(place == 0, got, 0.0)
    mean = group_sum(column_sum(means)) / devices
    spread = group_sum(column_sum(jnp.where(place == 1, got, 0.0)))
    off = jnp.where(place == 0, got - mean[:1], 0.0)
    between = group_sum(column_sum(off * off))
    var = (spread + between * cells) / (cells * devices)
    return mean, lax.rsqrt(var + EPS)


def put_act(off, slope, half_shift, keep, out, f, r):
    h = off * slope + half_shift
    y = h + h * jnp.tanh(h)
    if keep is not None:
        y = y * keep
    row = lax.broadcasted_iota(jnp.int32, y.shape, 0)
    out[0, f, r] = jnp.where(row == 0, 0.0, pltpu.roll(y, 1, 0)).astype(BF16)
    out[1, f, r] = y.astype(BF16)
    out[2, f, r] = jnp.where(row == 127, 0.0, pltpu.roll(y, 127, 0)).astype(BF16)


def build_taps(kernel, taps):
    zero = jnp.zeros((9 * 128, 128), BF16)
    for f in range(4):
        at = pl.ds(f * 9 * 128, 9 * 128)
        taps[at, :128] = kernel[f] if f < 3 else zero
        taps[at, 128:] = kernel[f - 1] if f > 0 else zero


def conv_pair(acts, taps, first, rows):
    pieces = []
    for f in range(4):
        for i in range(3):
            for j in range(3):
                pieces.append(acts[j, first + f, pl.ds(i, rows)].reshape(rows * 128, 128))
    return jnp.dot(jnp.concatenate(pieces, axis=-1), taps[...], preferred_element_type=F32)


def stats_kernel(x_hbm, *refs):
    small, (x_ref, pay_ref, z_ref, in_ref, far_ref, small_ref, held, sems) = refs[:6], refs[6:]
    frames, per = x_ref.shape[:2]
    copies = [pltpu.make_async_copy(x_hbm.at[f], x_ref.at[f], sems.at[f]) for f in range(frames)]
    copies += [pltpu.make_async_copy(v, held.at[i], sems.at[frames + i]) for i, v in enumerate(small)]
    for copy in copies:
        copy.start()
    for copy in copies:
        copy.wait()
    small_ref[...] = held[...]
    z_ref[...] = x_ref[2:]
    odd = (lax.axis_index("space") & 1) == 1
    for f in range(4):
        for r in range(2):
            low, high = x_ref[f, r], x_ref[f, per - 2 + r]
            in_ref[f, r] = jnp.where(odd, low, high)
            far_ref[f, r] = jnp.where(odd, high, low)
    rows = frames * per
    load = lambda i: x_ref[i // per, i % per].astype(F32)
    mean, spread = local_stats(load, rows, float(rows * 128 * MEMBERS))
    pay_ref[...] = jnp.broadcast_to(payload(mean, spread)[:1], pay_ref.shape)


def norm_constants(got_ref, small_ref, at, cells):
    mean, scale = whole_stats(got_ref, cells)
    gain, shift, bias = (small_ref[at + i : at + i + 1] for i in range(3))
    return mean[:1], scale[:1] * gain * 0.5, shift * 0.5, bias


def edges(strips):
    space = lax.axis_index("space")
    return jnp.where(space == 0, 0.0, 1.0), jnp.where(space == strips - 1, 0.0, 1.0)


def first_kernel(cells, strips, kernel_hbm, got_ref, small_ref, x_ref, in_ref, far_ref,
                 z_ref, z_in_ref, z_far_ref, inner_ref, pay_ref, send_ref, acts, taps, kernel, sem):
    fetch = pltpu.make_async_copy(kernel_hbm, kernel, sem)
    fetch.start()
    mean, slope, half, bias = norm_constants(got_ref, small_ref, 0, cells)
    top, bottom = edges(strips)
    odd = (lax.axis_index("space") & 1) == 1
    start = lax.axis_index("tm") == 0

    def frame(own, near, far, f):
        for r in range(12):
            if 2 <= r < 10:
                x, keep = own(r - 2), None
            else:
                high = r >= 10
                i = r - 10 if high else r
                a, b = near(i), far(i)
                x, keep = (jnp.where(odd, b, a), bottom) if high else (jnp.where(odd, a, b), top)
            put_act(x.astype(F32) - mean, slope, half, keep, acts, f, r)

    def of(ref, f):
        return lambda r: ref[f, r]

    def carried(ref, z, f):
        return lambda r: jnp.where(start, ref[0, r], z[f, r])

    def conv(pair):
        got = conv_pair(acts, taps, 2 * pair, 10)
        for o in range(2):
            inner_ref[2 * pair + o] = (got[:, o * 128 : (o + 1) * 128] + bias).reshape(10, 128, 128)

    for f in range(4):
        if f == 2:
            fetch.wait()
            build_taps(kernel, taps)
        frame(of(x_ref, f), of(in_ref, f), of(far_ref, f), 2 + f)
    conv(1)
    for f in range(2):
        frame(carried(x_ref, z_ref, f), carried(in_ref, z_in_ref, f), carried(far_ref, z_far_ref, f), f)
    conv(0)
    load = lambda i: inner_ref[i // 8, 1 + i % 8]
    m, s = local_stats(load, 32, cells)
    pay_ref[...] = jnp.broadcast_to(payload(m, s)[:1], pay_ref.shape)
    for o in range(2):
        send_ref[o] = (inner_ref[2 + o] - m[:1]).astype(BF16)


def second_kernel(early, cells, strips, kernel_hbm, got_ref, small_ref, feat_ref, x_ref, *refs):
    if early:
        z_ref, _, out_hbm, acts, taps, kernel, out, sem, sems = refs
    else:
        out_hbm, acts, taps, kernel, out, sem, sems = refs
    base_frame = 0 if early else 2
    fetch = pltpu.make_async_copy(kernel_hbm, kernel, sem)
    fetch.start()
    mean, slope, half, bias = norm_constants(got_ref, small_ref, 3, cells)
    top, bottom = edges(strips)

    def frame(off, f):
        for r in range(10):
            put_act(off(r), slope, half, {0: top, 9: bottom}.get(r), acts, f, r)

    if early:
        tm = lax.axis_index("tm")
        start = tm == 0
        sender = got_ref[pl.ds(jnp.maximum(tm - 1, 0) * strips + lax.axis_index("space"), 1)]
        base = mean - pick(jnp.broadcast_to(sender, (8, 128)), 0)[:1]
    for f in range(4):
        if f == 2:
            fetch.wait()
            build_taps(kernel, taps)
        if not early:
            frame(lambda r: x_ref[f, r] - mean, f)
        elif f >= 2:
            frame(lambda r: x_ref[f - 2, r] - mean, f)
        else:
            frame(lambda r: jnp.where(start, x_ref[0, r] - mean, z_ref[f, r].astype(F32) - base), f)
    got = conv_pair(acts, taps, 0, 8)
    copies = []
    for o in range(2):
        conv = (got[:, o * 128 : (o + 1) * 128] + bias).reshape(8, 128, 128)
        out[o] = feat_ref[base_frame + o].astype(F32) + conv
        copies.append(pltpu.make_async_copy(out.at[o], out_hbm.at[base_frame + o], sems.at[o]))
        copies[o].start()
    for copy in copies:
        copy.wait()


VMEM = pl.BlockSpec(memory_space=pltpu.VMEM)
HBM = pl.BlockSpec(memory_space=pltpu.MemorySpace.HBM)
PARAMS = pltpu.CompilerParams(vmem_limit_bytes=32 * 1024 * 1024)
DMA = pltpu.SemaphoreType.DMA


def scratch(frames, rows):
    return [
        pltpu.VMEM((3, frames, rows, 128, 128), BF16),
        pltpu.VMEM((36 * 128, 256), BF16),
        pltpu.VMEM((3, 9 * 128, 128), BF16),
    ]


def cost(pairs, rows, more=1):
    positions = pairs * rows * 128
    return pl.CostEstimate(
        flops=2 * positions * 36 * 128 * 256 * more, bytes_accessed=4 << 20, transcendentals=2 * positions * 128
    )


def in_hbm(v):
    return pltpu.with_memory_space_constraint(v, pltpu.MemorySpace.HBM)


def shape(dims, dtype):
    return jax.ShapeDtypeStruct(dims, dtype)


def shards(features, gain_one, shift_one, kernel_one, bias_one, gain_two, shift_two, kernel_two, bias_two):
    slabs = lax.axis_size("tm")
    strips = lax.axis_size("space")
    devices = slabs * strips
    cells = float(4 * 8 * 128 * MEMBERS)
    swap_in = [(i, i ^ 1) for i in range(strips)]
    swap_far = [(i, i + 1) for i in range(1, strips - 1, 2)] + [(i + 1, i) for i in range(1, strips - 1, 2)]
    later = [(i, i + 1) for i in range(slabs - 1)]
    taps_one = kernel_one.reshape(3, 9 * 128, 128)
    taps_two = kernel_two.reshape(3, 9 * 128, 128)

    taps_one, taps_two = in_hbm(taps_one), in_hbm(taps_two)
    x, pay, z_send, in_send, far_send, small = pl.pallas_call(
        stats_kernel,
        out_shape=[
            shape((4, 8, 128, 128), BF16), shape((devices, 128), F32), shape((2, 8, 128, 128), BF16),
            shape((4, 2, 128, 128), BF16), shape((4, 2, 128, 128), BF16), shape((6, 128), F32),
        ],
        in_specs=[HBM] * 7, out_specs=[VMEM] * 6,
        scratch_shapes=[pltpu.VMEM((6, 128), F32), DMA((10,))], compiler_params=PARAMS,
        cost_estimate=pl.CostEstimate(flops=1 << 22, bytes_accessed=1 << 20, transcendentals=0), name="stats",
    )(*map(in_hbm, (features, gain_one, shift_one, bias_one, gain_two, shift_two, bias_two)))
    z_one = lax.ppermute(z_send, "tm", later)
    near = lax.ppermute(in_send, "space", swap_in)
    far = lax.ppermute(far_send, "space", swap_far)
    got = lax.all_to_all(pay, BOTH, 0, 0)
    odd = (lax.axis_index("space") & 1) == 1
    low, high = z_one[:, :2], z_one[:, 6:]
    z_near = lax.ppermute(jnp.where(odd, low, high), "space", swap_in)
    z_far = lax.ppermute(jnp.where(odd, high, low), "space", swap_far)
    inner, pay, send = pl.pallas_call(
        functools.partial(first_kernel, cells, strips),
        out_shape=[shape((4, 10, 128, 128), F32), shape((devices, 128), F32), shape((2, 10, 128, 128), BF16)],
        in_specs=[HBM] + [VMEM] * 8, out_specs=[VMEM] * 3, scratch_shapes=scratch(6, 12) + [DMA],
        compiler_params=PARAMS, cost_estimate=cost(2, 10), name="first",
    )(taps_one, got, small, x, near, far, z_one, z_near, z_far)
    got = lax.all_to_all(pay, BOTH, 0, 0)
    z_two = lax.ppermute(send, "tm", later)
    out_scratch = [pltpu.VMEM((2, 8, 128, 128), F32), DMA, DMA((2,))]
    out = pl.pallas_call(
        functools.partial(second_kernel, False, cells, strips),
        out_shape=shape((4, 8, 128, 128), F32),
        in_specs=[HBM] + [VMEM] * 4, out_specs=HBM, scratch_shapes=scratch(4, 10) + out_scratch,
        compiler_params=PARAMS, cost_estimate=cost(1, 8, LATE), name="second_late",
    )(taps_two, got, small, x, inner)
    return pl.pallas_call(
        functools.partial(second_kernel, True, cells, strips),
        out_shape=shape((4, 8, 128, 128), F32),
        in_specs=[HBM] + [VMEM] * 5 + [HBM], out_specs=HBM, scratch_shapes=scratch(4, 10) + out_scratch,
        input_output_aliases={6: 0}, compiler_params=PARAMS, cost_estimate=cost(1, 8), name="second_early",
    )(taps_two, got, small, x, inner, z_two, out)


def solution(mesh):
    placed = (P("tm", "space", None, None), P(), P(), P(), P(), P(), P(), P(), P())
    return jax.shard_map(
        shards, mesh=mesh, in_specs=placed, out_specs=P("tm", "space", None, None), check_vma=False
    )
```

time: 416 us -> 81.1 us (0.19); the launches traced: 409 us -> 80.7 us
  blocking collectives: 305 us -> 24.7 us
  waiting for transfers between devices: 31 us -> 4.71 us
  Pallas kernels: 0 us -> 21.7 us
  local copies, waits for them, and re-layouts: 21 us -> 0 us
  matrix products: 16.9 us -> 0 us
  other arithmetic: 16 us -> 0.02 us
  starting transfers between devices: 18.3 us -> 29.4 us
    psum x4 -> x0, blocking collectives: 305 us -> none  [the longest x2 158 us: group_stats(): mean = lax.psum(local_sum, ('tm', 'space')) / count]
    ppermute x6, waiting for transfers between devices: 31 us -> 0.02 us  [the longest x1 0.01 us: shards(): z_near = lax.ppermute(jnp.where(odd, low, high), 'space', swap_in)]
    all_to_all x0 -> x1, blocking collectives: none -> 24.7 us  [shards(): got = lax.all_to_all(pay, BOTH, 0, 0)]
    pallas_call x0 -> x4, Pallas kernels: none -> 21.7 us  [the longest x1 8.61 us: shards(): pl.pallas_call(functools.partial(first_kernel, cells, strips), out_shape=...]
    unnamed x28 -> x0, local copies, waits for them, and re-layouts: 17 us -> none
    dot_general x6 -> x0, matrix products: 16.9 us -> none  [causal_conv(): total = total + jnp.dot(patches, taps, preferred_element_type=jnp.float32)]
    all_to_all x0 -> x1, starting transfers between devices: none -> 14.2 us  [shards(): got = lax.all_to_all(pay, BOTH, 0, 0)]
    all_to_all x0 -> x1, waiting for transfers between devices: none -> 4.69 us  [shards(): got = lax.all_to_all(pay, BOTH, 0, 0)]
  transfers between devices with their start and end apart: 6 -> 7, of which waited for: 6 -> 1; matrix products, arithmetic and copies ran while one was open for 0% -> 0% of each run, Pallas kernels for 0% -> 6%
where the time goes in v2:
time: 81.1 us; the launch traced here: 80.7 us
  starting transfers between devices  29.4 us (36%)
  blocking collectives  24.7 us (30%)
  Pallas kernels  21.7 us (27%)
  waiting for transfers between devices  4.71 us (6%)
    all_to_all x1, blocking collectives, shards(): got = lax.all_to_all(pay, BOTH, 0, 0)  24.7 us
    all_to_all x1, starting transfers between devices, shards(): got = lax.all_to_all(pay, BOTH, 0, 0)  14.2 us
    pallas_call x1, Pallas kernels, shards(): pl.pallas_call(functools.partial(first_kernel, cells, strips), out_shape=...  8.61 us
    pallas_call x1, Pallas kernels, shards(): pl.pallas_call(functools.partial(second_kernel, True, cells, strips), out...  5.32 us
    pallas_call x1, Pallas kernels, shards(): pl.pallas_call(functools.partial(second_kernel, False, cells, strips), ou...  5.09 us
    all_to_all x1, waiting for transfers between devices, shards(): got = lax.all_to_all(pay, BOTH, 0, 0)  4.69 us
    ppermute x1, starting transfers between devices, shards(): z_one = lax.ppermute(z_send, 'tm', later)  4.4 us
    ppermute x1, starting transfers between devices, shards(): z_far = lax.ppermute(jnp.where(odd, high, low), 'space', swap_far)  3.64 us
  transfers between devices with their start and end apart: 7, of which 1 were waited for; matrix products, arithmetic and copies ran while one was open for 0% of the time, Pallas kernels for 6%

profile of v2, /device:TPU:1, one launch (start us, length us, event | category | flops | bytes accessed | tf_op | source)
XLA Modules:
  0.0 80.7 jit_solution(13522835033671925370)
XLA Ops:
  0.0 2.7 %stats.1 = (bf16[4,8,128,128]{3,2,1,0:T(8,128)(2,1)S(1)}, f32[256,128]{1,0:T(8,128)}, bf16[2,8,128,128]{3,2,1,0:T(8,128)(2,1)S(1)}, bf16[4,2,128,128]{3,2,1,0:T(...) custom-call(bf16[4,8,128,128]{3,2,1,0:T(8,128)(2,1)} %x_hbm.1, f32[128]{0:T(128)} %refs_0_.1, ...), custom_call_target="tpu_custom_call" | custom-call | flops 4194304 | bytes 1048576 | tf_op jit(solution)/shard_map/stats/pallas_call | solution.py:259
  2.7 4.4 %collective-permute-start.2 = (bf16[2,8,128,128]{3,2,1,0:T(8,128)(2,1)S(1)}, bf16[2,8,128,128]{3,2,1,0:T(8,128)(2,1)S(1)}, u32[]{:S(2)}, u32[]{:S(2)}) collective-permute-start(bf16[2,8,128,128]{3,2,1,0:T(8,128)(2,1)S(1)} %get-tuple-element.19), channel_id=1, source_target_pairs={{0,32},{32,64},{64,96},{96,128},{128,160},{160,192},{192,224},{1,3... | collective-permute-start | bytes 1572872 | tf_op jit(solution)/shard_map/ppermute | solution.py:269
  7.1 14.2 %all-to-all-start = ((f32[256,1,128]{2,1,0:T(1,128)}), f32[256,1,128]{2,1,0:T(1,128)S(1)}, u32[]{:S(2)}, u32[]{:S(2)}) async-start(f32[256,1,128]{2,1,0:T(1,128)} %bitcast.3), calls=%async_computation | async-start | bytes 262144 | tf_op jit(solution)/shard_map/all_to_all | solution.py:272
  21.3 2.2 %collective-permute-start = (bf16[4,2,128,128]{3,2,1,0:T(8,128)(2,1)S(1)}, bf16[4,2,128,128]{3,2,1,0:T(8,128)(2,1)S(1)}, u32[]{:S(2)}, u32[]{:S(2)}) collective-permute-start(bf16[4,2,128,128]{3,2,1,0:T(8,128)(2,1)S(1)} %get-tuple-element.17), channel_id=1, source_target_pairs={{0,1},{1,0},{2,3},{3,2},{4,5},{5,4},{6,7},{7,6},{8,9},{9,8},{10,11... | collective-permute-start | bytes 786440 | tf_op jit(solution)/shard_map/ppermute | solution.py:270
  23.5 1.9 %collective-permute-start.1 = (bf16[4,2,128,128]{3,2,1,0:T(8,128)(2,1)S(1)}, bf16[4,2,128,128]{3,2,1,0:T(8,128)(2,1)S(1)}, u32[]{:S(2)}, u32[]{:S(2)}) collective-permute-start(bf16[4,2,128,128]{3,2,1,0:T(8,128)(2,1)S(1)} %get-tuple-element.18), channel_id=1, source_target_pairs={{1,2},{3,4},{5,6},{7,8},{9,10},{11,12},{13,14},{15,16},{17,18},{19... | collective-permute-start | bytes 786440 | tf_op jit(solution)/shard_map/ppermute | solution.py:271
  25.4 0.0 collective-permute-done.2.z_ref
  25.5 3.6 %collective-permute-start.4 = (bf16[2,2,128,128]{3,2,1,0:T(8,128)(2,1)S(1)}, bf16[2,2,128,128]{3,2,1,0:T(8,128)(2,1)S(1)}, u32[]{:S(2)}, u32[]{:S(2)}) collective-permute-start(bf16[2,2,128,128]{3,2,1,0:T(8,128)(2,1)S(1)} %get-tuple-element.23), channel_id=1, source_target_pairs={{1,2},{3,4},{5,6},{7,8},{9,10},{11,12},{13,14},{15,16},{17,18},{19... | collective-permute-start | bytes 393224 | tf_op jit(solution)/shard_map/ppermute | solution.py:276
  29.1 0.1 collective-permute-start.3
  29.2 4.7 %all-to-all-done = f32[256,1,128]{2,1,0:T(1,128)S(1)} async-done(((f32[256,1,128]{2,1,0:T(1,128)}), f32[256,1,128]{2,1,0:T(1,128)S(1)}, u32[]{:S(2)}, u32[]{:S(2)}) %all-to-all-start) | async-done | bytes 131104 | tf_op jit(solution)/shard_map/all_to_all | solution.py:272
  33.9 0.0 collective-permute-done.in_ref
  33.9 0.0 collective-permute-done.1.far_ref
  33.9 0.0 collective-permute-done.4.z_far_ref
  33.9 0.0 collective-permute-done.3.z_in_ref
  33.9 8.6 %first.1 = (f32[4,10,128,128]{3,2,1,0:T(8,128)S(1)}, f32[256,128]{1,0:T(8,128)S(1)}, bf16[2,10,128,128]{3,2,1,0:T(8,128)(2,1)S(1)}) custom-call(bf16[3,1152,128]{2,1,0:T(8,128)(2,1)} %bitcast.16, f32[256,128]{1,0:T(8,128)S(1)} %bitcast.12, f32[6,128]{1,0:T(8,128)S(1)} %get-tuple-element.15.small_ref, ...), custom_call_target="tpu_custom_call" | custom-call | flops 6039797760 | bytes 4194304 | tf_op jit(solution)/shard_map/first/pallas_call | solution.py:277
  42.6 2.9 %collective-permute-start.5 = (bf16[2,10,128,128]{3,2,1,0:T(8,128)(2,1)S(1)}, bf16[2,10,128,128]{3,2,1,0:T(8,128)(2,1)S(1)}, u32[]{:S(2)}, u32[]{:S(2)}) collective-permute-start(bf16[2,10,128,128]{3,2,1,0:T(8,128)(2,1)S(1)} %get-tuple-element.22), channel_id=1, source_target_pairs={{0,32},{32,64},{64,96},{96,128},{128,160},{160,192},{192,224},{1,3... | collective-permute-start | bytes 1966088 | tf_op jit(solution)/shard_map/ppermute | solution.py:284
  45.5 24.7 %all_to_all.22 = f32[256,1,128]{2,1,0:T(1,128)S(1)} all-to-all(f32[256,1,128]{2,1,0:T(1,128)S(1)} %bitcast.13), channel_id=1, replica_groups=mesh['tm'=8,'space'=32] {'tm','space'}, dimensions={0} | all-to-all | bytes 262144 | tf_op jit(solution)/shard_map/all_to_all | solution.py:283
  70.2 5.1 %second_late.1.refs_1_ = f32[4,8,128,128]{3,2,1,0:T(8,128)} custom-call(bf16[3,1152,128]{2,1,0:T(8,128)(2,1)} %bitcast.14, f32[256,128]{1,0:T(8,128)S(1)} %bitcast.10, f32[6,128]{1,0:T(8,128)S(1)} %get-tuple-element.15.small_ref, bf16[4,8,128,128]{3,2,1,0:T(8,128)(2,1)S(1)} %get-tuple-element.16.x_ref.feat_ref, f32[4,10,128,128]{3,2,1,0:T(8,128)S(1)} %get-tuple-element.21.x_ref), custom_call_target="tpu_custom_call" | custom-call | flops 2415919104 | bytes 4194304 | tf_op jit(solution)/shard_map/second_late/pallas_call | solution.py:286
  75.2 0.0 collective-permute-done.5.refs_0_
  75.3 5.3 %second_early.1 = f32[4,8,128,128]{3,2,1,0:T(8,128)} custom-call(bf16[3,1152,128]{2,1,0:T(8,128)(2,1)} %bitcast.15, f32[256,128]{1,0:T(8,128)S(1)} %bitcast.11, f32[6,128]{1,0:T(8,128)S(1)} %get-tuple-element.15.small_ref, bf16[4,8,128,128]{3,2,1,0:T(8,128)(2,1)S(1)} %get-tuple-element.16.x_ref.feat_ref, ...), custom_call_target="tpu_custom_call", output_to_operand_aliasing={{}: (6, {})} | custom-call | flops 2415919104 | bytes 4194304 | tf_op jit(solution)/shard_map/second_early/pallas_call | solution.py:292
  (1 shorter events, 0.0 us)
Async XLA Ops:
  2.7 22.8 %collective-permute-start.2 = (bf16[2,8,128,128]{3,2,1,0:T(8,128)(2,1)S(1)}, bf16[2,8,128,128]{3,2,1,0:T(8,128)(2,1)S(1)}, u32[]{:S(2)}, u32[]{:S(2)}) collective-permute-start(bf16[2,8,128,128]{3,2,1,0:T(8,128)(2,1)S(1)} %get-tuple-element.19), channel_id=1, source_target_pairs={{0,32},{32,64},{64,96},{96,128},{128,160},{160,192},{192,224},{1,3... | collective-permute-start | bytes 1572872 | tf_op jit(solution)/shard_map/ppermute | solution.py:269
  7.1 26.8 %all-to-all-start = ((f32[256,1,128]{2,1,0:T(1,128)}), f32[256,1,128]{2,1,0:T(1,128)S(1)}, u32[]{:S(2)}, u32[]{:S(2)}) async-start(f32[256,1,128]{2,1,0:T(1,128)} %bitcast.3), calls=%async_computation | async-start | bytes 262144 | tf_op jit(solution)/shard_map/all_to_all | solution.py:272
  21.3 12.6 %collective-permute-start = (bf16[4,2,128,128]{3,2,1,0:T(8,128)(2,1)S(1)}, bf16[4,2,128,128]{3,2,1,0:T(8,128)(2,1)S(1)}, u32[]{:S(2)}, u32[]{:S(2)}) collective-permute-start(bf16[4,2,128,128]{3,2,1,0:T(8,128)(2,1)S(1)} %get-tuple-element.17), channel_id=1, source_target_pairs={{0,1},{1,0},{2,3},{3,2},{4,5},{5,4},{6,7},{7,6},{8,9},{9,8},{10,11... | collective-permute-start | bytes 786440 | tf_op jit(solution)/shard_map/ppermute | solution.py:270
  23.5 10.4 %collective-permute-start.1 = (bf16[4,2,128,128]{3,2,1,0:T(8,128)(2,1)S(1)}, bf16[4,2,128,128]{3,2,1,0:T(8,128)(2,1)S(1)}, u32[]{:S(2)}, u32[]{:S(2)}) collective-permute-start(bf16[4,2,128,128]{3,2,1,0:T(8,128)(2,1)S(1)} %get-tuple-element.18), channel_id=1, source_target_pairs={{1,2},{3,4},{5,6},{7,8},{9,10},{11,12},{13,14},{15,16},{17,18},{19... | collective-permute-start | bytes 786440 | tf_op jit(solution)/shard_map/ppermute | solution.py:271
  25.5 8.5 %collective-permute-start.4 = (bf16[2,2,128,128]{3,2,1,0:T(8,128)(2,1)S(1)}, bf16[2,2,128,128]{3,2,1,0:T(8,128)(2,1)S(1)}, u32[]{:S(2)}, u32[]{:S(2)}) collective-permute-start(bf16[2,2,128,128]{3,2,1,0:T(8,128)(2,1)S(1)} %get-tuple-element.23), channel_id=1, source_target_pairs={{1,2},{3,4},{5,6},{7,8},{9,10},{11,12},{13,14},{15,16},{17,18},{19... | collective-permute-start | bytes 393224 | tf_op jit(solution)/shard_map/ppermute | solution.py:276
  29.1 4.8 %collective-permute-start.3 = (bf16[2,2,128,128]{3,2,1,0:T(8,128)(2,1)S(1)}, bf16[2,2,128,128]{3,2,1,0:T(8,128)(2,1)S(1)}, u32[]{:S(2)}, u32[]{:S(2)}) collective-permute-start(bf16[2,2,128,128]{3,2,1,0:T(8,128)(2,1)S(1)} %get-tuple-element.24), channel_id=1, source_target_pairs={{0,1},{1,0},{2,3},{3,2},{4,5},{5,4},{6,7},{7,6},{8,9},{9,8},{10,11... | collective-permute-start | bytes 393224 | tf_op jit(solution)/shard_map/ppermute | solution.py:275
  42.6 32.7 %collective-permute-start.5 = (bf16[2,10,128,128]{3,2,1,0:T(8,128)(2,1)S(1)}, bf16[2,10,128,128]{3,2,1,0:T(8,128)(2,1)S(1)}, u32[]{:S(2)}, u32[]{:S(2)}) collective-permute-start(bf16[2,10,128,128]{3,2,1,0:T(8,128)(2,1)S(1)} %get-tuple-element.22), channel_id=1, source_target_pairs={{0,32},{32,64},{64,96},{96,128},{128,160},{160,192},{192,224},{1,3... | collective-permute-start | bytes 1966088 | tf_op jit(solution)/shard_map/ppermute | solution.py:284

commit v3 on v2

--- a/solution.py
+++ b/solution.py
@@ -9,7 +9,6 @@
 
 EPS = 1e-06
 MEMBERS = 4
-LATE = 1
 BOTH = ("tm", "space")
 F32 = jnp.float32
 BF16 = jnp.bfloat16
@@ -31,21 +30,31 @@
     return jnp.broadcast_to(jnp.sum(v, axis=0, keepdims=True), (8, v.shape[1]))
 
 
-def local_stats(load, rows, cells):
-    total = load(0)
-    for i in range(1, rows):
-        total = total + load(i)
+def add_up(blocks):
+    total = next(blocks)
+    for block in blocks:
+        total = total + block
+    return total
+
+
+def local_stats(load, rows, cells, total=None):
+    if total is None:
+        total = add_up(load(i) for i in range(rows))
     mean = group_sum(column_sum(total)) / cells
-    spread = jnp.zeros((128, 128), F32)
-    for i in range(rows):
+
+    def spread(i):
         d = load(i) - mean[:1]
-        spread = spread + d * d
-    return mean, group_sum(column_sum(spread))
-
-
-def payload(mean, spread):
-    place = lane_of(mean.shape) & 3
-    return jnp.where(place == 0, mean, jnp.where(place == 1, spread, 0.0))
+        return d * d
+
+    return mean, group_sum(column_sum(add_up(spread(i) for i in range(rows))))
+
+
+def payload(*entries):
+    place = lane_of(entries[0].shape) & 3
+    out = jnp.zeros_like(entries[0])
+    for i, entry in enumerate(entries):
+        out = jnp.where(place == i, entry, out)
+    return out
 
 
 def pick(rows, place):
@@ -84,36 +93,39 @@
         taps[at, 128:] = kernel[f - 1] if f > 0 else zero
 
 
-def conv_pair(acts, taps, first, rows):
+def conv_pair(acts, taps, first, at, rows):
     pieces = []
     for f in range(4):
         for i in range(3):
             for j in range(3):
-                pieces.append(acts[j, first + f, pl.ds(i, rows)].reshape(rows * 128, 128))
+                pieces.append(acts[j, first + f, pl.ds(at + i, rows)].reshape(rows * 128, 128))
     return jnp.dot(jnp.concatenate(pieces, axis=-1), taps[...], preferred_element_type=F32)
 
 
 def stats_kernel(x_hbm, *refs):
-    small, (x_ref, pay_ref, z_ref, in_ref, far_ref, small_ref, held, sems) = refs[:6], refs[6:]
+    small, (x_ref, pay_ref, z_ref, in_ref, far_ref, small_ref, sems) = refs[:6], refs[6:]
     frames, per = x_ref.shape[:2]
     copies = [pltpu.make_async_copy(x_hbm.at[f], x_ref.at[f], sems.at[f]) for f in range(frames)]
-    copies += [pltpu.make_async_copy(v, held.at[i], sems.at[frames + i]) for i, v in enumerate(small)]
+    copies += [pltpu.make_async_copy(v, small_ref.at[i], sems.at[frames + i]) for i, v in enumerate(small)]
     for copy in copies:
         copy.start()
-    for copy in copies:
-        copy.wait()
-    small_ref[...] = held[...]
-    z_ref[...] = x_ref[2:]
     odd = (lax.axis_index("space") & 1) == 1
-    for f in range(4):
+    total = None
+    for f in range(frames):
+        copies[f].wait()
+        part = add_up(x_ref[f, r].astype(F32) for r in range(per))
+        total = part if f == 0 else total + part
         for r in range(2):
             low, high = x_ref[f, r], x_ref[f, per - 2 + r]
             in_ref[f, r] = jnp.where(odd, low, high)
             far_ref[f, r] = jnp.where(odd, high, low)
+    z_ref[...] = x_ref[2:]
     rows = frames * per
     load = lambda i: x_ref[i // per, i % per].astype(F32)
-    mean, spread = local_stats(load, rows, float(rows * 128 * MEMBERS))
+    mean, spread = local_stats(load, rows, float(rows * 128 * MEMBERS), total)
     pay_ref[...] = jnp.broadcast_to(payload(mean, spread)[:1], pay_ref.shape)
+    for copy in copies[frames:]:
+        copy.wait()
 
 
 def norm_constants(got_ref, small_ref, at, cells):
@@ -154,7 +166,7 @@
         return lambda r: jnp.where(start, ref[0, r], z[f, r])
 
     def conv(pair):
-        got = conv_pair(acts, taps, 2 * pair, 10)
+        got = conv_pair(acts, taps, 2 * pair, 0, 10)
         for o in range(2):
             inner_ref[2 * pair + o] = (got[:, o * 128 : (o + 1) * 128] + bias).reshape(10, 128, 128)
 
@@ -163,54 +175,58 @@
             fetch.wait()
             build_taps(kernel, taps)
         frame(of(x_ref, f), of(in_ref, f), of(far_ref, f), 2 + f)
+    def stats(pair):
+        return local_stats(lambda i: inner_ref[2 * pair + i // 8, 1 + i % 8], 16, cells / 2)
+
     conv(1)
     for f in range(2):
         frame(carried(x_ref, z_ref, f), carried(in_ref, z_in_ref, f), carried(far_ref, z_far_ref, f), f)
+    late, late_spread = stats(1)
+    for o in range(2):
+        send_ref[o] = (inner_ref[2 + o] - late[:1]).astype(BF16)
     conv(0)
-    load = lambda i: inner_ref[i // 8, 1 + i % 8]
-    m, s = local_stats(load, 32, cells)
-    pay_ref[...] = jnp.broadcast_to(payload(m, s)[:1], pay_ref.shape)
-    for o in range(2):
-        send_ref[o] = (inner_ref[2 + o] - m[:1]).astype(BF16)
-
-
-def second_kernel(early, cells, strips, kernel_hbm, got_ref, small_ref, feat_ref, x_ref, *refs):
-    if early:
-        z_ref, _, out_hbm, acts, taps, kernel, out, sem, sems = refs
-    else:
-        out_hbm, acts, taps, kernel, out, sem, sems = refs
-    base_frame = 0 if early else 2
+    early, early_spread = stats(0)
+    gap = late - early
+    spread = late_spread + early_spread + gap * gap * (cells / 4)
+    pay_ref[...] = jnp.broadcast_to(payload((late + early) * 0.5, spread, late)[:1], pay_ref.shape)
+
+
+def second_kernel(cells, strips, kernel_hbm, got_ref, small_ref, feat_ref, x_ref, z_ref, out_hbm, acts, taps, kernel, out, sem, sems):
     fetch = pltpu.make_async_copy(kernel_hbm, kernel, sem)
     fetch.start()
     mean, slope, half, bias = norm_constants(got_ref, small_ref, 3, cells)
     top, bottom = edges(strips)
+    tm = lax.axis_index("tm")
+    start = tm == 0
+    sender = got_ref[pl.ds(jnp.maximum(tm - 1, 0) * strips + lax.axis_index("space"), 1)]
+    base = mean - pick(jnp.broadcast_to(sender, (8, 128)), 2)[:1]
 
     def frame(off, f):
         for r in range(10):
             put_act(off(r), slope, half, {0: top, 9: bottom}.get(r), acts, f, r)
 
-    if early:
-        tm = lax.axis_index("tm")
-        start = tm == 0
-        sender = got_ref[pl.ds(jnp.maximum(tm - 1, 0) * strips + lax.axis_index("space"), 1)]
-        base = mean - pick(jnp.broadcast_to(sender, (8, 128)), 0)[:1]
+    copies = []
+
+    def conv(pair, at, rows):
+        got = conv_pair(acts, taps, 2 * pair, at, rows)
+        for o in range(2):
+            f = 2 * pair + o
+            part = (got[:, o * 128 : (o + 1) * 128] + bias).reshape(rows, 128, 128)
+            out[f, pl.ds(at, rows)] = feat_ref[f, pl.ds(at, rows)].astype(F32) + part
+            here = (f, pl.ds(at, rows))
+            copies.append(pltpu.make_async_copy(out.at[here], out_hbm.at[here], sems.at[len(copies)]))
+            copies[-1].start()
+
     for f in range(4):
         if f == 2:
             fetch.wait()
             build_taps(kernel, taps)
-        if not early:
-            frame(lambda r: x_ref[f, r] - mean, f)
-        elif f >= 2:
-            frame(lambda r: x_ref[f - 2, r] - mean, f)
-        else:
-            frame(lambda r: jnp.where(start, x_ref[0, r] - mean, z_ref[f, r].astype(F32) - base), f)
-    got = conv_pair(acts, taps, 0, 8)
-    copies = []
-    for o in range(2):
-        conv = (got[:, o * 128 : (o + 1) * 128] + bias).reshape(8, 128, 128)
-        out[o] = feat_ref[base_frame + o].astype(F32) + conv
-        copies.append(pltpu.make_async_copy(out.at[o], out_hbm.at[base_frame + o], sems.at[o]))
-        copies[o].start()
+        frame(lambda r: x_ref[f, r] - mean, 2 + f)
+    conv(1, 0, 8)
+    for f in range(2):
+        frame(lambda r: jnp.where(start, x_ref[0, r] - mean, z_ref[f, r].astype(F32) - base), f)
+    for at in (0, 4):
+        conv(0, at, 4)
     for copy in copies:
         copy.wait()
 
@@ -229,10 +245,10 @@
     ]
 
 
-def cost(pairs, rows, more=1):
+def cost(pairs, rows):
     positions = pairs * rows * 128
     return pl.CostEstimate(
-        flops=2 * positions * 36 * 128 * 256 * more, bytes_accessed=4 << 20, transcendentals=2 * positions * 128
+        flops=2 * positions * 36 * 128 * 256, bytes_accessed=4 << 20, transcendentals=2 * positions * 128
     )
 
 
@@ -263,7 +279,7 @@
             shape((4, 2, 128, 128), BF16), shape((4, 2, 128, 128), BF16), shape((6, 128), F32),
         ],
         in_specs=[HBM] * 7, out_specs=[VMEM] * 6,
-        scratch_shapes=[pltpu.VMEM((6, 128), F32), DMA((10,))], compiler_params=PARAMS,
+        scratch_shapes=[DMA((10,))], compiler_params=PARAMS,
         cost_estimate=pl.CostEstimate(flops=1 << 22, bytes_accessed=1 << 20, transcendentals=0), name="stats",
     )(*map(in_hbm, (features, gain_one, shift_one, bias_one, gain_two, shift_two, bias_two)))
     z_one = lax.ppermute(z_send, "tm", later)
@@ -282,19 +298,13 @@
     )(taps_one, got, small, x, near, far, z_one, z_near, z_far)
     got = lax.all_to_all(pay, BOTH, 0, 0)
     z_two = lax.ppermute(send, "tm", later)
-    out_scratch = [pltpu.VMEM((2, 8, 128, 128), F32), DMA, DMA((2,))]
-    out = pl.pallas_call(
-        functools.partial(second_kernel, False, cells, strips),
+    return pl.pallas_call(
+        functools.partial(second_kernel, cells, strips),
         out_shape=shape((4, 8, 128, 128), F32),
-        in_specs=[HBM] + [VMEM] * 4, out_specs=HBM, scratch_shapes=scratch(4, 10) + out_scratch,
-        compiler_params=PARAMS, cost_estimate=cost(1, 8, LATE), name="second_late",
-    )(taps_two, got, small, x, inner)
-    return pl.pallas_call(
-        functools.partial(second_kernel, True, cells, strips),
-        out_shape=shape((4, 8, 128, 128), F32),
-        in_specs=[HBM] + [VMEM] * 5 + [HBM], out_specs=HBM, scratch_shapes=scratch(4, 10) + out_scratch,
-        input_output_aliases={6: 0}, compiler_params=PARAMS, cost_estimate=cost(1, 8), name="second_early",
-    )(taps_two, got, small, x, inner, z_two, out)
+        in_specs=[HBM] + [VMEM] * 5, out_specs=HBM,
+        scratch_shapes=scratch(6, 10) + [pltpu.VMEM((4, 8, 128, 128), F32), DMA, DMA((6,))],
+        compiler_params=PARAMS, cost_estimate=cost(2, 8), name="second",
+    )(taps_two, got, small, x, inner, z_two)
 
 
 def solution(mesh):

time: 81.1 us -> 78.7 us (0.970)
  Pallas kernels: 21.7 us -> 19.3 us
    pallas_call x2 -> x1, Pallas kernels: 10.4 us -> 8.18 us  [shards(): pl.pallas_call(functools.partial(second_kernel, cells, strips), out_shape...]
  transfers between devices with their start and end apart: 7 -> 7, of which waited for: 1 -> 1; matrix products, arithmetic and copies ran while one was open for 0% -> 0% of each run, Pallas kernels for 6% -> 0%
where the time goes in v3:
time: 78.7 us; the launch traced here: 78.4 us
  starting transfers between devices  29.4 us (37%)
  blocking collectives  24.7 us (31%)
  Pallas kernels  19.3 us (25%)
  waiting for transfers between devices  4.71 us (6%)
    all_to_all x1, blocking collectives, shards(): got = lax.all_to_all(pay, BOTH, 0, 0)  24.7 us
    all_to_all x1, starting transfers between devices, shards(): got = lax.all_to_all(pay, BOTH, 0, 0)  14.2 us
    pallas_call x1, Pallas kernels, shards(): pl.pallas_call(functools.partial(first_kernel, cells, strips), out_shape=...  8.59 us
    pallas_call x1, Pallas kernels, shards(): pl.pallas_call(functools.partial(second_kernel, cells, strips), out_shape...  8.18 us
    all_to_all x1, waiting for transfers between devices, shards(): got = lax.all_to_all(pay, BOTH, 0, 0)  4.69 us
    ppermute x1, starting transfers between devices, shards(): z_one = lax.ppermute(z_send, 'tm', later)  4.4 us
    ppermute x1, starting transfers between devices, shards(): z_far = lax.ppermute(jnp.where(odd, high, low), 'space', swap_far)  3.64 us
    ppermute x1, starting transfers between devices, shards(): z_two = lax.ppermute(send, 'tm', later)  2.91 us
  transfers between devices with their start and end apart: 7, of which 1 were waited for; matrix products, arithmetic and copies ran while one was open for 0% of the time, Pallas kernels for 0%

profile of v3, /device:TPU:1, one launch (start us, length us, event | category | flops | bytes accessed | tf_op | source)
XLA Modules:
  0.0 78.4 jit_solution(939510919076792719)
XLA Ops:
  0.0 2.6 %stats.1 = (bf16[4,8,128,128]{3,2,1,0:T(8,128)(2,1)S(1)}, f32[256,128]{1,0:T(8,128)}, bf16[2,8,128,128]{3,2,1,0:T(8,128)(2,1)S(1)}, bf16[4,2,128,128]{3,2,1,0:T(...) custom-call(bf16[4,8,128,128]{3,2,1,0:T(8,128)(2,1)} %x_hbm.1, f32[128]{0:T(128)} %refs_0_.1, ...), custom_call_target="tpu_custom_call" | custom-call | flops 4194304 | bytes 1048576 | tf_op jit(solution)/shard_map/stats/pallas_call | solution.py:275
  2.6 4.4 %collective-permute-start.2 = (bf16[2,8,128,128]{3,2,1,0:T(8,128)(2,1)S(1)}, bf16[2,8,128,128]{3,2,1,0:T(8,128)(2,1)S(1)}, u32[]{:S(2)}, u32[]{:S(2)}) collective-permute-start(bf16[2,8,128,128]{3,2,1,0:T(8,128)(2,1)S(1)} %get-tuple-element.19), channel_id=1, source_target_pairs={{0,32},{32,64},{64,96},{96,128},{128,160},{160,192},{192,224},{1,3... | collective-permute-start | bytes 1572872 | tf_op jit(solution)/shard_map/ppermute | solution.py:285
  7.0 14.2 %all-to-all-start = ((f32[256,1,128]{2,1,0:T(1,128)}), f32[256,1,128]{2,1,0:T(1,128)S(1)}, u32[]{:S(2)}, u32[]{:S(2)}) async-start(f32[256,1,128]{2,1,0:T(1,128)} %bitcast.3), calls=%async_computation | async-start | bytes 262144 | tf_op jit(solution)/shard_map/all_to_all | solution.py:288
  21.2 2.2 %collective-permute-start = (bf16[4,2,128,128]{3,2,1,0:T(8,128)(2,1)S(1)}, bf16[4,2,128,128]{3,2,1,0:T(8,128)(2,1)S(1)}, u32[]{:S(2)}, u32[]{:S(2)}) collective-permute-start(bf16[4,2,128,128]{3,2,1,0:T(8,128)(2,1)S(1)} %get-tuple-element.17), channel_id=1, source_target_pairs={{0,1},{1,0},{2,3},{3,2},{4,5},{5,4},{6,7},{7,6},{8,9},{9,8},{10,11... | collective-permute-start | bytes 786440 | tf_op jit(solution)/shard_map/ppermute | solution.py:286
  23.4 1.9 %collective-permute-start.1 = (bf16[4,2,128,128]{3,2,1,0:T(8,128)(2,1)S(1)}, bf16[4,2,128,128]{3,2,1,0:T(8,128)(2,1)S(1)}, u32[]{:S(2)}, u32[]{:S(2)}) collective-permute-start(bf16[4,2,128,128]{3,2,1,0:T(8,128)(2,1)S(1)} %get-tuple-element.18), channel_id=1, source_target_pairs={{1,2},{3,4},{5,6},{7,8},{9,10},{11,12},{13,14},{15,16},{17,18},{19... | collective-permute-start | bytes 786440 | tf_op jit(solution)/shard_map/ppermute | solution.py:287
  25.3 0.0 collective-permute-done.2.z_ref
  25.4 3.6 %collective-permute-start.4 = (bf16[2,2,128,128]{3,2,1,0:T(8,128)(2,1)S(1)}, bf16[2,2,128,128]{3,2,1,0:T(8,128)(2,1)S(1)}, u32[]{:S(2)}, u32[]{:S(2)}) collective-permute-start(bf16[2,2,128,128]{3,2,1,0:T(8,128)(2,1)S(1)} %get-tuple-element.23), channel_id=1, source_target_pairs={{1,2},{3,4},{5,6},{7,8},{9,10},{11,12},{13,14},{15,16},{17,18},{19... | collective-permute-start | bytes 393224 | tf_op jit(solution)/shard_map/ppermute | solution.py:292
  29.0 0.1 collective-permute-start.3
  29.1 4.7 %all-to-all-done = f32[256,1,128]{2,1,0:T(1,128)S(1)} async-done(((f32[256,1,128]{2,1,0:T(1,128)}), f32[256,1,128]{2,1,0:T(1,128)S(1)}, u32[]{:S(2)}, u32[]{:S(2)}) %all-to-all-start) | async-done | bytes 131104 | tf_op jit(solution)/shard_map/all_to_all | solution.py:288
  33.8 0.0 collective-permute-done.in_ref
  33.8 0.0 collective-permute-done.1.far_ref
  33.8 0.0 collective-permute-done.4.z_far_ref
  33.8 0.0 collective-permute-done.3.z_in_ref
  33.8 8.6 %first.1 = (f32[4,10,128,128]{3,2,1,0:T(8,128)S(1)}, f32[256,128]{1,0:T(8,128)S(1)}, bf16[2,10,128,128]{3,2,1,0:T(8,128)(2,1)S(1)}) custom-call(bf16[3,1152,128]{2,1,0:T(8,128)(2,1)} %bitcast.13, f32[256,128]{1,0:T(8,128)S(1)} %bitcast.10, f32[6,128]{1,0:T(8,128)S(1)} %get-tuple-element.15.small_ref, ...), custom_call_target="tpu_custom_call" | custom-call | flops 6039797760 | bytes 4194304 | tf_op jit(solution)/shard_map/first/pallas_call | solution.py:293
  42.4 2.9 %collective-permute-start.5 = (bf16[2,10,128,128]{3,2,1,0:T(8,128)(2,1)S(1)}, bf16[2,10,128,128]{3,2,1,0:T(8,128)(2,1)S(1)}, u32[]{:S(2)}, u32[]{:S(2)}) collective-permute-start(bf16[2,10,128,128]{3,2,1,0:T(8,128)(2,1)S(1)} %get-tuple-element.22), channel_id=1, source_target_pairs={{0,32},{32,64},{64,96},{96,128},{128,160},{160,192},{192,224},{1,3... | collective-permute-start | bytes 1966088 | tf_op jit(solution)/shard_map/ppermute | solution.py:300
  45.4 24.7 %all_to_all.22 = f32[256,1,128]{2,1,0:T(1,128)S(1)} all-to-all(f32[256,1,128]{2,1,0:T(1,128)S(1)} %bitcast.11), channel_id=1, replica_groups=mesh['tm'=8,'space'=32] {'tm','space'}, dimensions={0} | all-to-all | bytes 262144 | tf_op jit(solution)/shard_map/all_to_all | solution.py:299
  70.0 0.0 collective-permute-done.5.z_ref
  70.0 8.2 %second.1 = f32[4,8,128,128]{3,2,1,0:T(8,128)} custom-call(bf16[3,1152,128]{2,1,0:T(8,128)(2,1)} %bitcast.14, f32[256,128]{1,0:T(8,128)S(1)} %bitcast.12, f32[6,128]{1,0:T(8,128)S(1)} %get-tuple-element.15.small_ref, bf16[4,8,128,128]{3,2,1,0:T(8,128)(2,1)S(1)} %get-tuple-element.16.x_ref.feat_ref, f32[4,10,128,128]{3,2,1,0:T(8,128)S(1)} %get-tuple-element.21.x_ref, ...), custom_call_target="tpu_custom_call" | custom-call | flops 4831838208 | bytes 4194304 | tf_op jit(solution)/shard_map/second/pallas_call | solution.py:301
  (1 shorter events, 0.0 us)
Async XLA Ops:
  2.6 22.8 %collective-permute-start.2 = (bf16[2,8,128,128]{3,2,1,0:T(8,128)(2,1)S(1)}, bf16[2,8,128,128]{3,2,1,0:T(8,128)(2,1)S(1)}, u32[]{:S(2)}, u32[]{:S(2)}) collective-permute-start(bf16[2,8,128,128]{3,2,1,0:T(8,128)(2,1)S(1)} %get-tuple-element.19), channel_id=1, source_target_pairs={{0,32},{32,64},{64,96},{96,128},{128,160},{160,192},{192,224},{1,3... | collective-permute-start | bytes 1572872 | tf_op jit(solution)/shard_map/ppermute | solution.py:285
  7.0 26.8 %all-to-all-start = ((f32[256,1,128]{2,1,0:T(1,128)}), f32[256,1,128]{2,1,0:T(1,128)S(1)}, u32[]{:S(2)}, u32[]{:S(2)}) async-start(f32[256,1,128]{2,1,0:T(1,128)} %bitcast.3), calls=%async_computation | async-start | bytes 262144 | tf_op jit(solution)/shard_map/all_to_all | solution.py:288
  21.2 12.6 %collective-permute-start = (bf16[4,2,128,128]{3,2,1,0:T(8,128)(2,1)S(1)}, bf16[4,2,128,128]{3,2,1,0:T(8,128)(2,1)S(1)}, u32[]{:S(2)}, u32[]{:S(2)}) collective-permute-start(bf16[4,2,128,128]{3,2,1,0:T(8,128)(2,1)S(1)} %get-tuple-element.17), channel_id=1, source_target_pairs={{0,1},{1,0},{2,3},{3,2},{4,5},{5,4},{6,7},{7,6},{8,9},{9,8},{10,11... | collective-permute-start | bytes 786440 | tf_op jit(solution)/shard_map/ppermute | solution.py:286
  23.4 10.4 %collective-permute-start.1 = (bf16[4,2,128,128]{3,2,1,0:T(8,128)(2,1)S(1)}, bf16[4,2,128,128]{3,2,1,0:T(8,128)(2,1)S(1)}, u32[]{:S(2)}, u32[]{:S(2)}) collective-permute-start(bf16[4,2,128,128]{3,2,1,0:T(8,128)(2,1)S(1)} %get-tuple-element.18), channel_id=1, source_target_pairs={{1,2},{3,4},{5,6},{7,8},{9,10},{11,12},{13,14},{15,16},{17,18},{19... | collective-permute-start | bytes 786440 | tf_op jit(solution)/shard_map/ppermute | solution.py:287
  25.4 8.5 %collective-permute-start.4 = (bf16[2,2,128,128]{3,2,1,0:T(8,128)(2,1)S(1)}, bf16[2,2,128,128]{3,2,1,0:T(8,128)(2,1)S(1)}, u32[]{:S(2)}, u32[]{:S(2)}) collective-permute-start(bf16[2,2,128,128]{3,2,1,0:T(8,128)(2,1)S(1)} %get-tuple-element.23), channel_id=1, source_target_pairs={{1,2},{3,4},{5,6},{7,8},{9,10},{11,12},{13,14},{15,16},{17,18},{19... | collective-permute-start | bytes 393224 | tf_op jit(solution)/shard_map/ppermute | solution.py:292
  29.0 4.8 %collective-permute-start.3 = (bf16[2,2,128,128]{3,2,1,0:T(8,128)(2,1)S(1)}, bf16[2,2,128,128]{3,2,1,0:T(8,128)(2,1)S(1)}, u32[]{:S(2)}, u32[]{:S(2)}) collective-permute-start(bf16[2,2,128,128]{3,2,1,0:T(8,128)(2,1)S(1)} %get-tuple-element.24), channel_id=1, source_target_pairs={{0,1},{1,0},{2,3},{3,2},{4,5},{5,4},{6,7},{7,6},{8,9},{9,8},{10,11... | collective-permute-start | bytes 393224 | tf_op jit(solution)/shard_map/ppermute | solution.py:291
  42.4 27.6 %collective-permute-start.5 = (bf16[2,10,128,128]{3,2,1,0:T(8,128)(2,1)S(1)}, bf16[2,10,128,128]{3,2,1,0:T(8,128)(2,1)S(1)}, u32[]{:S(2)}, u32[]{:S(2)}) collective-permute-start(bf16[2,10,128,128]{3,2,1,0:T(8,128)(2,1)S(1)} %get-tuple-element.22), channel_id=1, source_target_pairs={{0,32},{32,64},{64,96},{96,128},{128,160},{160,192},{192,224},{1,3... | collective-permute-start | bytes 1966088 | tf_op jit(solution)/shard_map/ppermute | solution.py:300

commit v4 on v3

--- a/solution.py
+++ b/solution.py
@@ -47,6 +47,20 @@
         return d * d
 
     return mean, group_sum(column_sum(add_up(spread(i) for i in range(rows))))
+
+
+def shifted_sums(load, rows, shift):
+    first = second = None
+    for i in range(rows):
+        d = load(i) - shift[:1]
+        first = d if i == 0 else first + d
+        second = d * d if i == 0 else second + d * d
+    return group_sum(column_sum(first)), group_sum(column_sum(second))
+
+
+def joined(mean, spread, cells, first, second, more):
+    whole = cells + more
+    return mean + first / whole, spread + second - first * first / whole
 
 
 def payload(*entries):
@@ -110,19 +124,19 @@
     for copy in copies:
         copy.start()
     odd = (lax.axis_index("space") & 1) == 1
-    total = None
+    cells = float(per * 128 * MEMBERS)
+    load = lambda i: x_ref[i // per, i % per].astype(F32)
     for f in range(frames):
         copies[f].wait()
-        part = add_up(x_ref[f, r].astype(F32) for r in range(per))
-        total = part if f == 0 else total + part
+        if f == 0:
+            mean, spread = local_stats(load, per, cells)
         for r in range(2):
             low, high = x_ref[f, r], x_ref[f, per - 2 + r]
             in_ref[f, r] = jnp.where(odd, low, high)
             far_ref[f, r] = jnp.where(odd, high, low)
     z_ref[...] = x_ref[2:]
-    rows = frames * per
-    load = lambda i: x_ref[i // per, i % per].astype(F32)
-    mean, spread = local_stats(load, rows, float(rows * 128 * MEMBERS), total)
+    sums = shifted_sums(lambda i: load(per + i), (frames - 1) * per, mean)
+    mean, spread = joined(mean, spread, cells, *sums, (frames - 1) * cells)
     pay_ref[...] = jnp.broadcast_to(payload(mean, spread)[:1], pay_ref.shape)
     for copy in copies[frames:]:
         copy.wait()
@@ -139,25 +153,29 @@
     return jnp.where(space == 0, 0.0, 1.0), jnp.where(space == strips - 1, 0.0, 1.0)
 
 
-def first_kernel(cells, strips, kernel_hbm, got_ref, small_ref, x_ref, in_ref, far_ref,
-                 z_ref, z_in_ref, z_far_ref, inner_ref, pay_ref, send_ref, acts, taps, kernel, sem):
-    fetch = pltpu.make_async_copy(kernel_hbm, kernel, sem)
-    fetch.start()
-    mean, slope, half, bias = norm_constants(got_ref, small_ref, 0, cells)
+def first_kernel(early, cells, strips, *refs):
+    if early:
+        kernel, consts_ref, small_ref, x_ref, in_ref, far_ref, z_ref, z_in_ref, z_far_ref, inner_ref, pay_ref, acts, taps = refs
+        mean, slope, half, late, spread = (consts_ref[i : i + 1] for i in range(5))
+        bias = small_ref[2:3]
+    else:
+        kernel_hbm, got_ref, small_ref, x_ref, in_ref, far_ref, inner_ref, send_ref, consts_ref, kernel, acts, taps, sem = refs
+        fetch = pltpu.make_async_copy(kernel_hbm, kernel, sem)
+        fetch.start()
+        mean, slope, half, bias = norm_constants(got_ref, small_ref, 0, cells)
     top, bottom = edges(strips)
     odd = (lax.axis_index("space") & 1) == 1
     start = lax.axis_index("tm") == 0
 
-    def frame(own, near, far, f):
-        for r in range(12):
-            if 2 <= r < 10:
-                x, keep = own(r - 2), None
-            else:
-                high = r >= 10
-                i = r - 10 if high else r
-                a, b = near(i), far(i)
-                x, keep = (jnp.where(odd, b, a), bottom) if high else (jnp.where(odd, a, b), top)
-            put_act(x.astype(F32) - mean, slope, half, keep, acts, f, r)
+    def act(own, near, far, f, r):
+        if 2 <= r < 10:
+            x, keep = own(r - 2), None
+        else:
+            high = r >= 10
+            i = r - 10 if high else r
+            a, b = near(i), far(i)
+            x, keep = (jnp.where(odd, b, a), bottom) if high else (jnp.where(odd, a, b), top)
+        put_act(x.astype(F32) - mean, slope, half, keep, acts, f, r)
 
     def of(ref, f):
         return lambda r: ref[f, r]
@@ -165,35 +183,36 @@
     def carried(ref, z, f):
         return lambda r: jnp.where(start, ref[0, r], z[f, r])
 
-    def conv(pair):
-        got = conv_pair(acts, taps, 2 * pair, 0, 10)
+    if early:
+        build_taps(kernel, taps)
+        for r in range(12):
+            for f in range(2):
+                act(carried(x_ref, z_ref, f), carried(in_ref, z_in_ref, f), carried(far_ref, z_far_ref, f), f, r)
+                act(of(x_ref, f), of(in_ref, f), of(far_ref, f), 2 + f, r)
+    else:
+        for f in range(4):
+            if f == 2:
+                fetch.wait()
+                build_taps(kernel, taps)
+            for r in range(12):
+                act(of(x_ref, f), of(in_ref, f), of(far_ref, f), f, r)
+    got = conv_pair(acts, taps, 0, 0, 10)
+    for o in range(2):
+        inner_ref[o] = (got[:, o * 128 : (o + 1) * 128] + bias).reshape(10, 128, 128)
+    own = lambda i: inner_ref[i // 8, 1 + i % 8]
+    if early:
+        m, spread = joined(late, spread, cells / 2, *shifted_sums(own, 16, late), cells / 2)
+        m, spread, late = (jnp.broadcast_to(v[:1], (8, 128)) for v in (m, spread, late))
+        pay_ref[...] = jnp.broadcast_to(payload(m, spread, late)[:1], pay_ref.shape)
+    else:
+        late, spread = local_stats(own, 16, cells / 2)
         for o in range(2):
-            inner_ref[2 * pair + o] = (got[:, o * 128 : (o + 1) * 128] + bias).reshape(10, 128, 128)
-
-    for f in range(4):
-        if f == 2:
-            fetch.wait()
-            build_taps(kernel, taps)
-        frame(of(x_ref, f), of(in_ref, f), of(far_ref, f), 2 + f)
-    def stats(pair):
-        return local_stats(lambda i: inner_ref[2 * pair + i // 8, 1 + i % 8], 16, cells / 2)
-
-    conv(1)
-    for f in range(2):
-        frame(carried(x_ref, z_ref, f), carried(in_ref, z_in_ref, f), carried(far_ref, z_far_ref, f), f)
-    late, late_spread = stats(1)
-    for o in range(2):
-        send_ref[o] = (inner_ref[2 + o] - late[:1]).astype(BF16)
-    conv(0)
-    early, early_spread = stats(0)
-    gap = late - early
-    spread = late_spread + early_spread + gap * gap * (cells / 4)
-    pay_ref[...] = jnp.broadcast_to(payload((late + early) * 0.5, spread, late)[:1], pay_ref.shape)
-
-
-def second_kernel(cells, strips, kernel_hbm, got_ref, small_ref, feat_ref, x_ref, z_ref, out_hbm, acts, taps, kernel, out, sem, sems):
-    fetch = pltpu.make_async_copy(kernel_hbm, kernel, sem)
-    fetch.start()
+            send_ref[o] = (inner_ref[o] - late[:1]).astype(BF16)
+        for i, v in enumerate((mean, slope, half, late, spread)):
+            consts_ref[i : i + 1] = v[:1]
+
+
+def second_kernel(cells, strips, kernel_ref, got_ref, small_ref, feat_ref, b_ref, a_ref, z_ref, out_hbm, acts, taps, out, sems):
     mean, slope, half, bias = norm_constants(got_ref, small_ref, 3, cells)
     top, bottom = edges(strips)
     tm = lax.axis_index("tm")
@@ -201,9 +220,8 @@
     sender = got_ref[pl.ds(jnp.maximum(tm - 1, 0) * strips + lax.axis_index("space"), 1)]
     base = mean - pick(jnp.broadcast_to(sender, (8, 128)), 2)[:1]
 
-    def frame(off, f):
-        for r in range(10):
-            put_act(off(r), slope, half, {0: top, 9: bottom}.get(r), acts, f, r)
+    def act(off, f, r):
+        put_act(off, slope, half, {0: top, 9: bottom}.get(r), acts, f, r)
 
     copies = []
 
@@ -217,14 +235,14 @@
             copies.append(pltpu.make_async_copy(out.at[here], out_hbm.at[here], sems.at[len(copies)]))
             copies[-1].start()
 
-    for f in range(4):
-        if f == 2:
-            fetch.wait()
-            build_taps(kernel, taps)
-        frame(lambda r: x_ref[f, r] - mean, 2 + f)
+    build_taps(kernel_ref, taps)
+    for r in range(10):
+        for f in range(4):
+            act((b_ref if f < 2 else a_ref)[f % 2, r] - mean, 2 + f, r)
     conv(1, 0, 8)
-    for f in range(2):
-        frame(lambda r: jnp.where(start, x_ref[0, r] - mean, z_ref[f, r].astype(F32) - base), f)
+    for r in range(10):
+        for f in range(2):
+            act(jnp.where(start, b_ref[0, r] - mean, z_ref[f, r].astype(F32) - base), f, r)
     for at in (0, 4):
         conv(0, at, 4)
     for copy in copies:
@@ -241,7 +259,6 @@
     return [
         pltpu.VMEM((3, frames, rows, 128, 128), BF16),
         pltpu.VMEM((36 * 128, 256), BF16),
-        pltpu.VMEM((3, 9 * 128, 128), BF16),
     ]
 
 
@@ -271,7 +288,7 @@
     taps_one = kernel_one.reshape(3, 9 * 128, 128)
     taps_two = kernel_two.reshape(3, 9 * 128, 128)
 
-    taps_one, taps_two = in_hbm(taps_one), in_hbm(taps_two)
+    taps_one = in_hbm(taps_one)
     x, pay, z_send, in_send, far_send, small = pl.pallas_call(
         stats_kernel,
         out_shape=[
@@ -290,21 +307,27 @@
     low, high = z_one[:, :2], z_one[:, 6:]
     z_near = lax.ppermute(jnp.where(odd, low, high), "space", swap_in)
     z_far = lax.ppermute(jnp.where(odd, high, low), "space", swap_far)
-    inner, pay, send = pl.pallas_call(
-        functools.partial(first_kernel, cells, strips),
-        out_shape=[shape((4, 10, 128, 128), F32), shape((devices, 128), F32), shape((2, 10, 128, 128), BF16)],
-        in_specs=[HBM] + [VMEM] * 8, out_specs=[VMEM] * 3, scratch_shapes=scratch(6, 12) + [DMA],
-        compiler_params=PARAMS, cost_estimate=cost(2, 10), name="first",
-    )(taps_one, got, small, x, near, far, z_one, z_near, z_far)
+    inner_a, send, consts, kernel = pl.pallas_call(
+        functools.partial(first_kernel, False, cells, strips),
+        out_shape=[shape((2, 10, 128, 128), F32), shape((2, 10, 128, 128), BF16), shape((8, 128), F32), shape((3, 9 * 128, 128), BF16)],
+        in_specs=[HBM] + [VMEM] * 5, out_specs=[VMEM] * 4, scratch_shapes=scratch(4, 12) + [DMA],
+        compiler_params=PARAMS, cost_estimate=cost(1, 10), name="first_late",
+    )(taps_one, got, small, x, near, far)
+    z_two = lax.ppermute(send, "tm", later)
+    inner_b, pay = pl.pallas_call(
+        functools.partial(first_kernel, True, cells, strips),
+        out_shape=[shape((2, 10, 128, 128), F32), shape((devices, 128), F32)],
+        in_specs=[VMEM] * 9, out_specs=[VMEM] * 2, scratch_shapes=scratch(4, 12),
+        compiler_params=PARAMS, cost_estimate=cost(1, 10), name="first_early",
+    )(kernel, consts, small, x, near, far, z_one, z_near, z_far)
     got = lax.all_to_all(pay, BOTH, 0, 0)
-    z_two = lax.ppermute(send, "tm", later)
     return pl.pallas_call(
         functools.partial(second_kernel, cells, strips),
         out_shape=shape((4, 8, 128, 128), F32),
-        in_specs=[HBM] + [VMEM] * 5, out_specs=HBM,
-        scratch_shapes=scratch(6, 10) + [pltpu.VMEM((4, 8, 128, 128), F32), DMA, DMA((6,))],
+        in_specs=[VMEM] * 7, out_specs=HBM,
+        scratch_shapes=scratch(6, 10) + [pltpu.VMEM((4, 8, 128, 128), F32), DMA((6,))],
         compiler_params=PARAMS, cost_estimate=cost(2, 8), name="second",
-    )(taps_two, got, small, x, inner, z_two)
+    )(taps_two, got, small, x, inner_b, inner_a, z_two)
 
 
 def solution(mesh):

time: 78.7 us -> 76.3 us (0.970)
  blocking collectives: 24.7 us -> 18.9 us
  waiting for transfers between devices: 4.71 us -> 9.24 us
  starting transfers between devices: 29.4 us -> 27.8 us
    all_to_all x1, blocking collectives: 24.7 us -> 18.9 us  [shards(): got = lax.all_to_all(pay, BOTH, 0, 0)]
    all_to_all x1, waiting for transfers between devices: 4.69 us -> 9.22 us  [shards(): got = lax.all_to_all(pay, BOTH, 0, 0)]
    pallas_call x1 -> x2, Pallas kernels: 8.59 us -> 9.96 us  [the longest x1 5.4 us: shards(): pl.pallas_call(functools.partial(first_kernel, False, cells, strips), out...]
    ppermute x1, starting transfers between devices: 2.23 us -> 1.04 us  [shards(): near = lax.ppermute(in_send, 'space', swap_in)]
    all_to_all x1, starting transfers between devices: 14.2 us -> 13.1 us  [shards(): got = lax.all_to_all(pay, BOTH, 0, 0)]
    ppermute x1, starting transfers between devices: 1.91 us -> 3.02 us  [shards(): far = lax.ppermute(far_send, 'space', swap_far)]
    pallas_call x1, Pallas kernels: 8.18 us -> 7.19 us  [shards(): pl.pallas_call(functools.partial(second_kernel, cells, strips), out_shape...]
  transfers between devices with their start and end apart: 7 -> 7, of which waited for: 1 -> 1; matrix products, arithmetic and copies ran while one was open for 0% -> 0% of each run, Pallas kernels for 0% -> 13%
where the time goes in v4:
time: 76.3 us; the launch traced here: 76 us
  starting transfers between devices  27.8 us (36%)
  Pallas kernels  19.8 us (26%)
  blocking collectives  18.9 us (25%)
  waiting for transfers between devices  9.24 us (12%)
    all_to_all x1, blocking collectives, shards(): got = lax.all_to_all(pay, BOTH, 0, 0)  18.9 us
    all_to_all x1, starting transfers between devices, shards(): got = lax.all_to_all(pay, BOTH, 0, 0)  13.1 us
    all_to_all x1, waiting for transfers between devices, shards(): got = lax.all_to_all(pay, BOTH, 0, 0)  9.22 us
    pallas_call x1, Pallas kernels, shards(): pl.pallas_call(functools.partial(second_kernel, cells, strips), out_shape...  7.19 us
    pallas_call x1, Pallas kernels, shards(): pl.pallas_call(functools.partial(first_kernel, False, cells, strips), out...  5.4 us
    pallas_call x1, Pallas kernels, shards(): pl.pallas_call(functools.partial(first_kernel, True, cells, strips), out_...  4.56 us
    ppermute x1, starting transfers between devices, shards(): z_one = lax.ppermute(z_send, 'tm', later)  4.4 us
    ppermute x1, starting transfers between devices, shards(): z_far = lax.ppermute(jnp.where(odd, high, low), 'space', swap_far)  3.54 us
  transfers between devices with their start and end apart: 7, of which 1 were waited for; matrix products, arithmetic and copies ran while one was open for 0% of the time, Pallas kernels for 13%

profile of v4, /device:TPU:1, one launch (start us, length us, event | category | flops | bytes accessed | tf_op | source)
XLA Modules:
  0.0 76.0 jit_solution(16422392929163488459)
XLA Ops:
  0.0 2.6 %stats.1 = (bf16[4,8,128,128]{3,2,1,0:T(8,128)(2,1)S(1)}, f32[256,128]{1,0:T(8,128)}, bf16[2,8,128,128]{3,2,1,0:T(8,128)(2,1)S(1)}, bf16[4,2,128,128]{3,2,1,0:T(...) custom-call(bf16[4,8,128,128]{3,2,1,0:T(8,128)(2,1)} %x_hbm.1, f32[128]{0:T(128)} %refs_0_.1, ...), custom_call_target="tpu_custom_call" | custom-call | flops 4194304 | bytes 1048576 | tf_op jit(solution)/shard_map/stats/pallas_call | solution.py:292
  2.6 4.4 %collective-permute-start.2 = (bf16[2,8,128,128]{3,2,1,0:T(8,128)(2,1)S(1)}, bf16[2,8,128,128]{3,2,1,0:T(8,128)(2,1)S(1)}, u32[]{:S(2)}, u32[]{:S(2)}) collective-permute-start(bf16[2,8,128,128]{3,2,1,0:T(8,128)(2,1)S(1)} %get-tuple-element.24), channel_id=1, source_target_pairs={{0,32},{32,64},{64,96},{96,128},{128,160},{160,192},{192,224},{1,3... | collective-permute-start | bytes 1572872 | tf_op jit(solution)/shard_map/ppermute | solution.py:302
  7.0 1.0 %collective-permute-start = (bf16[4,2,128,128]{3,2,1,0:T(8,128)(2,1)S(1)}, bf16[4,2,128,128]{3,2,1,0:T(8,128)(2,1)S(1)}, u32[]{:S(2)}, u32[]{:S(2)}) collective-permute-start(bf16[4,2,128,128]{3,2,1,0:T(8,128)(2,1)S(1)} %get-tuple-element.20), channel_id=1, source_target_pairs={{0,1},{1,0},{2,3},{3,2},{4,5},{5,4},{6,7},{7,6},{8,9},{9,8},{10,11... | collective-permute-start | bytes 786440 | tf_op jit(solution)/shard_map/ppermute | solution.py:303
  8.1 3.0 %collective-permute-start.1 = (bf16[4,2,128,128]{3,2,1,0:T(8,128)(2,1)S(1)}, bf16[4,2,128,128]{3,2,1,0:T(8,128)(2,1)S(1)}, u32[]{:S(2)}, u32[]{:S(2)}) collective-permute-start(bf16[4,2,128,128]{3,2,1,0:T(8,128)(2,1)S(1)} %get-tuple-element.21), channel_id=1, source_target_pairs={{1,2},{3,4},{5,6},{7,8},{9,10},{11,12},{13,14},{15,16},{17,18},{19... | collective-permute-start | bytes 786440 | tf_op jit(solution)/shard_map/ppermute | solution.py:304
  11.1 13.1 %all-to-all-start = ((f32[256,1,128]{2,1,0:T(1,128)}), f32[256,1,128]{2,1,0:T(1,128)S(1)}, u32[]{:S(2)}, u32[]{:S(2)}) async-start(f32[256,1,128]{2,1,0:T(1,128)} %bitcast.3), calls=%async_computation | async-start | bytes 262144 | tf_op jit(solution)/shard_map/all_to_all | solution.py:305
  24.2 0.0 collective-permute-done.2.refs_6_
  24.2 3.5 %collective-permute-start.4 = (bf16[2,2,128,128]{3,2,1,0:T(8,128)(2,1)S(1)}, bf16[2,2,128,128]{3,2,1,0:T(8,128)(2,1)S(1)}, u32[]{:S(2)}, u32[]{:S(2)}) collective-permute-start(bf16[2,2,128,128]{3,2,1,0:T(8,128)(2,1)S(1)} %get-tuple-element.29), channel_id=1, source_target_pairs={{1,2},{3,4},{5,6},{7,8},{9,10},{11,12},{13,14},{15,16},{17,18},{19... | collective-permute-start | bytes 393224 | tf_op jit(solution)/shard_map/ppermute | solution.py:309
  27.8 0.1 collective-permute-start.3
  27.9 9.2 %all-to-all-done = f32[256,1,128]{2,1,0:T(1,128)S(1)} async-done(((f32[256,1,128]{2,1,0:T(1,128)}), f32[256,1,128]{2,1,0:T(1,128)S(1)}, u32[]{:S(2)}, u32[]{:S(2)}) %all-to-all-start) | async-done | bytes 131104 | tf_op jit(solution)/shard_map/all_to_all | solution.py:305
  37.1 0.0 collective-permute-done.refs_4_
  37.1 0.0 collective-permute-done.1.refs_5_
  37.1 5.4 %first_late.1 = (f32[2,10,128,128]{3,2,1,0:T(8,128)S(1)}, bf16[2,10,128,128]{3,2,1,0:T(8,128)(2,1)S(1)}, f32[8,128]{1,0:T(8,128)S(1)}, bf16[3,1152,128]{2,1,0:T(8,128)(2,1)S(1)}) custom-call(bf16[3,1152,128]{2,1,0:T(8,128)(2,1)} %bitcast.14, f32[256,128]{1,0:T(8,128)S(1)} %bitcast.10, f32[6,128]{1,0:T(8,128)S(1)} %get-tuple-element.18.refs_2_.small_ref, ...), custom_call_target="tpu_custom_call" | custom-call | flops 3019898880 | bytes 4194304 | tf_op jit(solution)/shard_map/first_late/pallas_call | solution.py:310
  42.5 2.6 %collective-permute-start.5 = (bf16[2,10,128,128]{3,2,1,0:T(8,128)(2,1)S(1)}, bf16[2,10,128,128]{3,2,1,0:T(8,128)(2,1)S(1)}, u32[]{:S(2)}, u32[]{:S(2)}) collective-permute-start(bf16[2,10,128,128]{3,2,1,0:T(8,128)(2,1)S(1)} %get-tuple-element.28), channel_id=1, source_target_pairs={{0,32},{32,64},{64,96},{96,128},{128,160},{160,192},{192,224},{1,3... | collective-permute-start | bytes 1966088 | tf_op jit(solution)/shard_map/ppermute | solution.py:316
  45.1 0.0 collective-permute-done.4.refs_8_
  45.1 0.0 collective-permute-done.3.refs_7_
  45.1 0.0 copy-start
  45.2 4.6 %first_early.1 = (f32[2,10,128,128]{3,2,1,0:T(8,128)S(1)}, f32[256,128]{1,0:T(8,128)S(1)}) custom-call(bf16[3,1152,128]{2,1,0:T(8,128)(2,1)S(1)} %get-tuple-element.22.refs_0_, f32[8,128]{1,0:T(8,128)S(1)} %get-tuple-element.23.refs_1_, f32[6,128]{1,0:T(8,128)S(1)} %get-tuple-element.18.refs_2_.small_ref, ...), custom_call_target="tpu_custom_call" | custom-call | flops 3019898880 | bytes 4194304 | tf_op jit(solution)/shard_map/first_early/pallas_call | solution.py:317
  49.7 18.9 %all_to_all.22 = f32[256,1,128]{2,1,0:T(1,128)S(1)} all-to-all(f32[256,1,128]{2,1,0:T(1,128)S(1)} %bitcast.12), channel_id=1, replica_groups=mesh['tm'=8,'space'=32] {'tm','space'}, dimensions={0} | all-to-all | bytes 262144 | tf_op jit(solution)/shard_map/all_to_all | solution.py:323
  68.6 0.0 collective-permute-done.5.z_ref
  68.6 0.0 copy-done
  68.6 7.2 %second.1 = f32[4,8,128,128]{3,2,1,0:T(8,128)} custom-call(bf16[3,1152,128]{2,1,0:T(8,128)(2,1)S(1)} %bitcast.13, f32[256,128]{1,0:T(8,128)S(1)} %bitcast.11, f32[6,128]{1,0:T(8,128)S(1)} %get-tuple-element.18.refs_2_.small_ref, bf16[4,8,128,128]{3,2,1,0:T(8,128)(2,1)S(1)} %get-tuple-element.19.refs_3_.feat_ref, ...), custom_call_target="tpu_custom_call" | custom-call | flops 4831838208 | bytes 4194304 | tf_op jit(solution)/shard_map/second/pallas_call | solution.py:324
  (1 shorter events, 0.0 us)
Async XLA Ops:
  2.6 21.5 %collective-permute-start.2 = (bf16[2,8,128,128]{3,2,1,0:T(8,128)(2,1)S(1)}, bf16[2,8,128,128]{3,2,1,0:T(8,128)(2,1)S(1)}, u32[]{:S(2)}, u32[]{:S(2)}) collective-permute-start(bf16[2,8,128,128]{3,2,1,0:T(8,128)(2,1)S(1)} %get-tuple-element.24), channel_id=1, source_target_pairs={{0,32},{32,64},{64,96},{96,128},{128,160},{160,192},{192,224},{1,3... | collective-permute-start | bytes 1572872 | tf_op jit(solution)/shard_map/ppermute | solution.py:302
  7.0 30.1 %collective-permute-start = (bf16[4,2,128,128]{3,2,1,0:T(8,128)(2,1)S(1)}, bf16[4,2,128,128]{3,2,1,0:T(8,128)(2,1)S(1)}, u32[]{:S(2)}, u32[]{:S(2)}) collective-permute-start(bf16[4,2,128,128]{3,2,1,0:T(8,128)(2,1)S(1)} %get-tuple-element.20), channel_id=1, source_target_pairs={{0,1},{1,0},{2,3},{3,2},{4,5},{5,4},{6,7},{7,6},{8,9},{9,8},{10,11... | collective-permute-start | bytes 786440 | tf_op jit(solution)/shard_map/ppermute | solution.py:303
  8.1 29.0 %collective-permute-start.1 = (bf16[4,2,128,128]{3,2,1,0:T(8,128)(2,1)S(1)}, bf16[4,2,128,128]{3,2,1,0:T(8,128)(2,1)S(1)}, u32[]{:S(2)}, u32[]{:S(2)}) collective-permute-start(bf16[4,2,128,128]{3,2,1,0:T(8,128)(2,1)S(1)} %get-tuple-element.21), channel_id=1, source_target_pairs={{1,2},{3,4},{5,6},{7,8},{9,10},{11,12},{13,14},{15,16},{17,18},{19... | collective-permute-start | bytes 786440 | tf_op jit(solution)/shard_map/ppermute | solution.py:304
  11.1 26.0 %all-to-all-start = ((f32[256,1,128]{2,1,0:T(1,128)}), f32[256,1,128]{2,1,0:T(1,128)S(1)}, u32[]{:S(2)}, u32[]{:S(2)}) async-start(f32[256,1,128]{2,1,0:T(1,128)} %bitcast.3), calls=%async_computation | async-start | bytes 262144 | tf_op jit(solution)/shard_map/all_to_all | solution.py:305
  24.2 20.9 %collective-permute-start.4 = (bf16[2,2,128,128]{3,2,1,0:T(8,128)(2,1)S(1)}, bf16[2,2,128,128]{3,2,1,0:T(8,128)(2,1)S(1)}, u32[]{:S(2)}, u32[]{:S(2)}) collective-permute-start(bf16[2,2,128,128]{3,2,1,0:T(8,128)(2,1)S(1)} %get-tuple-element.29), channel_id=1, source_target_pairs={{1,2},{3,4},{5,6},{7,8},{9,10},{11,12},{13,14},{15,16},{17,18},{19... | collective-permute-start | bytes 393224 | tf_op jit(solution)/shard_map/ppermute | solution.py:309
  27.8 17.4 %collective-permute-start.3 = (bf16[2,2,128,128]{3,2,1,0:T(8,128)(2,1)S(1)}, bf16[2,2,128,128]{3,2,1,0:T(8,128)(2,1)S(1)}, u32[]{:S(2)}, u32[]{:S(2)}) collective-permute-start(bf16[2,2,128,128]{3,2,1,0:T(8,128)(2,1)S(1)} %get-tuple-element.30), channel_id=1, source_target_pairs={{0,1},{1,0},{2,3},{3,2},{4,5},{5,4},{6,7},{7,6},{8,9},{9,8},{10,11... | collective-permute-start | bytes 393224 | tf_op jit(solution)/shard_map/ppermute | solution.py:308
  42.5 26.2 %collective-permute-start.5 = (bf16[2,10,128,128]{3,2,1,0:T(8,128)(2,1)S(1)}, bf16[2,10,128,128]{3,2,1,0:T(8,128)(2,1)S(1)}, u32[]{:S(2)}, u32[]{:S(2)}) collective-permute-start(bf16[2,10,128,128]{3,2,1,0:T(8,128)(2,1)S(1)} %get-tuple-element.28), channel_id=1, source_target_pairs={{0,32},{32,64},{64,96},{96,128},{128,160},{160,192},{192,224},{1,3... | collective-permute-start | bytes 1966088 | tf_op jit(solution)/shard_map/ppermute | solution.py:316
  45.1 23.5 %copy-start = (bf16[3,3,3,128,128]{4,3,2,1,0:T(8,128)(2,1)S(1)}, bf16[3,3,3,128,128]{4,3,2,1,0:T(8,128)(2,1)}, u32[]{:S(2)}) copy-start(bf16[3,3,3,128,128]{4,3,2,1,0:T(8,128)(2,1)} %param.16) | copy-start | bytes 2654212

commit v5 on v4

--- a/solution.py
+++ b/solution.py
@@ -93,27 +93,34 @@
     y = h + h * jnp.tanh(h)
     if keep is not None:
         y = y * keep
-    row = lax.broadcasted_iota(jnp.int32, y.shape, 0)
-    out[0, f, r] = jnp.where(row == 0, 0.0, pltpu.roll(y, 1, 0)).astype(BF16)
-    out[1, f, r] = y.astype(BF16)
-    out[2, f, r] = jnp.where(row == 127, 0.0, pltpu.roll(y, 127, 0)).astype(BF16)
-
-
-def build_taps(kernel, taps):
-    zero = jnp.zeros((9 * 128, 128), BF16)
-    for f in range(4):
-        at = pl.ds(f * 9 * 128, 9 * 128)
-        taps[at, :128] = kernel[f] if f < 3 else zero
-        taps[at, 128:] = kernel[f - 1] if f > 0 else zero
-
-
-def conv_pair(acts, taps, first, at, rows):
-    pieces = []
+    out[f, r] = y.astype(BF16)
+
+
+def build_taps(kernel, mid, side):
+    zero = jnp.zeros((128, 128), BF16)
+    tap = lambda a, i, j: kernel[a, (3 * i + j) * 128 : (3 * i + j + 1) * 128]
     for f in range(4):
         for i in range(3):
-            for j in range(3):
-                pieces.append(acts[j, first + f, pl.ds(at + i, rows)].reshape(rows * 128, 128))
-    return jnp.dot(jnp.concatenate(pieces, axis=-1), taps[...], preferred_element_type=F32)
+            at = pl.ds((3 * f + i) * 128, 128)
+            mid[at, :128] = tap(f, i, 1) if f < 3 else zero
+            mid[at, 128:] = tap(f - 1, i, 1) if f > 0 else zero
+            if f < 3:
+                side[at, :128] = tap(f, i, 0)
+                side[at, 128:] = tap(f, i, 2)
+
+
+def conv_pair(acts, mid, side, first, at, rows, put):
+    pieces = [[acts[first + f, pl.ds(at + i, rows)].reshape(rows * 128, 128) for i in range(3)] for f in range(4)]
+    dot = lambda blocks, taps: jnp.dot(jnp.concatenate(blocks, axis=-1), taps[...], preferred_element_type=F32)
+    centre = dot(sum(pieces, []), mid)
+    col = lax.broadcasted_iota(jnp.int32, (128, 128), 0)
+    for o in range(2):
+        sides = dot(sum(pieces[o : o + 3], []), side)
+        for r in range(rows):
+            here = slice(r * 128, (r + 1) * 128)
+            left = jnp.where(col == 0, 0.0, pltpu.roll(sides[here, :128], 1, 0))
+            right = jnp.where(col == 127, 0.0, pltpu.roll(sides[here, 128:], 127, 0))
+            put(o, at + r, centre[here, o * 128 : (o + 1) * 128] + left + right)
 
 
 def stats_kernel(x_hbm, *refs):
@@ -142,6 +149,14 @@
         copy.wait()
 
 
+def pack_kernel(z_ref, near_ref, far_ref):
+    per = z_ref.shape[1]
+    odd = lax.axis_index("space") & 1
+    for f in range(2):
+        near_ref[f] = z_ref[f, pl.ds((1 - odd) * (per - 2), 2)]
+        far_ref[f] = z_ref[f, pl.ds(odd * (per - 2), 2)]
+
+
 def norm_constants(got_ref, small_ref, at, cells):
     mean, scale = whole_stats(got_ref, cells)
     gain, shift, bias = (small_ref[at + i : at + i + 1] for i in range(3))
@@ -155,11 +170,11 @@
 
 def first_kernel(early, cells, strips, *refs):
     if early:
-        kernel, consts_ref, small_ref, x_ref, in_ref, far_ref, z_ref, z_in_ref, z_far_ref, inner_ref, pay_ref, acts, taps = refs
+        kernel, consts_ref, small_ref, x_ref, in_ref, far_ref, z_ref, z_in_ref, z_far_ref, inner_ref, pay_ref, acts, mid, side = refs
         mean, slope, half, late, spread = (consts_ref[i : i + 1] for i in range(5))
         bias = small_ref[2:3]
     else:
-        kernel_hbm, got_ref, small_ref, x_ref, in_ref, far_ref, inner_ref, send_ref, consts_ref, kernel, acts, taps, sem = refs
+        kernel_hbm, got_ref, small_ref, x_ref, in_ref, far_ref, inner_ref, send_ref, consts_ref, kernel, acts, mid, side, sem = refs
         fetch = pltpu.make_async_copy(kernel_hbm, kernel, sem)
         fetch.start()
         mean, slope, half, bias = norm_constants(got_ref, small_ref, 0, cells)
@@ -184,7 +199,7 @@
         return lambda r: jnp.where(start, ref[0, r], z[f, r])
 
     if early:
-        build_taps(kernel, taps)
+        build_taps(kernel, mid, side)
         for r in range(12):
             for f in range(2):
                 act(carried(x_ref, z_ref, f), carried(in_ref, z_in_ref, f), carried(far_ref, z_far_ref, f), f, r)
@@ -193,12 +208,14 @@
         for f in range(4):
             if f == 2:
                 fetch.wait()
-                build_taps(kernel, taps)
+                build_taps(kernel, mid, side)
             for r in range(12):
                 act(of(x_ref, f), of(in_ref, f), of(far_ref, f), f, r)
-    got = conv_pair(acts, taps, 0, 0, 10)
-    for o in range(2):
-        inner_ref[o] = (got[:, o * 128 : (o + 1) * 128] + bias).reshape(10, 128, 128)
+
+    def put(o, r, value):
+        inner_ref[o, r] = value + bias
+
+    conv_pair(acts, mid, side, 0, 0, 10, put)
     own = lambda i: inner_ref[i // 8, 1 + i % 8]
     if early:
         m, spread = joined(late, spread, cells / 2, *shifted_sums(own, 16, late), cells / 2)
@@ -212,7 +229,7 @@
             consts_ref[i : i + 1] = v[:1]
 
 
-def second_kernel(cells, strips, kernel_ref, got_ref, small_ref, feat_ref, b_ref, a_ref, z_ref, out_hbm, acts, taps, out, sems):
+def second_kernel(cells, strips, kernel_ref, got_ref, small_ref, feat_ref, b_ref, a_ref, z_ref, out_hbm, acts, mid, side, out, sems):
     mean, slope, half, bias = norm_constants(got_ref, small_ref, 3, cells)
     top, bottom = edges(strips)
     tm = lax.axis_index("tm")
@@ -226,16 +243,18 @@
     copies = []
 
     def conv(pair, at, rows):
-        got = conv_pair(acts, taps, 2 * pair, at, rows)
+        def put(o, r, value):
+            f = 2 * pair + o
+            out[f, r] = feat_ref[f, r].astype(F32) + (value + bias)
+
+        conv_pair(acts, mid, side, 2 * pair, at, rows, put)
         for o in range(2):
             f = 2 * pair + o
-            part = (got[:, o * 128 : (o + 1) * 128] + bias).reshape(rows, 128, 128)
-            out[f, pl.ds(at, rows)] = feat_ref[f, pl.ds(at, rows)].astype(F32) + part
             here = (f, pl.ds(at, rows))
             copies.append(pltpu.make_async_copy(out.at[here], out_hbm.at[here], sems.at[len(copies)]))
             copies[-1].start()
 
-    build_taps(kernel_ref, taps)
+    build_taps(kernel_ref, mid, side)
     for r in range(10):
         for f in range(4):
             act((b_ref if f < 2 else a_ref)[f % 2, r] - mean, 2 + f, r)
@@ -257,8 +276,9 @@
 
 def scratch(frames, rows):
     return [
-        pltpu.VMEM((3, frames, rows, 128, 128), BF16),
-        pltpu.VMEM((36 * 128, 256), BF16),
+        pltpu.VMEM((frames, rows, 128, 128), BF16),
+        pltpu.VMEM((12 * 128, 256), BF16),
+        pltpu.VMEM((9 * 128, 256), BF16),
     ]
 
 
@@ -303,10 +323,12 @@
     near = lax.ppermute(in_send, "space", swap_in)
     far = lax.ppermute(far_send, "space", swap_far)
     got = lax.all_to_all(pay, BOTH, 0, 0)
-    odd = (lax.axis_index("space") & 1) == 1
-    low, high = z_one[:, :2], z_one[:, 6:]
-    z_near = lax.ppermute(jnp.where(odd, low, high), "space", swap_in)
-    z_far = lax.ppermute(jnp.where(odd, high, low), "space", swap_far)
+    near_send, far_send = pl.pallas_call(
+        pack_kernel, out_shape=[shape((2, 2, 128, 128), BF16)] * 2, in_specs=[VMEM], out_specs=[VMEM] * 2, compiler_params=PARAMS,
+        cost_estimate=pl.CostEstimate(flops=0, bytes_accessed=1 << 19, transcendentals=0), name="pack",
+    )(z_one)
+    z_near = lax.ppermute(near_send, "space", swap_in)
+    z_far = lax.ppermute(far_send, "space", swap_far)
     inner_a, send, consts, kernel = pl.pallas_call(
         functools.partial(first_kernel, False, cells, strips),
         out_shape=[shape((2, 10, 128, 128), F32), shape((2, 10, 128, 128), BF16), shape((8, 128), F32), shape((3, 9 * 128, 128), BF16)],

time: 76.3 us -> 73.9 us (0.969)
  Pallas kernels: 19.8 us -> 17.6 us
    pallas_call x1, Pallas kernels: 7.19 us -> 6.11 us  [shards(): pl.pallas_call(functools.partial(second_kernel, cells, strips), out_shape...]
  transfers between devices with their start and end apart: 7 -> 7, of which waited for: 1 -> 1; matrix products, arithmetic and copies ran while one was open for 0% -> 0% of each run, Pallas kernels for 13% -> 12%
where the time goes in v5:
time: 73.9 us; the launch traced here: 73.6 us
  starting transfers between devices  28.3 us (38%)
  blocking collectives  18.7 us (25%)
  Pallas kernels  17.6 us (24%)
  waiting for transfers between devices  8.74 us (12%)
    all_to_all x1, blocking collectives, shards(): got = lax.all_to_all(pay, BOTH, 0, 0)  18.7 us
    all_to_all x1, starting transfers between devices, shards(): got = lax.all_to_all(pay, BOTH, 0, 0)  13.1 us
    all_to_all x1, waiting for transfers between devices, shards(): got = lax.all_to_all(pay, BOTH, 0, 0)  8.72 us
    pallas_call x1, Pallas kernels, shards(): pl.pallas_call(functools.partial(second_kernel, cells, strips), out_shape...  6.11 us
    pallas_call x1, Pallas kernels, shards(): pl.pallas_call(functools.partial(first_kernel, False, cells, strips), out...  5.02 us
    ppermute x1, starting transfers between devices, shards(): z_one = lax.ppermute(z_send, 'tm', later)  4.4 us
    pallas_call x1, Pallas kernels, shards(): pl.pallas_call(functools.partial(first_kernel, True, cells, strips), out_...  3.82 us
    ppermute x1, starting transfers between devices, shards(): far = lax.ppermute(far_send, 'space', swap_far)  3.02 us
  transfers between devices with their start and end apart: 7, of which 1 were waited for; matrix products, arithmetic and copies ran while one was open for 0% of the time, Pallas kernels for 12%

profile of v5, /device:TPU:1, one launch (start us, length us, event | category | flops | bytes accessed | tf_op | source)
XLA Modules:
  0.0 73.6 jit_solution(4072296866553768708)
XLA Ops:
  0.0 2.6 %stats.1 = (bf16[4,8,128,128]{3,2,1,0:T(8,128)(2,1)S(1)}, f32[256,128]{1,0:T(8,128)}, bf16[2,8,128,128]{3,2,1,0:T(8,128)(2,1)S(1)}, bf16[4,2,128,128]{3,2,1,0:T(...) custom-call(bf16[4,8,128,128]{3,2,1,0:T(8,128)(2,1)} %x_hbm.1, f32[128]{0:T(128)} %refs_0_.1, ...), custom_call_target="tpu_custom_call" | custom-call | flops 4194304 | bytes 1048576 | tf_op jit(solution)/shard_map/stats/pallas_call | solution.py:312
  2.6 4.4 %collective-permute-start.2 = (bf16[2,8,128,128]{3,2,1,0:T(8,128)(2,1)S(1)}, bf16[2,8,128,128]{3,2,1,0:T(8,128)(2,1)S(1)}, u32[]{:S(2)}, u32[]{:S(2)}) collective-permute-start(bf16[2,8,128,128]{3,2,1,0:T(8,128)(2,1)S(1)} %get-tuple-element.26), channel_id=1, source_target_pairs={{0,32},{32,64},{64,96},{96,128},{128,160},{160,192},{192,224},{1,3... | collective-permute-start | bytes 1572872 | tf_op jit(solution)/shard_map/ppermute | solution.py:322
  7.0 1.0 %collective-permute-start = (bf16[4,2,128,128]{3,2,1,0:T(8,128)(2,1)S(1)}, bf16[4,2,128,128]{3,2,1,0:T(8,128)(2,1)S(1)}, u32[]{:S(2)}, u32[]{:S(2)}) collective-permute-start(bf16[4,2,128,128]{3,2,1,0:T(8,128)(2,1)S(1)} %get-tuple-element.22), channel_id=1, source_target_pairs={{0,1},{1,0},{2,3},{3,2},{4,5},{5,4},{6,7},{7,6},{8,9},{9,8},{10,11... | collective-permute-start | bytes 786440 | tf_op jit(solution)/shard_map/ppermute | solution.py:323
  8.1 3.0 %collective-permute-start.1 = (bf16[4,2,128,128]{3,2,1,0:T(8,128)(2,1)S(1)}, bf16[4,2,128,128]{3,2,1,0:T(8,128)(2,1)S(1)}, u32[]{:S(2)}, u32[]{:S(2)}) collective-permute-start(bf16[4,2,128,128]{3,2,1,0:T(8,128)(2,1)S(1)} %get-tuple-element.23), channel_id=1, source_target_pairs={{1,2},{3,4},{5,6},{7,8},{9,10},{11,12},{13,14},{15,16},{17,18},{19... | collective-permute-start | bytes 786440 | tf_op jit(solution)/shard_map/ppermute | solution.py:324
  11.1 13.1 %all-to-all-start = ((f32[256,1,128]{2,1,0:T(1,128)}), f32[256,1,128]{2,1,0:T(1,128)S(1)}, u32[]{:S(2)}, u32[]{:S(2)}) async-start(f32[256,1,128]{2,1,0:T(1,128)} %bitcast.3), calls=%async_computation | async-start | bytes 262144 | tf_op jit(solution)/shard_map/all_to_all | solution.py:325
  24.2 0.0 collective-permute-done.2.z_ref.refs_6_
  24.2 2.2 %collective-permute-start.3 = (bf16[2,2,128,128]{3,2,1,0:T(8,128)(2,1)S(1)}, bf16[2,2,128,128]{3,2,1,0:T(8,128)(2,1)S(1)}, u32[]{:S(2)}, u32[]{:S(2)}) collective-permute-start(bf16[2,2,128,128]{3,2,1,0:T(8,128)(2,1)S(1)} %get-tuple-element.27), channel_id=1, source_target_pairs={{0,1},{1,0},{2,3},{3,2},{4,5},{5,4},{6,7},{7,6},{8,9},{9,8},{10,11... | collective-permute-start | bytes 393224 | tf_op jit(solution)/shard_map/ppermute | solution.py:330
  26.4 1.9 %collective-permute-start.4 = (bf16[2,2,128,128]{3,2,1,0:T(8,128)(2,1)S(1)}, bf16[2,2,128,128]{3,2,1,0:T(8,128)(2,1)S(1)}, u32[]{:S(2)}, u32[]{:S(2)}) collective-permute-start(bf16[2,2,128,128]{3,2,1,0:T(8,128)(2,1)S(1)} %get-tuple-element.28), channel_id=1, source_target_pairs={{1,2},{3,4},{5,6},{7,8},{9,10},{11,12},{13,14},{15,16},{17,18},{19... | collective-permute-start | bytes 393224 | tf_op jit(solution)/shard_map/ppermute | solution.py:331
  28.4 8.7 %all-to-all-done = f32[256,1,128]{2,1,0:T(1,128)S(1)} async-done(((f32[256,1,128]{2,1,0:T(1,128)}), f32[256,1,128]{2,1,0:T(1,128)S(1)}, u32[]{:S(2)}, u32[]{:S(2)}) %all-to-all-start) | async-done | bytes 131104 | tf_op jit(solution)/shard_map/all_to_all | solution.py:325
  37.1 0.0 collective-permute-done.refs_4_
  37.1 0.0 collective-permute-done.1.refs_5_
  37.1 5.0 %first_late.1 = (f32[2,10,128,128]{3,2,1,0:T(8,128)S(1)}, bf16[2,10,128,128]{3,2,1,0:T(8,128)(2,1)S(1)}, f32[8,128]{1,0:T(8,128)S(1)}, bf16[3,1152,128]{2,1,0:T(8,128)(2,1)S(1)}) custom-call(bf16[3,1152,128]{2,1,0:T(8,128)(2,1)} %bitcast.14, f32[256,128]{1,0:T(8,128)S(1)} %bitcast.10, f32[6,128]{1,0:T(8,128)S(1)} %get-tuple-element.20.refs_2_.small_ref, ...), custom_call_target="tpu_custom_call" | custom-call | flops 3019898880 | bytes 4194304 | tf_op jit(solution)/shard_map/first_late/pallas_call | solution.py:332
  42.1 2.6 %collective-permute-start.5 = (bf16[2,10,128,128]{3,2,1,0:T(8,128)(2,1)S(1)}, bf16[2,10,128,128]{3,2,1,0:T(8,128)(2,1)S(1)}, u32[]{:S(2)}, u32[]{:S(2)}) collective-permute-start(bf16[2,10,128,128]{3,2,1,0:T(8,128)(2,1)S(1)} %get-tuple-element.32), channel_id=1, source_target_pairs={{0,32},{32,64},{64,96},{96,128},{128,160},{160,192},{192,224},{1,3... | collective-permute-start | bytes 1966088 | tf_op jit(solution)/shard_map/ppermute | solution.py:338
  44.7 0.0 collective-permute-done.3.refs_7_
  44.8 0.0 collective-permute-done.4.refs_8_
  44.8 0.0 copy-start
  44.8 3.8 %first_early.1 = (f32[2,10,128,128]{3,2,1,0:T(8,128)S(1)}, f32[256,128]{1,0:T(8,128)S(1)}) custom-call(bf16[3,1152,128]{2,1,0:T(8,128)(2,1)S(1)} %get-tuple-element.24.refs_0_, f32[8,128]{1,0:T(8,128)S(1)} %get-tuple-element.25.refs_1_, f32[6,128]{1,0:T(8,128)S(1)} %get-tuple-element.20.refs_2_.small_ref, ...), custom_call_target="tpu_custom_call" | custom-call | flops 3019898880 | bytes 4194304 | tf_op jit(solution)/shard_map/first_early/pallas_call | solution.py:339
  48.6 18.7 %all_to_all.22 = f32[256,1,128]{2,1,0:T(1,128)S(1)} all-to-all(f32[256,1,128]{2,1,0:T(1,128)S(1)} %bitcast.12), channel_id=1, replica_groups=mesh['tm'=8,'space'=32] {'tm','space'}, dimensions={0} | all-to-all | bytes 262144 | tf_op jit(solution)/shard_map/all_to_all | solution.py:345
  67.3 0.0 collective-permute-done.5.z_ref
  67.3 0.0 copy-done
  67.3 6.1 %second.1 = f32[4,8,128,128]{3,2,1,0:T(8,128)} custom-call(bf16[3,1152,128]{2,1,0:T(8,128)(2,1)S(1)} %bitcast.13, f32[256,128]{1,0:T(8,128)S(1)} %bitcast.11, f32[6,128]{1,0:T(8,128)S(1)} %get-tuple-element.20.refs_2_.small_ref, bf16[4,8,128,128]{3,2,1,0:T(8,128)(2,1)S(1)} %get-tuple-element.21.refs_3_.feat_ref, ...), custom_call_target="tpu_custom_call" | custom-call | flops 4831838208 | bytes 4194304 | tf_op jit(solution)/shard_map/second/pallas_call | solution.py:346
  (1 shorter events, 0.0 us)
Async XLA Ops:
  2.6 21.5 %collective-permute-start.2 = (bf16[2,8,128,128]{3,2,1,0:T(8,128)(2,1)S(1)}, bf16[2,8,128,128]{3,2,1,0:T(8,128)(2,1)S(1)}, u32[]{:S(2)}, u32[]{:S(2)}) collective-permute-start(bf16[2,8,128,128]{3,2,1,0:T(8,128)(2,1)S(1)} %get-tuple-element.26), channel_id=1, source_target_pairs={{0,32},{32,64},{64,96},{96,128},{128,160},{160,192},{192,224},{1,3... | collective-permute-start | bytes 1572872 | tf_op jit(solution)/shard_map/ppermute | solution.py:322
  7.0 30.1 %collective-permute-start = (bf16[4,2,128,128]{3,2,1,0:T(8,128)(2,1)S(1)}, bf16[4,2,128,128]{3,2,1,0:T(8,128)(2,1)S(1)}, u32[]{:S(2)}, u32[]{:S(2)}) collective-permute-start(bf16[4,2,128,128]{3,2,1,0:T(8,128)(2,1)S(1)} %get-tuple-element.22), channel_id=1, source_target_pairs={{0,1},{1,0},{2,3},{3,2},{4,5},{5,4},{6,7},{7,6},{8,9},{9,8},{10,11... | collective-permute-start | bytes 786440 | tf_op jit(solution)/shard_map/ppermute | solution.py:323
  8.1 29.0 %collective-permute-start.1 = (bf16[4,2,128,128]{3,2,1,0:T(8,128)(2,1)S(1)}, bf16[4,2,128,128]{3,2,1,0:T(8,128)(2,1)S(1)}, u32[]{:S(2)}, u32[]{:S(2)}) collective-permute-start(bf16[4,2,128,128]{3,2,1,0:T(8,128)(2,1)S(1)} %get-tuple-element.23), channel_id=1, source_target_pairs={{1,2},{3,4},{5,6},{7,8},{9,10},{11,12},{13,14},{15,16},{17,18},{19... | collective-permute-start | bytes 786440 | tf_op jit(solution)/shard_map/ppermute | solution.py:324
  11.1 26.0 %all-to-all-start = ((f32[256,1,128]{2,1,0:T(1,128)}), f32[256,1,128]{2,1,0:T(1,128)S(1)}, u32[]{:S(2)}, u32[]{:S(2)}) async-start(f32[256,1,128]{2,1,0:T(1,128)} %bitcast.3), calls=%async_computation | async-start | bytes 262144 | tf_op jit(solution)/shard_map/all_to_all | solution.py:325
  24.2 20.5 %collective-permute-start.3 = (bf16[2,2,128,128]{3,2,1,0:T(8,128)(2,1)S(1)}, bf16[2,2,128,128]{3,2,1,0:T(8,128)(2,1)S(1)}, u32[]{:S(2)}, u32[]{:S(2)}) collective-permute-start(bf16[2,2,128,128]{3,2,1,0:T(8,128)(2,1)S(1)} %get-tuple-element.27), channel_id=1, source_target_pairs={{0,1},{1,0},{2,3},{3,2},{4,5},{5,4},{6,7},{7,6},{8,9},{9,8},{10,11... | collective-permute-start | bytes 393224 | tf_op jit(solution)/shard_map/ppermute | solution.py:330
  26.4 18.3 %collective-permute-start.4 = (bf16[2,2,128,128]{3,2,1,0:T(8,128)(2,1)S(1)}, bf16[2,2,128,128]{3,2,1,0:T(8,128)(2,1)S(1)}, u32[]{:S(2)}, u32[]{:S(2)}) collective-permute-start(bf16[2,2,128,128]{3,2,1,0:T(8,128)(2,1)S(1)} %get-tuple-element.28), channel_id=1, source_target_pairs={{1,2},{3,4},{5,6},{7,8},{9,10},{11,12},{13,14},{15,16},{17,18},{19... | collective-permute-start | bytes 393224 | tf_op jit(solution)/shard_map/ppermute | solution.py:331
  42.1 25.2 %collective-permute-start.5 = (bf16[2,10,128,128]{3,2,1,0:T(8,128)(2,1)S(1)}, bf16[2,10,128,128]{3,2,1,0:T(8,128)(2,1)S(1)}, u32[]{:S(2)}, u32[]{:S(2)}) collective-permute-start(bf16[2,10,128,128]{3,2,1,0:T(8,128)(2,1)S(1)} %get-tuple-element.32), channel_id=1, source_target_pairs={{0,32},{32,64},{64,96},{96,128},{128,160},{160,192},{192,224},{1,3... | collective-permute-start | bytes 1966088 | tf_op jit(solution)/shard_map/ppermute | solution.py:338
  44.8 22.5 %copy-start = (bf16[3,3,3,128,128]{4,3,2,1,0:T(8,128)(2,1)S(1)}, bf16[3,3,3,128,128]{4,3,2,1,0:T(8,128)(2,1)}, u32[]{:S(2)}) copy-start(bf16[3,3,3,128,128]{4,3,2,1,0:T(8,128)(2,1)} %param.16) | copy-start | bytes 2654212

commit v6 on v5

--- a/solution.py
+++ b/solution.py
@@ -79,13 +79,16 @@
     got = got_ref[...]
     devices = got.shape[0]
     place = lane_of(got.shape) & 3
-    means = jnp.where(place == 0, got, 0.0)
-    mean = group_sum(column_sum(means)) / devices
-    spread = group_sum(column_sum(jnp.where(place == 1, got, 0.0)))
-    off = jnp.where(place == 0, got - mean[:1], 0.0)
-    between = group_sum(column_sum(off * off))
-    var = (spread + between * cells) / (cells * devices)
-    return mean, lax.rsqrt(var + EPS)
+    off = got - got[:1]
+    sums = jnp.where(place == 0, off, jnp.where(place == 1, got, 0.0))
+    sums = column_sum(sums)
+    squares = group_sum(column_sum(jnp.where(place == 0, off * off, 0.0)))
+    here = lane_of(sums.shape) & 3
+    shift = group_sum(jnp.where(here == 0, sums, 0.0)) / devices
+    spread = group_sum(jnp.where(here == 1, sums, 0.0))
+    first = group_sum(jnp.where(here == 0, jnp.broadcast_to(got[:1], sums.shape), 0.0))
+    var = spread / (cells * devices) + (squares / devices - shift * shift)
+    return first + shift, lax.rsqrt(var + EPS)
 
 
 def put_act(off, slope, half_shift, keep, out, f, r):
@@ -198,24 +201,25 @@
     def carried(ref, z, f):
         return lambda r: jnp.where(start, ref[0, r], z[f, r])
 
-    if early:
-        build_taps(kernel, mid, side)
-        for r in range(12):
-            for f in range(2):
-                act(carried(x_ref, z_ref, f), carried(in_ref, z_in_ref, f), carried(far_ref, z_far_ref, f), f, r)
-                act(of(x_ref, f), of(in_ref, f), of(far_ref, f), 2 + f, r)
-    else:
-        for f in range(4):
-            if f == 2:
-                fetch.wait()
-                build_taps(kernel, mid, side)
-            for r in range(12):
-                act(of(x_ref, f), of(in_ref, f), of(far_ref, f), f, r)
-
     def put(o, r, value):
         inner_ref[o, r] = value + bias
 
-    conv_pair(acts, mid, side, 0, 0, 10, put)
+    done = 0
+    for at, rows in (((0, 6), (6, 4)) if early else ((0, 5), (5, 5))):
+        for r in range(done, at + rows + 2):
+            for f in range(2):
+                if early:
+                    act(carried(x_ref, z_ref, f), carried(in_ref, z_in_ref, f), carried(far_ref, z_far_ref, f), f, r)
+                    act(of(x_ref, f), of(in_ref, f), of(far_ref, f), 2 + f, r)
+                else:
+                    act(of(x_ref, 2 * f), of(in_ref, 2 * f), of(far_ref, 2 * f), 2 * f, r)
+                    act(of(x_ref, 2 * f + 1), of(in_ref, 2 * f + 1), of(far_ref, 2 * f + 1), 2 * f + 1, r)
+        done = at + rows + 2
+        if at == 0:
+            if not early:
+                fetch.wait()
+            build_taps(kernel, mid, side)
+        conv_pair(acts, mid, side, 0, at, rows, put)
     own = lambda i: inner_ref[i // 8, 1 + i % 8]
     if early:
         m, spread = joined(late, spread, cells / 2, *shifted_sums(own, 16, late), cells / 2)
@@ -255,15 +259,17 @@
             copies[-1].start()
 
     build_taps(kernel_ref, mid, side)
-    for r in range(10):
-        for f in range(4):
-            act((b_ref if f < 2 else a_ref)[f % 2, r] - mean, 2 + f, r)
-    conv(1, 0, 8)
-    for r in range(10):
-        for f in range(2):
-            act(jnp.where(start, b_ref[0, r] - mean, z_ref[f, r].astype(F32) - base), f, r)
-    for at in (0, 4):
-        conv(0, at, 4)
+    for pair, chunks in ((1, ((0, 4), (4, 4))), (0, ((0, 5), (5, 3)))):
+        done = 0
+        for at, rows in chunks:
+            for r in range(done, at + rows + 2):
+                for f in range(4 if pair else 2):
+                    if pair:
+                        act((b_ref if f < 2 else a_ref)[f % 2, r] - mean, 2 + f, r)
+                    else:
+                        act(jnp.where(start, b_ref[0, r] - mean, z_ref[f, r].astype(F32) - base), f, r)
+            done = at + rows + 2
+            conv(pair, at, rows)
     for copy in copies:
         copy.wait()
 
@@ -347,7 +353,7 @@
         functools.partial(second_kernel, cells, strips),
         out_shape=shape((4, 8, 128, 128), F32),
         in_specs=[VMEM] * 7, out_specs=HBM,
-        scratch_shapes=scratch(6, 10) + [pltpu.VMEM((4, 8, 128, 128), F32), DMA((6,))],
+        scratch_shapes=scratch(6, 10) + [pltpu.VMEM((4, 8, 128, 128), F32), DMA((8,))],
         compiler_params=PARAMS, cost_estimate=cost(2, 8), name="second",
     )(taps_two, got, small, x, inner_b, inner_a, z_two)
 

time: 73.9 us -> 73 us (0.988)
  Pallas kernels: 17.6 us -> 16.6 us
  transfers between devices with their start and end apart: 7 -> 7, of which waited for: 1 -> 1; matrix products, arithmetic and copies ran while one was open for 0% -> 0% of each run, Pallas kernels for 12% -> 11%
where the time goes in v6:
time: 73 us; the launch traced here: 72.7 us
  starting transfers between devices  28.3 us (39%)
  blocking collectives  18.7 us (26%)
  Pallas kernels  16.6 us (23%)
  waiting for transfers between devices  8.74 us (12%)
    all_to_all x1, blocking collectives, shards(): got = lax.all_to_all(pay, BOTH, 0, 0)  18.7 us
    all_to_all x1, starting transfers between devices, shards(): got = lax.all_to_all(pay, BOTH, 0, 0)  13.1 us
    all_to_all x1, waiting for transfers between devices, shards(): got = lax.all_to_all(pay, BOTH, 0, 0)  8.72 us
    pallas_call x1, Pallas kernels, shards(): pl.pallas_call(functools.partial(second_kernel, cells, strips), out_shape...  5.8 us
    pallas_call x1, Pallas kernels, shards(): pl.pallas_call(functools.partial(first_kernel, False, cells, strips), out...  4.83 us
    ppermute x1, starting transfers between devices, shards(): z_one = lax.ppermute(z_send, 'tm', later)  4.4 us
    pallas_call x1, Pallas kernels, shards(): pl.pallas_call(functools.partial(first_kernel, True, cells, strips), out_...  3.38 us
    ppermute x1, starting transfers between devices, shards(): far = lax.ppermute(far_send, 'space', swap_far)  3.02 us
  transfers between devices with their start and end apart: 7, of which 1 were waited for; matrix products, arithmetic and copies ran while one was open for 0% of the time, Pallas kernels for 11%

profile of v6, /device:TPU:1, one launch (start us, length us, event | category | flops | bytes accessed | tf_op | source)
XLA Modules:
  0.0 72.7 jit_solution(4728647536465420563)
XLA Ops:
  0.0 2.6 %stats.1 = (bf16[4,8,128,128]{3,2,1,0:T(8,128)(2,1)S(1)}, f32[256,128]{1,0:T(8,128)}, bf16[2,8,128,128]{3,2,1,0:T(8,128)(2,1)S(1)}, bf16[4,2,128,128]{3,2,1,0:T(...) custom-call(bf16[4,8,128,128]{3,2,1,0:T(8,128)(2,1)} %x_hbm.1, f32[128]{0:T(128)} %refs_0_.1, ...), custom_call_target="tpu_custom_call" | custom-call | flops 4194304 | bytes 1048576 | tf_op jit(solution)/shard_map/stats/pallas_call | solution.py:318
  2.6 4.4 %collective-permute-start.2 = (bf16[2,8,128,128]{3,2,1,0:T(8,128)(2,1)S(1)}, bf16[2,8,128,128]{3,2,1,0:T(8,128)(2,1)S(1)}, u32[]{:S(2)}, u32[]{:S(2)}) collective-permute-start(bf16[2,8,128,128]{3,2,1,0:T(8,128)(2,1)S(1)} %get-tuple-element.26), channel_id=1, source_target_pairs={{0,32},{32,64},{64,96},{96,128},{128,160},{160,192},{192,224},{1,3... | collective-permute-start | bytes 1572872 | tf_op jit(solution)/shard_map/ppermute | solution.py:328
  7.0 1.0 %collective-permute-start = (bf16[4,2,128,128]{3,2,1,0:T(8,128)(2,1)S(1)}, bf16[4,2,128,128]{3,2,1,0:T(8,128)(2,1)S(1)}, u32[]{:S(2)}, u32[]{:S(2)}) collective-permute-start(bf16[4,2,128,128]{3,2,1,0:T(8,128)(2,1)S(1)} %get-tuple-element.22), channel_id=1, source_target_pairs={{0,1},{1,0},{2,3},{3,2},{4,5},{5,4},{6,7},{7,6},{8,9},{9,8},{10,11... | collective-permute-start | bytes 786440 | tf_op jit(solution)/shard_map/ppermute | solution.py:329
  8.1 3.0 %collective-permute-start.1 = (bf16[4,2,128,128]{3,2,1,0:T(8,128)(2,1)S(1)}, bf16[4,2,128,128]{3,2,1,0:T(8,128)(2,1)S(1)}, u32[]{:S(2)}, u32[]{:S(2)}) collective-permute-start(bf16[4,2,128,128]{3,2,1,0:T(8,128)(2,1)S(1)} %get-tuple-element.23), channel_id=1, source_target_pairs={{1,2},{3,4},{5,6},{7,8},{9,10},{11,12},{13,14},{15,16},{17,18},{19... | collective-permute-start | bytes 786440 | tf_op jit(solution)/shard_map/ppermute | solution.py:330
  11.1 13.1 %all-to-all-start = ((f32[256,1,128]{2,1,0:T(1,128)}), f32[256,1,128]{2,1,0:T(1,128)S(1)}, u32[]{:S(2)}, u32[]{:S(2)}) async-start(f32[256,1,128]{2,1,0:T(1,128)} %bitcast.3), calls=%async_computation | async-start | bytes 262144 | tf_op jit(solution)/shard_map/all_to_all | solution.py:331
  24.2 0.0 collective-permute-done.2.z_ref.refs_6_
  24.2 2.2 %collective-permute-start.3 = (bf16[2,2,128,128]{3,2,1,0:T(8,128)(2,1)S(1)}, bf16[2,2,128,128]{3,2,1,0:T(8,128)(2,1)S(1)}, u32[]{:S(2)}, u32[]{:S(2)}) collective-permute-start(bf16[2,2,128,128]{3,2,1,0:T(8,128)(2,1)S(1)} %get-tuple-element.27), channel_id=1, source_target_pairs={{0,1},{1,0},{2,3},{3,2},{4,5},{5,4},{6,7},{7,6},{8,9},{9,8},{10,11... | collective-permute-start | bytes 393224 | tf_op jit(solution)/shard_map/ppermute | solution.py:336
  26.4 1.9 %collective-permute-start.4 = (bf16[2,2,128,128]{3,2,1,0:T(8,128)(2,1)S(1)}, bf16[2,2,128,128]{3,2,1,0:T(8,128)(2,1)S(1)}, u32[]{:S(2)}, u32[]{:S(2)}) collective-permute-start(bf16[2,2,128,128]{3,2,1,0:T(8,128)(2,1)S(1)} %get-tuple-element.28), channel_id=1, source_target_pairs={{1,2},{3,4},{5,6},{7,8},{9,10},{11,12},{13,14},{15,16},{17,18},{19... | collective-permute-start | bytes 393224 | tf_op jit(solution)/shard_map/ppermute | solution.py:337
  28.4 8.7 %all-to-all-done = f32[256,1,128]{2,1,0:T(1,128)S(1)} async-done(((f32[256,1,128]{2,1,0:T(1,128)}), f32[256,1,128]{2,1,0:T(1,128)S(1)}, u32[]{:S(2)}, u32[]{:S(2)}) %all-to-all-start) | async-done | bytes 131104 | tf_op jit(solution)/shard_map/all_to_all | solution.py:331
  37.1 0.0 collective-permute-done.refs_4_
  37.1 0.0 collective-permute-done.1.refs_5_
  37.1 4.8 %first_late.1 = (f32[2,10,128,128]{3,2,1,0:T(8,128)S(1)}, bf16[2,10,128,128]{3,2,1,0:T(8,128)(2,1)S(1)}, f32[8,128]{1,0:T(8,128)S(1)}, bf16[3,1152,128]{2,1,0:T(8,128)(2,1)S(1)}) custom-call(bf16[3,1152,128]{2,1,0:T(8,128)(2,1)} %bitcast.14, f32[256,128]{1,0:T(8,128)S(1)} %bitcast.10, f32[6,128]{1,0:T(8,128)S(1)} %get-tuple-element.20.refs_2_.small_ref, ...), custom_call_target="tpu_custom_call" | custom-call | flops 3019898880 | bytes 4194304 | tf_op jit(solution)/shard_map/first_late/pallas_call | solution.py:338
  41.9 2.6 %collective-permute-start.5 = (bf16[2,10,128,128]{3,2,1,0:T(8,128)(2,1)S(1)}, bf16[2,10,128,128]{3,2,1,0:T(8,128)(2,1)S(1)}, u32[]{:S(2)}, u32[]{:S(2)}) collective-permute-start(bf16[2,10,128,128]{3,2,1,0:T(8,128)(2,1)S(1)} %get-tuple-element.32), channel_id=1, source_target_pairs={{0,32},{32,64},{64,96},{96,128},{128,160},{160,192},{192,224},{1,3... | collective-permute-start | bytes 1966088 | tf_op jit(solution)/shard_map/ppermute | solution.py:344
  44.5 0.0 collective-permute-done.3.refs_7_
  44.6 0.0 collective-permute-done.4.refs_8_
  44.6 0.0 copy-start
  44.6 3.4 %first_early.1 = (f32[2,10,128,128]{3,2,1,0:T(8,128)S(1)}, f32[256,128]{1,0:T(8,128)S(1)}) custom-call(bf16[3,1152,128]{2,1,0:T(8,128)(2,1)S(1)} %get-tuple-element.24.refs_0_, f32[8,128]{1,0:T(8,128)S(1)} %get-tuple-element.25.refs_1_, f32[6,128]{1,0:T(8,128)S(1)} %get-tuple-element.20.refs_2_.small_ref, ...), custom_call_target="tpu_custom_call" | custom-call | flops 3019898880 | bytes 4194304 | tf_op jit(solution)/shard_map/first_early/pallas_call | solution.py:345
  48.0 18.7 %all_to_all.22 = f32[256,1,128]{2,1,0:T(1,128)S(1)} all-to-all(f32[256,1,128]{2,1,0:T(1,128)S(1)} %bitcast.12), channel_id=1, replica_groups=mesh['tm'=8,'space'=32] {'tm','space'}, dimensions={0} | all-to-all | bytes 262144 | tf_op jit(solution)/shard_map/all_to_all | solution.py:351
  66.7 0.0 collective-permute-done.5.z_ref
  66.7 0.0 copy-done
  66.7 5.8 %second.1 = f32[4,8,128,128]{3,2,1,0:T(8,128)} custom-call(bf16[3,1152,128]{2,1,0:T(8,128)(2,1)S(1)} %bitcast.13, f32[256,128]{1,0:T(8,128)S(1)} %bitcast.11, f32[6,128]{1,0:T(8,128)S(1)} %get-tuple-element.20.refs_2_.small_ref, bf16[4,8,128,128]{3,2,1,0:T(8,128)(2,1)S(1)} %get-tuple-element.21.refs_3_.feat_ref, ...), custom_call_target="tpu_custom_call" | custom-call | flops 4831838208 | bytes 4194304 | tf_op jit(solution)/shard_map/second/pallas_call | solution.py:352
  (1 shorter events, 0.0 us)
Async XLA Ops:
  2.6 21.5 %collective-permute-start.2 = (bf16[2,8,128,128]{3,2,1,0:T(8,128)(2,1)S(1)}, bf16[2,8,128,128]{3,2,1,0:T(8,128)(2,1)S(1)}, u32[]{:S(2)}, u32[]{:S(2)}) collective-permute-start(bf16[2,8,128,128]{3,2,1,0:T(8,128)(2,1)S(1)} %get-tuple-element.26), channel_id=1, source_target_pairs={{0,32},{32,64},{64,96},{96,128},{128,160},{160,192},{192,224},{1,3... | collective-permute-start | bytes 1572872 | tf_op jit(solution)/shard_map/ppermute | solution.py:328
  7.0 30.1 %collective-permute-start = (bf16[4,2,128,128]{3,2,1,0:T(8,128)(2,1)S(1)}, bf16[4,2,128,128]{3,2,1,0:T(8,128)(2,1)S(1)}, u32[]{:S(2)}, u32[]{:S(2)}) collective-permute-start(bf16[4,2,128,128]{3,2,1,0:T(8,128)(2,1)S(1)} %get-tuple-element.22), channel_id=1, source_target_pairs={{0,1},{1,0},{2,3},{3,2},{4,5},{5,4},{6,7},{7,6},{8,9},{9,8},{10,11... | collective-permute-start | bytes 786440 | tf_op jit(solution)/shard_map/ppermute | solution.py:329
  8.1 29.0 %collective-permute-start.1 = (bf16[4,2,128,128]{3,2,1,0:T(8,128)(2,1)S(1)}, bf16[4,2,128,128]{3,2,1,0:T(8,128)(2,1)S(1)}, u32[]{:S(2)}, u32[]{:S(2)}) collective-permute-start(bf16[4,2,128,128]{3,2,1,0:T(8,128)(2,1)S(1)} %get-tuple-element.23), channel_id=1, source_target_pairs={{1,2},{3,4},{5,6},{7,8},{9,10},{11,12},{13,14},{15,16},{17,18},{19... | collective-permute-start | bytes 786440 | tf_op jit(solution)/shard_map/ppermute | solution.py:330
  11.1 26.0 %all-to-all-start = ((f32[256,1,128]{2,1,0:T(1,128)}), f32[256,1,128]{2,1,0:T(1,128)S(1)}, u32[]{:S(2)}, u32[]{:S(2)}) async-start(f32[256,1,128]{2,1,0:T(1,128)} %bitcast.3), calls=%async_computation | async-start | bytes 262144 | tf_op jit(solution)/shard_map/all_to_all | solution.py:331
  24.2 20.3 %collective-permute-start.3 = (bf16[2,2,128,128]{3,2,1,0:T(8,128)(2,1)S(1)}, bf16[2,2,128,128]{3,2,1,0:T(8,128)(2,1)S(1)}, u32[]{:S(2)}, u32[]{:S(2)}) collective-permute-start(bf16[2,2,128,128]{3,2,1,0:T(8,128)(2,1)S(1)} %get-tuple-element.27), channel_id=1, source_target_pairs={{0,1},{1,0},{2,3},{3,2},{4,5},{5,4},{6,7},{7,6},{8,9},{9,8},{10,11... | collective-permute-start | bytes 393224 | tf_op jit(solution)/shard_map/ppermute | solution.py:336
  26.4 18.1 %collective-permute-start.4 = (bf16[2,2,128,128]{3,2,1,0:T(8,128)(2,1)S(1)}, bf16[2,2,128,128]{3,2,1,0:T(8,128)(2,1)S(1)}, u32[]{:S(2)}, u32[]{:S(2)}) collective-permute-start(bf16[2,2,128,128]{3,2,1,0:T(8,128)(2,1)S(1)} %get-tuple-element.28), channel_id=1, source_target_pairs={{1,2},{3,4},{5,6},{7,8},{9,10},{11,12},{13,14},{15,16},{17,18},{19... | collective-permute-start | bytes 393224 | tf_op jit(solution)/shard_map/ppermute | solution.py:337
  41.9 24.8 %collective-permute-start.5 = (bf16[2,10,128,128]{3,2,1,0:T(8,128)(2,1)S(1)}, bf16[2,10,128,128]{3,2,1,0:T(8,128)(2,1)S(1)}, u32[]{:S(2)}, u32[]{:S(2)}) collective-permute-start(bf16[2,10,128,128]{3,2,1,0:T(8,128)(2,1)S(1)} %get-tuple-element.32), channel_id=1, source_target_pairs={{0,32},{32,64},{64,96},{96,128},{128,160},{160,192},{192,224},{1,3... | collective-permute-start | bytes 1966088 | tf_op jit(solution)/shard_map/ppermute | solution.py:344
  44.6 22.1 %copy-start = (bf16[3,3,3,128,128]{4,3,2,1,0:T(8,128)(2,1)S(1)}, bf16[3,3,3,128,128]{4,3,2,1,0:T(8,128)(2,1)}, u32[]{:S(2)}) copy-start(bf16[3,3,3,128,128]{4,3,2,1,0:T(8,128)(2,1)} %param.16) | copy-start | bytes 2654212

commit v7 on v6

--- a/solution.py
+++ b/solution.py
@@ -309,8 +309,8 @@
     devices = slabs * strips
     cells = float(4 * 8 * 128 * MEMBERS)
     swap_in = [(i, i ^ 1) for i in range(strips)]
-    swap_far = [(i, i + 1) for i in range(1, strips - 1, 2)] + [(i + 1, i) for i in range(1, strips - 1, 2)]
-    later = [(i, i + 1) for i in range(slabs - 1)]
+    swap_far = [(i, (i + 1) % strips) for i in range(1, strips, 2)] + [((i + 1) % strips, i) for i in range(1, strips, 2)]
+    later = [(i, (i + 1) % slabs) for i in range(slabs)]
     taps_one = kernel_one.reshape(3, 9 * 128, 128)
     taps_two = kernel_two.reshape(3, 9 * 128, 128)
 

time: 73 us -> 67.4 us (0.923)
  starting transfers between devices: 28.3 us -> 20.9 us
  waiting for transfers between devices: 8.74 us -> 10.4 us
    ppermute x1, starting transfers between devices: 3.02 us -> 1.1 us  [shards(): far = lax.ppermute(far_send, 'space', swap_far)]
    ppermute x1, starting transfers between devices: 2.62 us -> 0.76 us  [shards(): z_two = lax.ppermute(send, 'tm', later)]
    ppermute x1, starting transfers between devices: 4.4 us -> 2.54 us  [shards(): z_one = lax.ppermute(z_send, 'tm', later)]
    all_to_all x1, waiting for transfers between devices: 8.72 us -> 9.93 us  [shards(): got = lax.all_to_all(pay, BOTH, 0, 0)]
    ppermute x1, starting transfers between devices: 1.91 us -> 0.7 us  [shards(): z_far = lax.ppermute(far_send, 'space', swap_far)]
  transfers between devices with their start and end apart: 7 -> 7, of which waited for: 1 -> 2; matrix products, arithmetic and copies ran while one was open for 0% -> 0% of each run, Pallas kernels for 11% -> 12%
where the time goes in v7:
time: 67.4 us; the launch traced here: 67.2 us
  starting transfers between devices  20.9 us (31%)
  blocking collectives  19.1 us (28%)
  Pallas kernels  16.6 us (25%)
  waiting for transfers between devices  10.4 us (15%)
    all_to_all x1, blocking collectives, shards(): got = lax.all_to_all(pay, BOTH, 0, 0)  19.1 us
    all_to_all x1, starting transfers between devices, shards(): got = lax.all_to_all(pay, BOTH, 0, 0)  13.1 us
    all_to_all x1, waiting for transfers between devices, shards(): got = lax.all_to_all(pay, BOTH, 0, 0)  9.93 us
    pallas_call x1, Pallas kernels, shards(): pl.pallas_call(functools.partial(second_kernel, cells, strips), out_shape...  5.8 us
    pallas_call x1, Pallas kernels, shards(): pl.pallas_call(functools.partial(first_kernel, False, cells, strips), out...  4.83 us
    pallas_call x1, Pallas kernels, shards(): pl.pallas_call(functools.partial(first_kernel, True, cells, strips), out_...  3.38 us
    pallas_call x1, Pallas kernels, shards(): pl.pallas_call(stats_kernel, out_shape=[shape((4, 8, 128, 128), BF16), sh...  2.61 us
    ppermute x1, starting transfers between devices, shards(): z_one = lax.ppermute(z_send, 'tm', later)  2.54 us
  transfers between devices with their start and end apart: 7, of which 2 were waited for; matrix products, arithmetic and copies ran while one was open for 0% of the time, Pallas kernels for 12%

profile of v7, /device:TPU:1, one launch (start us, length us, event | category | flops | bytes accessed | tf_op | source)
XLA Modules:
  0.0 67.2 jit_solution(10147240518471983155)
XLA Ops:
  0.0 2.6 %stats.1 = (bf16[4,8,128,128]{3,2,1,0:T(8,128)(2,1)S(1)}, f32[256,128]{1,0:T(8,128)}, bf16[2,8,128,128]{3,2,1,0:T(8,128)(2,1)S(1)}, bf16[4,2,128,128]{3,2,1,0:T(...) custom-call(bf16[4,8,128,128]{3,2,1,0:T(8,128)(2,1)} %x_hbm.1, f32[128]{0:T(128)} %refs_0_.1, ...), custom_call_target="tpu_custom_call" | custom-call | flops 4194304 | bytes 1048576 | tf_op jit(solution)/shard_map/stats/pallas_call | solution.py:318
  2.6 2.5 %collective-permute-start.2 = (bf16[2,8,128,128]{3,2,1,0:T(8,128)(2,1)S(1)}, bf16[2,8,128,128]{3,2,1,0:T(8,128)(2,1)S(1)}, u32[]{:S(2)}, u32[]{:S(2)}) collective-permute-start(bf16[2,8,128,128]{3,2,1,0:T(8,128)(2,1)S(1)} %get-tuple-element.26), channel_id=1, source_target_pairs={{0,32},{32,64},{64,96},{96,128},{128,160},{160,192},{192,224},{224... | collective-permute-start | bytes 1572872 | tf_op jit(solution)/shard_map/ppermute | solution.py:328
  5.2 1.0 %collective-permute-start = (bf16[4,2,128,128]{3,2,1,0:T(8,128)(2,1)S(1)}, bf16[4,2,128,128]{3,2,1,0:T(8,128)(2,1)S(1)}, u32[]{:S(2)}, u32[]{:S(2)}) collective-permute-start(bf16[4,2,128,128]{3,2,1,0:T(8,128)(2,1)S(1)} %get-tuple-element.22), channel_id=1, source_target_pairs={{0,1},{1,0},{2,3},{3,2},{4,5},{5,4},{6,7},{7,6},{8,9},{9,8},{10,11... | collective-permute-start | bytes 786440 | tf_op jit(solution)/shard_map/ppermute | solution.py:329
  6.1 1.1 %collective-permute-start.1 = (bf16[4,2,128,128]{3,2,1,0:T(8,128)(2,1)S(1)}, bf16[4,2,128,128]{3,2,1,0:T(8,128)(2,1)S(1)}, u32[]{:S(2)}, u32[]{:S(2)}) collective-permute-start(bf16[4,2,128,128]{3,2,1,0:T(8,128)(2,1)S(1)} %get-tuple-element.23), channel_id=1, source_target_pairs={{1,2},{3,4},{5,6},{7,8},{9,10},{11,12},{13,14},{15,16},{17,18},{19... | collective-permute-start | bytes 786440 | tf_op jit(solution)/shard_map/ppermute | solution.py:330
  7.2 13.1 %all-to-all-start = ((f32[256,1,128]{2,1,0:T(1,128)}), f32[256,1,128]{2,1,0:T(1,128)S(1)}, u32[]{:S(2)}, u32[]{:S(2)}) async-start(f32[256,1,128]{2,1,0:T(1,128)} %bitcast.3), calls=%async_computation | async-start | bytes 262144 | tf_op jit(solution)/shard_map/all_to_all | solution.py:331
  20.3 0.4 collective-permute-done.2.z_ref.refs_6_
  20.8 1.8 %collective-permute-start.3 = (bf16[2,2,128,128]{3,2,1,0:T(8,128)(2,1)S(1)}, bf16[2,2,128,128]{3,2,1,0:T(8,128)(2,1)S(1)}, u32[]{:S(2)}, u32[]{:S(2)}) collective-permute-start(bf16[2,2,128,128]{3,2,1,0:T(8,128)(2,1)S(1)} %get-tuple-element.27), channel_id=1, source_target_pairs={{0,1},{1,0},{2,3},{3,2},{4,5},{5,4},{6,7},{7,6},{8,9},{9,8},{10,11... | collective-permute-start | bytes 393224 | tf_op jit(solution)/shard_map/ppermute | solution.py:336
  22.6 0.7 %collective-permute-start.4 = (bf16[2,2,128,128]{3,2,1,0:T(8,128)(2,1)S(1)}, bf16[2,2,128,128]{3,2,1,0:T(8,128)(2,1)S(1)}, u32[]{:S(2)}, u32[]{:S(2)}) collective-permute-start(bf16[2,2,128,128]{3,2,1,0:T(8,128)(2,1)S(1)} %get-tuple-element.28), channel_id=1, source_target_pairs={{1,2},{3,4},{5,6},{7,8},{9,10},{11,12},{13,14},{15,16},{17,18},{19... | collective-permute-start | bytes 393224 | tf_op jit(solution)/shard_map/ppermute | solution.py:337
  23.3 9.9 %all-to-all-done = f32[256,1,128]{2,1,0:T(1,128)S(1)} async-done(((f32[256,1,128]{2,1,0:T(1,128)}), f32[256,1,128]{2,1,0:T(1,128)S(1)}, u32[]{:S(2)}, u32[]{:S(2)}) %all-to-all-start) | async-done | bytes 131104 | tf_op jit(solution)/shard_map/all_to_all | solution.py:331
  33.2 0.0 collective-permute-done.refs_4_
  33.2 0.0 collective-permute-done.1.refs_5_
  33.2 4.8 %first_late.1 = (f32[2,10,128,128]{3,2,1,0:T(8,128)S(1)}, bf16[2,10,128,128]{3,2,1,0:T(8,128)(2,1)S(1)}, f32[8,128]{1,0:T(8,128)S(1)}, bf16[3,1152,128]{2,1,0:T(8,128)(2,1)S(1)}) custom-call(bf16[3,1152,128]{2,1,0:T(8,128)(2,1)} %bitcast.14, f32[256,128]{1,0:T(8,128)S(1)} %bitcast.10, f32[6,128]{1,0:T(8,128)S(1)} %get-tuple-element.20.refs_2_.small_ref, ...), custom_call_target="tpu_custom_call" | custom-call | flops 3019898880 | bytes 4194304 | tf_op jit(solution)/shard_map/first_late/pallas_call | solution.py:338
  38.1 0.8 %collective-permute-start.5 = (bf16[2,10,128,128]{3,2,1,0:T(8,128)(2,1)S(1)}, bf16[2,10,128,128]{3,2,1,0:T(8,128)(2,1)S(1)}, u32[]{:S(2)}, u32[]{:S(2)}) collective-permute-start(bf16[2,10,128,128]{3,2,1,0:T(8,128)(2,1)S(1)} %get-tuple-element.32), channel_id=1, source_target_pairs={{0,32},{32,64},{64,96},{96,128},{128,160},{160,192},{192,224},{224... | collective-permute-start | bytes 1966088 | tf_op jit(solution)/shard_map/ppermute | solution.py:344
  38.8 0.0 collective-permute-done.3.refs_7_
  38.8 0.0 collective-permute-done.4.refs_8_
  38.8 0.0 copy-start
  38.8 3.4 %first_early.1 = (f32[2,10,128,128]{3,2,1,0:T(8,128)S(1)}, f32[256,128]{1,0:T(8,128)S(1)}) custom-call(bf16[3,1152,128]{2,1,0:T(8,128)(2,1)S(1)} %get-tuple-element.24.refs_0_, f32[8,128]{1,0:T(8,128)S(1)} %get-tuple-element.25.refs_1_, f32[6,128]{1,0:T(8,128)S(1)} %get-tuple-element.20.refs_2_.small_ref, ...), custom_call_target="tpu_custom_call" | custom-call | flops 3019898880 | bytes 4194304 | tf_op jit(solution)/shard_map/first_early/pallas_call | solution.py:345
  42.2 19.1 %all_to_all.22 = f32[256,1,128]{2,1,0:T(1,128)S(1)} all-to-all(f32[256,1,128]{2,1,0:T(1,128)S(1)} %bitcast.12), channel_id=1, replica_groups=mesh['tm'=8,'space'=32] {'tm','space'}, dimensions={0} | all-to-all | bytes 262144 | tf_op jit(solution)/shard_map/all_to_all | solution.py:351
  61.3 0.0 collective-permute-done.5.z_ref
  61.3 0.0 copy-done
  61.3 5.8 %second.1 = f32[4,8,128,128]{3,2,1,0:T(8,128)} custom-call(bf16[3,1152,128]{2,1,0:T(8,128)(2,1)S(1)} %bitcast.13, f32[256,128]{1,0:T(8,128)S(1)} %bitcast.11, f32[6,128]{1,0:T(8,128)S(1)} %get-tuple-element.20.refs_2_.small_ref, bf16[4,8,128,128]{3,2,1,0:T(8,128)(2,1)S(1)} %get-tuple-element.21.refs_3_.feat_ref, ...), custom_call_target="tpu_custom_call" | custom-call | flops 4831838208 | bytes 4194304 | tf_op jit(solution)/shard_map/second/pallas_call | solution.py:352
  (1 shorter events, 0.0 us)
Async XLA Ops:
  2.6 18.1 %collective-permute-start.2 = (bf16[2,8,128,128]{3,2,1,0:T(8,128)(2,1)S(1)}, bf16[2,8,128,128]{3,2,1,0:T(8,128)(2,1)S(1)}, u32[]{:S(2)}, u32[]{:S(2)}) collective-permute-start(bf16[2,8,128,128]{3,2,1,0:T(8,128)(2,1)S(1)} %get-tuple-element.26), channel_id=1, source_target_pairs={{0,32},{32,64},{64,96},{96,128},{128,160},{160,192},{192,224},{224... | collective-permute-start | bytes 1572872 | tf_op jit(solution)/shard_map/ppermute | solution.py:328
  5.2 28.1 %collective-permute-start = (bf16[4,2,128,128]{3,2,1,0:T(8,128)(2,1)S(1)}, bf16[4,2,128,128]{3,2,1,0:T(8,128)(2,1)S(1)}, u32[]{:S(2)}, u32[]{:S(2)}) collective-permute-start(bf16[4,2,128,128]{3,2,1,0:T(8,128)(2,1)S(1)} %get-tuple-element.22), channel_id=1, source_target_pairs={{0,1},{1,0},{2,3},{3,2},{4,5},{5,4},{6,7},{7,6},{8,9},{9,8},{10,11... | collective-permute-start | bytes 786440 | tf_op jit(solution)/shard_map/ppermute | solution.py:329
  6.1 27.1 %collective-permute-start.1 = (bf16[4,2,128,128]{3,2,1,0:T(8,128)(2,1)S(1)}, bf16[4,2,128,128]{3,2,1,0:T(8,128)(2,1)S(1)}, u32[]{:S(2)}, u32[]{:S(2)}) collective-permute-start(bf16[4,2,128,128]{3,2,1,0:T(8,128)(2,1)S(1)} %get-tuple-element.23), channel_id=1, source_target_pairs={{1,2},{3,4},{5,6},{7,8},{9,10},{11,12},{13,14},{15,16},{17,18},{19... | collective-permute-start | bytes 786440 | tf_op jit(solution)/shard_map/ppermute | solution.py:330
  7.2 26.0 %all-to-all-start = ((f32[256,1,128]{2,1,0:T(1,128)}), f32[256,1,128]{2,1,0:T(1,128)S(1)}, u32[]{:S(2)}, u32[]{:S(2)}) async-start(f32[256,1,128]{2,1,0:T(1,128)} %bitcast.3), calls=%async_computation | async-start | bytes 262144 | tf_op jit(solution)/shard_map/all_to_all | solution.py:331
  20.8 18.0 %collective-permute-start.3 = (bf16[2,2,128,128]{3,2,1,0:T(8,128)(2,1)S(1)}, bf16[2,2,128,128]{3,2,1,0:T(8,128)(2,1)S(1)}, u32[]{:S(2)}, u32[]{:S(2)}) collective-permute-start(bf16[2,2,128,128]{3,2,1,0:T(8,128)(2,1)S(1)} %get-tuple-element.27), channel_id=1, source_target_pairs={{0,1},{1,0},{2,3},{3,2},{4,5},{5,4},{6,7},{7,6},{8,9},{9,8},{10,11... | collective-permute-start | bytes 393224 | tf_op jit(solution)/shard_map/ppermute | solution.py:336
  22.6 16.2 %collective-permute-start.4 = (bf16[2,2,128,128]{3,2,1,0:T(8,128)(2,1)S(1)}, bf16[2,2,128,128]{3,2,1,0:T(8,128)(2,1)S(1)}, u32[]{:S(2)}, u32[]{:S(2)}) collective-permute-start(bf16[2,2,128,128]{3,2,1,0:T(8,128)(2,1)S(1)} %get-tuple-element.28), channel_id=1, source_target_pairs={{1,2},{3,4},{5,6},{7,8},{9,10},{11,12},{13,14},{15,16},{17,18},{19... | collective-permute-start | bytes 393224 | tf_op jit(solution)/shard_map/ppermute | solution.py:337
  38.1 23.2 %collective-permute-start.5 = (bf16[2,10,128,128]{3,2,1,0:T(8,128)(2,1)S(1)}, bf16[2,10,128,128]{3,2,1,0:T(8,128)(2,1)S(1)}, u32[]{:S(2)}, u32[]{:S(2)}) collective-permute-start(bf16[2,10,128,128]{3,2,1,0:T(8,128)(2,1)S(1)} %get-tuple-element.32), channel_id=1, source_target_pairs={{0,32},{32,64},{64,96},{96,128},{128,160},{160,192},{192,224},{224... | collective-permute-start | bytes 1966088 | tf_op jit(solution)/shard_map/ppermute | solution.py:344
  38.8 22.5 %copy-start = (bf16[3,3,3,128,128]{4,3,2,1,0:T(8,128)(2,1)S(1)}, bf16[3,3,3,128,128]{4,3,2,1,0:T(8,128)(2,1)}, u32[]{:S(2)}) copy-start(bf16[3,3,3,128,128]{4,3,2,1,0:T(8,128)(2,1)} %param.16) | copy-start | bytes 2654212

commit v8 on v7

--- a/solution.py
+++ b/solution.py
@@ -152,12 +152,15 @@
         copy.wait()
 
 
-def pack_kernel(z_ref, near_ref, far_ref):
+def pack_kernel(kernel_hbm, z_ref, near_ref, far_ref, kernel_ref, sem):
+    fetch = pltpu.make_async_copy(kernel_hbm, kernel_ref, sem)
+    fetch.start()
     per = z_ref.shape[1]
     odd = lax.axis_index("space") & 1
     for f in range(2):
         near_ref[f] = z_ref[f, pl.ds((1 - odd) * (per - 2), 2)]
         far_ref[f] = z_ref[f, pl.ds(odd * (per - 2), 2)]
+    fetch.wait()
 
 
 def norm_constants(got_ref, small_ref, at, cells):
@@ -177,9 +180,7 @@
         mean, slope, half, late, spread = (consts_ref[i : i + 1] for i in range(5))
         bias = small_ref[2:3]
     else:
-        kernel_hbm, got_ref, small_ref, x_ref, in_ref, far_ref, inner_ref, send_ref, consts_ref, kernel, acts, mid, side, sem = refs
-        fetch = pltpu.make_async_copy(kernel_hbm, kernel, sem)
-        fetch.start()
+        kernel, got_ref, small_ref, x_ref, in_ref, far_ref, inner_ref, send_ref, consts_ref, acts, mid, side = refs
         mean, slope, half, bias = norm_constants(got_ref, small_ref, 0, cells)
     top, bottom = edges(strips)
     odd = (lax.axis_index("space") & 1) == 1
@@ -216,8 +217,6 @@
                     act(of(x_ref, 2 * f + 1), of(in_ref, 2 * f + 1), of(far_ref, 2 * f + 1), 2 * f + 1, r)
         done = at + rows + 2
         if at == 0:
-            if not early:
-                fetch.wait()
             build_taps(kernel, mid, side)
         conv_pair(acts, mid, side, 0, at, rows, put)
     own = lambda i: inner_ref[i // 8, 1 + i % 8]
@@ -319,7 +318,7 @@
         stats_kernel,
         out_shape=[
             shape((4, 8, 128, 128), BF16), shape((devices, 128), F32), shape((2, 8, 128, 128), BF16),
-            shape((4, 2, 128, 128), BF16), shape((4, 2, 128, 128), BF16), shape((6, 128), F32),
+            pltpu.HBM((4, 2, 128, 128), BF16), pltpu.HBM((4, 2, 128, 128), BF16), shape((6, 128), F32),
         ],
         in_specs=[HBM] * 7, out_specs=[VMEM] * 6,
         scratch_shapes=[DMA((10,))], compiler_params=PARAMS,
@@ -329,16 +328,17 @@
     near = lax.ppermute(in_send, "space", swap_in)
     far = lax.ppermute(far_send, "space", swap_far)
     got = lax.all_to_all(pay, BOTH, 0, 0)
-    near_send, far_send = pl.pallas_call(
-        pack_kernel, out_shape=[shape((2, 2, 128, 128), BF16)] * 2, in_specs=[VMEM], out_specs=[VMEM] * 2, compiler_params=PARAMS,
+    near_send, far_send, taps_one = pl.pallas_call(
+        pack_kernel, out_shape=[pltpu.HBM((2, 2, 128, 128), BF16)] * 2 + [shape((3, 9 * 128, 128), BF16)],
+        in_specs=[HBM, VMEM], out_specs=[VMEM] * 3, scratch_shapes=[DMA], compiler_params=PARAMS,
         cost_estimate=pl.CostEstimate(flops=0, bytes_accessed=1 << 19, transcendentals=0), name="pack",
-    )(z_one)
+    )(taps_one, z_one)
     z_near = lax.ppermute(near_send, "space", swap_in)
     z_far = lax.ppermute(far_send, "space", swap_far)
-    inner_a, send, consts, kernel = pl.pallas_call(
+    inner_a, send, consts = pl.pallas_call(
         functools.partial(first_kernel, False, cells, strips),
-        out_shape=[shape((2, 10, 128, 128), F32), shape((2, 10, 128, 128), BF16), shape((8, 128), F32), shape((3, 9 * 128, 128), BF16)],
-        in_specs=[HBM] + [VMEM] * 5, out_specs=[VMEM] * 4, scratch_shapes=scratch(4, 12) + [DMA],
+        out_shape=[shape((2, 10, 128, 128), F32), shape((2, 10, 128, 128), BF16), shape((8, 128), F32)],
+        in_specs=[VMEM] * 6, out_specs=[VMEM] * 3, scratch_shapes=scratch(4, 12),
         compiler_params=PARAMS, cost_estimate=cost(1, 10), name="first_late",
     )(taps_one, got, small, x, near, far)
     z_two = lax.ppermute(send, "tm", later)
@@ -347,7 +347,7 @@
         out_shape=[shape((2, 10, 128, 128), F32), shape((devices, 128), F32)],
         in_specs=[VMEM] * 9, out_specs=[VMEM] * 2, scratch_shapes=scratch(4, 12),
         compiler_params=PARAMS, cost_estimate=cost(1, 10), name="first_early",
-    )(kernel, consts, small, x, near, far, z_one, z_near, z_far)
+    )(taps_one, consts, small, x, near, far, z_one, z_near, z_far)
     got = lax.all_to_all(pay, BOTH, 0, 0)
     return pl.pallas_call(
         functools.partial(second_kernel, cells, strips),

time: 67.4 us -> 66.6 us (0.988)
  waiting for transfers between devices: 10.4 us -> 8.61 us
  Pallas kernels: 16.6 us -> 17.6 us
    pallas_call x1, Pallas kernels: 0.02 us -> 1.87 us  [shards(): pl.pallas_call(pack_kernel, out_shape=[pltpu.HBM((2, 2, 128, 128), BF16)]...]
    all_to_all x1, waiting for transfers between devices: 9.93 us -> 8.15 us  [shards(): got = lax.all_to_all(pay, BOTH, 0, 0)]
    pallas_call x1, Pallas kernels: 4.83 us -> 3.82 us  [shards(): pl.pallas_call(functools.partial(first_kernel, False, cells, strips), out...]
  transfers between devices with their start and end apart: 7 -> 7, of which waited for: 2 -> 2; matrix products, arithmetic and copies ran while one was open for 0% -> 0% of each run, Pallas kernels for 12% -> 14%
where the time goes in v8:
time: 66.6 us; the launch traced here: 66.4 us
  starting transfers between devices  20.9 us (31%)
  blocking collectives  19.1 us (29%)
  Pallas kernels  17.6 us (26%)
  waiting for transfers between devices  8.61 us (13%)
    all_to_all x1, blocking collectives, shards(): got = lax.all_to_all(pay, BOTH, 0, 0)  19.1 us
    all_to_all x1, starting transfers between devices, shards(): got = lax.all_to_all(pay, BOTH, 0, 0)  13.1 us
    all_to_all x1, waiting for transfers between devices, shards(): got = lax.all_to_all(pay, BOTH, 0, 0)  8.15 us
    pallas_call x1, Pallas kernels, shards(): pl.pallas_call(functools.partial(second_kernel, cells, strips), out_shape...  5.8 us
    pallas_call x1, Pallas kernels, shards(): pl.pallas_call(functools.partial(first_kernel, False, cells, strips), out...  3.82 us
    pallas_call x1, Pallas kernels, shards(): pl.pallas_call(functools.partial(first_kernel, True, cells, strips), out_...  3.35 us
    pallas_call x1, Pallas kernels, shards(): pl.pallas_call(stats_kernel, out_shape=[shape((4, 8, 128, 128), BF16), sh...  2.78 us
    ppermute x1, starting transfers between devices, shards(): z_one = lax.ppermute(z_send, 'tm', later)  2.54 us
  transfers between devices with their start and end apart: 7, of which 2 were waited for; matrix products, arithmetic and copies ran while one was open for 0% of the time, Pallas kernels for 14%

profile of v8, /device:TPU:1, one launch (start us, length us, event | category | flops | bytes accessed | tf_op | source)
XLA Modules:
  0.0 66.4 jit_solution(10908579868567234950)
XLA Ops:
  0.0 2.8 %stats.1 = (bf16[4,8,128,128]{3,2,1,0:T(8,128)(2,1)S(1)}, f32[256,128]{1,0:T(8,128)}, bf16[2,8,128,128]{3,2,1,0:T(8,128)(2,1)S(1)}, bf16[4,2,128,128]{3,2,1,0:T(...) custom-call(bf16[4,8,128,128]{3,2,1,0:T(8,128)(2,1)} %x_hbm.1, f32[128]{0:T(128)} %refs_0_.1, ...), custom_call_target="tpu_custom_call" | custom-call | flops 4194304 | bytes 1048576 | tf_op jit(solution)/shard_map/stats/pallas_call | solution.py:317
  2.8 2.5 %collective-permute-start = (bf16[2,8,128,128]{3,2,1,0:T(8,128)(2,1)S(1)}, bf16[2,8,128,128]{3,2,1,0:T(8,128)(2,1)S(1)}, u32[]{:S(2)}, u32[]{:S(2)}) collective-permute-start(bf16[2,8,128,128]{3,2,1,0:T(8,128)(2,1)S(1)} %get-tuple-element.19), channel_id=1, source_target_pairs={{0,32},{32,64},{64,96},{96,128},{128,160},{160,192},{192,224},{224... | collective-permute-start | bytes 1572872 | tf_op jit(solution)/shard_map/ppermute | solution.py:327
  5.3 1.0 %collective-permute-start.1 = (bf16[4,2,128,128]{3,2,1,0:T(8,128)(2,1)}, bf16[4,2,128,128]{3,2,1,0:T(8,128)(2,1)S(1)}, u32[]{:S(2)}, u32[]{:S(2)}) collective-permute-start(bf16[4,2,128,128]{3,2,1,0:T(8,128)(2,1)} %get-tuple-element.24), channel_id=1, source_target_pairs={{0,1},{1,0},{2,3},{3,2},{4,5},{5,4},{6,7},{7,6},{8,9},{9,8},{10,11... | collective-permute-start | bytes 786440 | tf_op jit(solution)/shard_map/ppermute | solution.py:328
  6.3 1.1 %collective-permute-start.2 = (bf16[4,2,128,128]{3,2,1,0:T(8,128)(2,1)}, bf16[4,2,128,128]{3,2,1,0:T(8,128)(2,1)S(1)}, u32[]{:S(2)}, u32[]{:S(2)}) collective-permute-start(bf16[4,2,128,128]{3,2,1,0:T(8,128)(2,1)} %get-tuple-element.25), channel_id=1, source_target_pairs={{1,2},{3,4},{5,6},{7,8},{9,10},{11,12},{13,14},{15,16},{17,18},{19... | collective-permute-start | bytes 786440 | tf_op jit(solution)/shard_map/ppermute | solution.py:329
  7.4 13.1 %all-to-all-start = ((f32[256,1,128]{2,1,0:T(1,128)}), f32[256,1,128]{2,1,0:T(1,128)S(1)}, u32[]{:S(2)}, u32[]{:S(2)}) async-start(f32[256,1,128]{2,1,0:T(1,128)} %bitcast.3), calls=%async_computation | async-start | bytes 262144 | tf_op jit(solution)/shard_map/all_to_all | solution.py:330
  20.5 0.4 collective-permute-done.z_ref.refs_6_
  20.9 1.9 %pack.1 = (bf16[2,2,128,128]{3,2,1,0:T(8,128)(2,1)}, bf16[2,2,128,128]{3,2,1,0:T(8,128)(2,1)}, bf16[3,1152,128]{2,1,0:T(8,128)(2,1)S(1)}) custom-call(bf16[3,1152,128]{2,1,0:T(8,128)(2,1)} %bitcast.14, bf16[2,8,128,128]{3,2,1,0:T(8,128)(2,1)S(1)} %collective-permute-done.z_ref.refs_6_), custom_call_target="tpu_custom_call" | custom-call | bytes 524288 | tf_op jit(solution)/shard_map/pack/pallas_call | solution.py:331
  22.8 1.8 %collective-permute-start.3 = (bf16[2,2,128,128]{3,2,1,0:T(8,128)(2,1)}, bf16[2,2,128,128]{3,2,1,0:T(8,128)(2,1)S(1)}, u32[]{:S(2)}, u32[]{:S(2)}) collective-permute-start(bf16[2,2,128,128]{3,2,1,0:T(8,128)(2,1)} %get-tuple-element.27), channel_id=1, source_target_pairs={{0,1},{1,0},{2,3},{3,2},{4,5},{5,4},{6,7},{7,6},{8,9},{9,8},{10,11... | collective-permute-start | bytes 393224 | tf_op jit(solution)/shard_map/ppermute | solution.py:336
  24.6 0.7 %collective-permute-start.4 = (bf16[2,2,128,128]{3,2,1,0:T(8,128)(2,1)}, bf16[2,2,128,128]{3,2,1,0:T(8,128)(2,1)S(1)}, u32[]{:S(2)}, u32[]{:S(2)}) collective-permute-start(bf16[2,2,128,128]{3,2,1,0:T(8,128)(2,1)} %get-tuple-element.28), channel_id=1, source_target_pairs={{1,2},{3,4},{5,6},{7,8},{9,10},{11,12},{13,14},{15,16},{17,18},{19... | collective-permute-start | bytes 393224 | tf_op jit(solution)/shard_map/ppermute | solution.py:337
  25.3 8.1 %all-to-all-done = f32[256,1,128]{2,1,0:T(1,128)S(1)} async-done(((f32[256,1,128]{2,1,0:T(1,128)}), f32[256,1,128]{2,1,0:T(1,128)S(1)}, u32[]{:S(2)}, u32[]{:S(2)}) %all-to-all-start) | async-done | bytes 131104 | tf_op jit(solution)/shard_map/all_to_all | solution.py:330
  33.5 0.0 collective-permute-done.1.refs_4_
  33.5 0.0 collective-permute-done.2.refs_5_
  33.5 3.8 %first_late.1 = (f32[2,10,128,128]{3,2,1,0:T(8,128)S(1)}, bf16[2,10,128,128]{3,2,1,0:T(8,128)(2,1)S(1)}, f32[8,128]{1,0:T(8,128)S(1)}) custom-call(bf16[3,1152,128]{2,1,0:T(8,128)(2,1)S(1)} %get-tuple-element.20.refs_0_, f32[256,128]{1,0:T(8,128)S(1)} %bitcast.10, f32[6,128]{1,0:T(8,128)S(1)} %get-tuple-element.22.refs_2_.small_ref, ...), custom_call_target="tpu_custom_call" | custom-call | flops 3019898880 | bytes 4194304 | tf_op jit(solution)/shard_map/first_late/pallas_call | solution.py:338
  37.3 0.7 %collective-permute-start.5 = (bf16[2,10,128,128]{3,2,1,0:T(8,128)(2,1)S(1)}, bf16[2,10,128,128]{3,2,1,0:T(8,128)(2,1)S(1)}, u32[]{:S(2)}, u32[]{:S(2)}) collective-permute-start(bf16[2,10,128,128]{3,2,1,0:T(8,128)(2,1)S(1)} %get-tuple-element.32), channel_id=1, source_target_pairs={{0,32},{32,64},{64,96},{96,128},{128,160},{160,192},{192,224},{224... | collective-permute-start | bytes 1966088 | tf_op jit(solution)/shard_map/ppermute | solution.py:344
  38.0 0.0 collective-permute-done.3.refs_7_
  38.0 0.0 collective-permute-done.4.refs_8_
  38.0 0.0 copy-start
  38.0 3.3 %first_early.1 = (f32[2,10,128,128]{3,2,1,0:T(8,128)S(1)}, f32[256,128]{1,0:T(8,128)S(1)}) custom-call(bf16[3,1152,128]{2,1,0:T(8,128)(2,1)S(1)} %get-tuple-element.20.refs_0_, f32[8,128]{1,0:T(8,128)S(1)} %get-tuple-element.26.refs_1_, f32[6,128]{1,0:T(8,128)S(1)} %get-tuple-element.22.refs_2_.small_ref, ...), custom_call_target="tpu_custom_call" | custom-call | flops 3019898880 | bytes 4194304 | tf_op jit(solution)/shard_map/first_early/pallas_call | solution.py:345
  41.3 19.1 %all_to_all.22 = f32[256,1,128]{2,1,0:T(1,128)S(1)} all-to-all(f32[256,1,128]{2,1,0:T(1,128)S(1)} %bitcast.12), channel_id=1, replica_groups=mesh['tm'=8,'space'=32] {'tm','space'}, dimensions={0} | all-to-all | bytes 262144 | tf_op jit(solution)/shard_map/all_to_all | solution.py:351
  60.4 0.0 collective-permute-done.5.z_ref
  60.4 0.0 copy-done
  60.4 5.8 %second.1 = f32[4,8,128,128]{3,2,1,0:T(8,128)} custom-call(bf16[3,1152,128]{2,1,0:T(8,128)(2,1)S(1)} %bitcast.13, f32[256,128]{1,0:T(8,128)S(1)} %bitcast.11, f32[6,128]{1,0:T(8,128)S(1)} %get-tuple-element.22.refs_2_.small_ref, bf16[4,8,128,128]{3,2,1,0:T(8,128)(2,1)S(1)} %get-tuple-element.23.refs_3_.feat_ref, ...), custom_call_target="tpu_custom_call" | custom-call | flops 4831838208 | bytes 4194304 | tf_op jit(solution)/shard_map/second/pallas_call | solution.py:352
Async XLA Ops:
  2.8 18.1 %collective-permute-start = (bf16[2,8,128,128]{3,2,1,0:T(8,128)(2,1)S(1)}, bf16[2,8,128,128]{3,2,1,0:T(8,128)(2,1)S(1)}, u32[]{:S(2)}, u32[]{:S(2)}) collective-permute-start(bf16[2,8,128,128]{3,2,1,0:T(8,128)(2,1)S(1)} %get-tuple-element.19), channel_id=1, source_target_pairs={{0,32},{32,64},{64,96},{96,128},{128,160},{160,192},{192,224},{224... | collective-permute-start | bytes 1572872 | tf_op jit(solution)/shard_map/ppermute | solution.py:327
  5.3 28.1 %collective-permute-start.1 = (bf16[4,2,128,128]{3,2,1,0:T(8,128)(2,1)}, bf16[4,2,128,128]{3,2,1,0:T(8,128)(2,1)S(1)}, u32[]{:S(2)}, u32[]{:S(2)}) collective-permute-start(bf16[4,2,128,128]{3,2,1,0:T(8,128)(2,1)} %get-tuple-element.24), channel_id=1, source_target_pairs={{0,1},{1,0},{2,3},{3,2},{4,5},{5,4},{6,7},{7,6},{8,9},{9,8},{10,11... | collective-permute-start | bytes 786440 | tf_op jit(solution)/shard_map/ppermute | solution.py:328
  6.3 27.2 %collective-permute-start.2 = (bf16[4,2,128,128]{3,2,1,0:T(8,128)(2,1)}, bf16[4,2,128,128]{3,2,1,0:T(8,128)(2,1)S(1)}, u32[]{:S(2)}, u32[]{:S(2)}) collective-permute-start(bf16[4,2,128,128]{3,2,1,0:T(8,128)(2,1)} %get-tuple-element.25), channel_id=1, source_target_pairs={{1,2},{3,4},{5,6},{7,8},{9,10},{11,12},{13,14},{15,16},{17,18},{19... | collective-permute-start | bytes 786440 | tf_op jit(solution)/shard_map/ppermute | solution.py:329
  7.4 26.1 %all-to-all-start = ((f32[256,1,128]{2,1,0:T(1,128)}), f32[256,1,128]{2,1,0:T(1,128)S(1)}, u32[]{:S(2)}, u32[]{:S(2)}) async-start(f32[256,1,128]{2,1,0:T(1,128)} %bitcast.3), calls=%async_computation | async-start | bytes 262144 | tf_op jit(solution)/shard_map/all_to_all | solution.py:330
  22.8 15.2 %collective-permute-start.3 = (bf16[2,2,128,128]{3,2,1,0:T(8,128)(2,1)}, bf16[2,2,128,128]{3,2,1,0:T(8,128)(2,1)S(1)}, u32[]{:S(2)}, u32[]{:S(2)}) collective-permute-start(bf16[2,2,128,128]{3,2,1,0:T(8,128)(2,1)} %get-tuple-element.27), channel_id=1, source_target_pairs={{0,1},{1,0},{2,3},{3,2},{4,5},{5,4},{6,7},{7,6},{8,9},{9,8},{10,11... | collective-permute-start | bytes 393224 | tf_op jit(solution)/shard_map/ppermute | solution.py:336
  24.6 13.4 %collective-permute-start.4 = (bf16[2,2,128,128]{3,2,1,0:T(8,128)(2,1)}, bf16[2,2,128,128]{3,2,1,0:T(8,128)(2,1)S(1)}, u32[]{:S(2)}, u32[]{:S(2)}) collective-permute-start(bf16[2,2,128,128]{3,2,1,0:T(8,128)(2,1)} %get-tuple-element.28), channel_id=1, source_target_pairs={{1,2},{3,4},{5,6},{7,8},{9,10},{11,12},{13,14},{15,16},{17,18},{19... | collective-permute-start | bytes 393224 | tf_op jit(solution)/shard_map/ppermute | solution.py:337
  37.3 23.1 %collective-permute-start.5 = (bf16[2,10,128,128]{3,2,1,0:T(8,128)(2,1)S(1)}, bf16[2,10,128,128]{3,2,1,0:T(8,128)(2,1)S(1)}, u32[]{:S(2)}, u32[]{:S(2)}) collective-permute-start(bf16[2,10,128,128]{3,2,1,0:T(8,128)(2,1)S(1)} %get-tuple-element.32), channel_id=1, source_target_pairs={{0,32},{32,64},{64,96},{96,128},{128,160},{160,192},{192,224},{224... | collective-permute-start | bytes 1966088 | tf_op jit(solution)/shard_map/ppermute | solution.py:344
  38.0 22.4 %copy-start = (bf16[3,3,3,128,128]{4,3,2,1,0:T(8,128)(2,1)S(1)}, bf16[3,3,3,128,128]{4,3,2,1,0:T(8,128)(2,1)}, u32[]{:S(2)}) copy-start(bf16[3,3,3,128,128]{4,3,2,1,0:T(8,128)(2,1)} %param.16) | copy-start | bytes 2654212

commit v9 on v8

--- a/solution.py
+++ b/solution.py
@@ -127,7 +127,7 @@
 
 
 def stats_kernel(x_hbm, *refs):
-    small, (x_ref, pay_ref, z_ref, in_ref, far_ref, small_ref, sems) = refs[:6], refs[6:]
+    small, (x_ref, pay_ref, z_ref, in_out, far_out, small_ref, in_ref, far_ref, sems, out_sems) = refs[:6], refs[6:]
     frames, per = x_ref.shape[:2]
     copies = [pltpu.make_async_copy(x_hbm.at[f], x_ref.at[f], sems.at[f]) for f in range(frames)]
     copies += [pltpu.make_async_copy(v, small_ref.at[i], sems.at[frames + i]) for i, v in enumerate(small)]
@@ -144,11 +144,17 @@
             low, high = x_ref[f, r], x_ref[f, per - 2 + r]
             in_ref[f, r] = jnp.where(odd, low, high)
             far_ref[f, r] = jnp.where(odd, high, low)
+    leaving = [
+        pltpu.make_async_copy(in_ref, in_out, out_sems.at[0]),
+        pltpu.make_async_copy(far_ref, far_out, out_sems.at[1]),
+    ]
+    for copy in leaving:
+        copy.start()
     z_ref[...] = x_ref[2:]
     sums = shifted_sums(lambda i: load(per + i), (frames - 1) * per, mean)
     mean, spread = joined(mean, spread, cells, *sums, (frames - 1) * cells)
     pay_ref[...] = jnp.broadcast_to(payload(mean, spread)[:1], pay_ref.shape)
-    for copy in copies[frames:]:
+    for copy in copies[frames:] + leaving:
         copy.wait()
 
 
@@ -176,11 +182,11 @@
 
 def first_kernel(early, cells, strips, *refs):
     if early:
-        kernel, consts_ref, small_ref, x_ref, in_ref, far_ref, z_ref, z_in_ref, z_far_ref, inner_ref, pay_ref, acts, mid, side = refs
+        mid, side, consts_ref, small_ref, x_ref, in_ref, far_ref, z_ref, z_in_ref, z_far_ref, inner_ref, pay_ref, acts = refs
         mean, slope, half, late, spread = (consts_ref[i : i + 1] for i in range(5))
         bias = small_ref[2:3]
     else:
-        kernel, got_ref, small_ref, x_ref, in_ref, far_ref, inner_ref, send_ref, consts_ref, acts, mid, side = refs
+        kernel, got_ref, small_ref, x_ref, in_ref, far_ref, inner_ref, send_ref, consts_ref, mid, side, acts = refs
         mean, slope, half, bias = norm_constants(got_ref, small_ref, 0, cells)
     top, bottom = edges(strips)
     odd = (lax.axis_index("space") & 1) == 1
@@ -206,7 +212,7 @@
         inner_ref[o, r] = value + bias
 
     done = 0
-    for at, rows in (((0, 6), (6, 4)) if early else ((0, 5), (5, 5))):
+    for at, rows in ((0, 6), (6, 4)):
         for r in range(done, at + rows + 2):
             for f in range(2):
                 if early:
@@ -217,7 +223,8 @@
                     act(of(x_ref, 2 * f + 1), of(in_ref, 2 * f + 1), of(far_ref, 2 * f + 1), 2 * f + 1, r)
         done = at + rows + 2
         if at == 0:
-            build_taps(kernel, mid, side)
+            if not early:
+                build_taps(kernel, mid, side)
         conv_pair(acts, mid, side, 0, at, rows, put)
     own = lambda i: inner_ref[i // 8, 1 + i % 8]
     if early:
@@ -320,8 +327,8 @@
             shape((4, 8, 128, 128), BF16), shape((devices, 128), F32), shape((2, 8, 128, 128), BF16),
             pltpu.HBM((4, 2, 128, 128), BF16), pltpu.HBM((4, 2, 128, 128), BF16), shape((6, 128), F32),
         ],
-        in_specs=[HBM] * 7, out_specs=[VMEM] * 6,
-        scratch_shapes=[DMA((10,))], compiler_params=PARAMS,
+        in_specs=[HBM] * 7, out_specs=[VMEM] * 3 + [HBM] * 2 + [VMEM],
+        scratch_shapes=[pltpu.VMEM((4, 2, 128, 128), BF16)] * 2 + [DMA((10,)), DMA((2,))], compiler_params=PARAMS,
         cost_estimate=pl.CostEstimate(flops=1 << 22, bytes_accessed=1 << 20, transcendentals=0), name="stats",
     )(*map(in_hbm, (features, gain_one, shift_one, bias_one, gain_two, shift_two, bias_two)))
     z_one = lax.ppermute(z_send, "tm", later)
@@ -335,19 +342,20 @@
     )(taps_one, z_one)
     z_near = lax.ppermute(near_send, "space", swap_in)
     z_far = lax.ppermute(far_send, "space", swap_far)
-    inner_a, send, consts = pl.pallas_call(
+    inner_a, send, consts, mid, side = pl.pallas_call(
         functools.partial(first_kernel, False, cells, strips),
-        out_shape=[shape((2, 10, 128, 128), F32), shape((2, 10, 128, 128), BF16), shape((8, 128), F32)],
-        in_specs=[VMEM] * 6, out_specs=[VMEM] * 3, scratch_shapes=scratch(4, 12),
+        out_shape=[shape((2, 10, 128, 128), F32), shape((2, 10, 128, 128), BF16), shape((8, 128), F32)]
+        + [shape((n * 128, 256), BF16) for n in (12, 9)],
+        in_specs=[VMEM] * 6, out_specs=[VMEM] * 5, scratch_shapes=scratch(4, 12)[:1],
         compiler_params=PARAMS, cost_estimate=cost(1, 10), name="first_late",
     )(taps_one, got, small, x, near, far)
     z_two = lax.ppermute(send, "tm", later)
     inner_b, pay = pl.pallas_call(
         functools.partial(first_kernel, True, cells, strips),
         out_shape=[shape((2, 10, 128, 128), F32), shape((devices, 128), F32)],
-        in_specs=[VMEM] * 9, out_specs=[VMEM] * 2, scratch_shapes=scratch(4, 12),
+        in_specs=[VMEM] * 10, out_specs=[VMEM] * 2, scratch_shapes=scratch(4, 12)[:1],
         compiler_params=PARAMS, cost_estimate=cost(1, 10), name="first_early",
-    )(taps_one, consts, small, x, near, far, z_one, z_near, z_far)
+    )(mid, side, consts, small, x, near, far, z_one, z_near, z_far)
     got = lax.all_to_all(pay, BOTH, 0, 0)
     return pl.pallas_call(
         functools.partial(second_kernel, cells, strips),

time: 66.6 us -> 67.1 us (level)
  transfers between devices with their start and end apart: 7 -> 7, of which waited for: 2 -> 2; matrix products, arithmetic and copies ran while one was open for 0% -> 0% of each run, Pallas kernels for 14% -> 13%
where the time goes in v9:
time: 67.1 us; the launch traced here: 66.9 us
  starting transfers between devices  20.9 us (31%)
  blocking collectives  19.1 us (28%)
  Pallas kernels  18.1 us (27%)
  waiting for transfers between devices  8.61 us (13%)
    all_to_all x1, blocking collectives, shards(): got = lax.all_to_all(pay, BOTH, 0, 0)  19.1 us
    all_to_all x1, starting transfers between devices, shards(): got = lax.all_to_all(pay, BOTH, 0, 0)  13.1 us
    all_to_all x1, waiting for transfers between devices, shards(): got = lax.all_to_all(pay, BOTH, 0, 0)  8.15 us
    pallas_call x1, Pallas kernels, shards(): pl.pallas_call(functools.partial(second_kernel, cells, strips), out_shape...  5.79 us
    pallas_call x1, Pallas kernels, shards(): pl.pallas_call(functools.partial(first_kernel, False, cells, strips), out...  3.87 us
    pallas_call x1, Pallas kernels, shards(): pl.pallas_call(stats_kernel, out_shape=[shape((4, 8, 128, 128), BF16), sh...  3.33 us
    pallas_call x1, Pallas kernels, shards(): pl.pallas_call(functools.partial(first_kernel, True, cells, strips), out_...  3.27 us
    ppermute x1, starting transfers between devices, shards(): z_one = lax.ppermute(z_send, 'tm', later)  2.54 us
  transfers between devices with their start and end apart: 7, of which 2 were waited for; matrix products, arithmetic and copies ran while one was open for 0% of the time, Pallas kernels for 13%

profile of v9, /device:TPU:1, one launch (start us, length us, event | category | flops | bytes accessed | tf_op | source)
XLA Modules:
  0.0 66.9 jit_solution(4747661360853720465)
XLA Ops:
  0.0 3.3 %stats.1 = (bf16[4,8,128,128]{3,2,1,0:T(8,128)(2,1)S(1)}, f32[256,128]{1,0:T(8,128)}, bf16[2,8,128,128]{3,2,1,0:T(8,128)(2,1)S(1)}, bf16[4,2,128,128]{3,2,1,0:T(...) custom-call(bf16[4,8,128,128]{3,2,1,0:T(8,128)(2,1)} %x_hbm.1, f32[128]{0:T(128)} %refs_0_.1, ...), custom_call_target="tpu_custom_call" | custom-call | flops 4194304 | bytes 1048576 | tf_op jit(solution)/shard_map/stats/pallas_call | solution.py:324
  3.3 2.5 %collective-permute-start = (bf16[2,8,128,128]{3,2,1,0:T(8,128)(2,1)S(1)}, bf16[2,8,128,128]{3,2,1,0:T(8,128)(2,1)S(1)}, u32[]{:S(2)}, u32[]{:S(2)}) collective-permute-start(bf16[2,8,128,128]{3,2,1,0:T(8,128)(2,1)S(1)} %get-tuple-element.21), channel_id=1, source_target_pairs={{0,32},{32,64},{64,96},{96,128},{128,160},{160,192},{192,224},{224... | collective-permute-start | bytes 1572872 | tf_op jit(solution)/shard_map/ppermute | solution.py:334
  5.9 1.0 %collective-permute-start.1 = (bf16[4,2,128,128]{3,2,1,0:T(8,128)(2,1)}, bf16[4,2,128,128]{3,2,1,0:T(8,128)(2,1)S(1)}, u32[]{:S(2)}, u32[]{:S(2)}) collective-permute-start(bf16[4,2,128,128]{3,2,1,0:T(8,128)(2,1)} %get-tuple-element.26), channel_id=1, source_target_pairs={{0,1},{1,0},{2,3},{3,2},{4,5},{5,4},{6,7},{7,6},{8,9},{9,8},{10,11... | collective-permute-start | bytes 786440 | tf_op jit(solution)/shard_map/ppermute | solution.py:335
  6.8 1.1 %collective-permute-start.2 = (bf16[4,2,128,128]{3,2,1,0:T(8,128)(2,1)}, bf16[4,2,128,128]{3,2,1,0:T(8,128)(2,1)S(1)}, u32[]{:S(2)}, u32[]{:S(2)}) collective-permute-start(bf16[4,2,128,128]{3,2,1,0:T(8,128)(2,1)} %get-tuple-element.27), channel_id=1, source_target_pairs={{1,2},{3,4},{5,6},{7,8},{9,10},{11,12},{13,14},{15,16},{17,18},{19... | collective-permute-start | bytes 786440 | tf_op jit(solution)/shard_map/ppermute | solution.py:336
  7.9 13.1 %all-to-all-start = ((f32[256,1,128]{2,1,0:T(1,128)}), f32[256,1,128]{2,1,0:T(1,128)S(1)}, u32[]{:S(2)}, u32[]{:S(2)}) async-start(f32[256,1,128]{2,1,0:T(1,128)} %bitcast.3), calls=%async_computation | async-start | bytes 262144 | tf_op jit(solution)/shard_map/all_to_all | solution.py:337
  21.0 0.4 collective-permute-done.z_ref.refs_7_
  21.5 1.9 %pack.1 = (bf16[2,2,128,128]{3,2,1,0:T(8,128)(2,1)}, bf16[2,2,128,128]{3,2,1,0:T(8,128)(2,1)}, bf16[3,1152,128]{2,1,0:T(8,128)(2,1)S(1)}) custom-call(bf16[3,1152,128]{2,1,0:T(8,128)(2,1)} %bitcast.14, bf16[2,8,128,128]{3,2,1,0:T(8,128)(2,1)S(1)} %collective-permute-done.z_ref.refs_7_), custom_call_target="tpu_custom_call" | custom-call | bytes 524288 | tf_op jit(solution)/shard_map/pack/pallas_call | solution.py:338
  23.4 1.8 %collective-permute-start.3 = (bf16[2,2,128,128]{3,2,1,0:T(8,128)(2,1)}, bf16[2,2,128,128]{3,2,1,0:T(8,128)(2,1)S(1)}, u32[]{:S(2)}, u32[]{:S(2)}) collective-permute-start(bf16[2,2,128,128]{3,2,1,0:T(8,128)(2,1)} %get-tuple-element.31), channel_id=1, source_target_pairs={{0,1},{1,0},{2,3},{3,2},{4,5},{5,4},{6,7},{7,6},{8,9},{9,8},{10,11... | collective-permute-start | bytes 393224 | tf_op jit(solution)/shard_map/ppermute | solution.py:343
  25.1 0.7 %collective-permute-start.4 = (bf16[2,2,128,128]{3,2,1,0:T(8,128)(2,1)}, bf16[2,2,128,128]{3,2,1,0:T(8,128)(2,1)S(1)}, u32[]{:S(2)}, u32[]{:S(2)}) collective-permute-start(bf16[2,2,128,128]{3,2,1,0:T(8,128)(2,1)} %get-tuple-element.32), channel_id=1, source_target_pairs={{1,2},{3,4},{5,6},{7,8},{9,10},{11,12},{13,14},{15,16},{17,18},{19... | collective-permute-start | bytes 393224 | tf_op jit(solution)/shard_map/ppermute | solution.py:344
  25.9 8.1 %all-to-all-done = f32[256,1,128]{2,1,0:T(1,128)S(1)} async-done(((f32[256,1,128]{2,1,0:T(1,128)}), f32[256,1,128]{2,1,0:T(1,128)S(1)}, u32[]{:S(2)}, u32[]{:S(2)}) %all-to-all-start) | async-done | bytes 131104 | tf_op jit(solution)/shard_map/all_to_all | solution.py:337
  34.0 0.0 collective-permute-done.1.refs_4_.refs_5_
  34.0 0.0 collective-permute-done.2.refs_5_.refs_6_
  34.0 3.9 %first_late.1 = (f32[2,10,128,128]{3,2,1,0:T(8,128)S(1)}, bf16[2,10,128,128]{3,2,1,0:T(8,128)(2,1)S(1)}, f32[8,128]{1,0:T(8,128)S(1)}, bf16[1536,256]{1,0:T(8,128)(2,1)S(1)}, bf16[1152,256]{1,0:T(8,128)(2,1)S(1)}) custom-call(bf16[3,1152,128]{2,1,0:T(8,128)(2,1)S(1)} %get-tuple-element.22.refs_0_, f32[256,128]{1,0:T(8,128)S(1)} %bitcast.10, ...), custom_call_target="tpu_custom_call" | custom-call | flops 3019898880 | bytes 4194304 | tf_op jit(solution)/shard_map/first_late/pallas_call | solution.py:345
  37.9 0.7 %collective-permute-start.5 = (bf16[2,10,128,128]{3,2,1,0:T(8,128)(2,1)S(1)}, bf16[2,10,128,128]{3,2,1,0:T(8,128)(2,1)S(1)}, u32[]{:S(2)}, u32[]{:S(2)}) collective-permute-start(bf16[2,10,128,128]{3,2,1,0:T(8,128)(2,1)S(1)} %get-tuple-element.36), channel_id=1, source_target_pairs={{0,32},{32,64},{64,96},{96,128},{128,160},{160,192},{192,224},{224... | collective-permute-start | bytes 1966088 | tf_op jit(solution)/shard_map/ppermute | solution.py:352
  38.6 0.0 collective-permute-done.3.refs_8_
  38.6 0.0 collective-permute-done.4.refs_9_
  38.6 0.0 copy-start
  38.6 3.3 %first_early.1 = (f32[2,10,128,128]{3,2,1,0:T(8,128)S(1)}, f32[256,128]{1,0:T(8,128)S(1)}) custom-call(bf16[1536,256]{1,0:T(8,128)(2,1)S(1)} %get-tuple-element.28.refs_0_, bf16[1152,256]{1,0:T(8,128)(2,1)S(1)} %get-tuple-element.29.refs_1_, f32[8,128]{1,0:T(8,128)S(1)} %get-tuple-element.30.refs_2_, ...), custom_call_target="tpu_custom_call" | custom-call | flops 3019898880 | bytes 4194304 | tf_op jit(solution)/shard_map/first_early/pallas_call | solution.py:353
  41.9 19.1 %all_to_all.22 = f32[256,1,128]{2,1,0:T(1,128)S(1)} all-to-all(f32[256,1,128]{2,1,0:T(1,128)S(1)} %bitcast.12), channel_id=1, replica_groups=mesh['tm'=8,'space'=32] {'tm','space'}, dimensions={0} | all-to-all | bytes 262144 | tf_op jit(solution)/shard_map/all_to_all | solution.py:359
  60.9 0.0 collective-permute-done.5.z_ref
  61.0 0.0 copy-done
  61.0 5.8 %second.1 = f32[4,8,128,128]{3,2,1,0:T(8,128)} custom-call(bf16[3,1152,128]{2,1,0:T(8,128)(2,1)S(1)} %bitcast.13, f32[256,128]{1,0:T(8,128)S(1)} %bitcast.11, f32[6,128]{1,0:T(8,128)S(1)} %get-tuple-element.24.refs_2_.refs_3_.small_ref, bf16[4,8,128,128]{3,2,1,0:T(8,128)(2,1)S(1)} %get-tuple-element.25.refs_3_.refs_4_.feat_ref, ...), custom_call_target="tpu_custom_call" | custom-call | flops 4831838208 | bytes 4194304 | tf_op jit(solution)/shard_map/second/pallas_call | solution.py:360
Async XLA Ops:
  3.3 18.1 %collective-permute-start = (bf16[2,8,128,128]{3,2,1,0:T(8,128)(2,1)S(1)}, bf16[2,8,128,128]{3,2,1,0:T(8,128)(2,1)S(1)}, u32[]{:S(2)}, u32[]{:S(2)}) collective-permute-start(bf16[2,8,128,128]{3,2,1,0:T(8,128)(2,1)S(1)} %get-tuple-element.21), channel_id=1, source_target_pairs={{0,32},{32,64},{64,96},{96,128},{128,160},{160,192},{192,224},{224... | collective-permute-start | bytes 1572872 | tf_op jit(solution)/shard_map/ppermute | solution.py:334
  5.9 28.1 %collective-permute-start.1 = (bf16[4,2,128,128]{3,2,1,0:T(8,128)(2,1)}, bf16[4,2,128,128]{3,2,1,0:T(8,128)(2,1)S(1)}, u32[]{:S(2)}, u32[]{:S(2)}) collective-permute-start(bf16[4,2,128,128]{3,2,1,0:T(8,128)(2,1)} %get-tuple-element.26), channel_id=1, source_target_pairs={{0,1},{1,0},{2,3},{3,2},{4,5},{5,4},{6,7},{7,6},{8,9},{9,8},{10,11... | collective-permute-start | bytes 786440 | tf_op jit(solution)/shard_map/ppermute | solution.py:335
  6.8 27.2 %collective-permute-start.2 = (bf16[4,2,128,128]{3,2,1,0:T(8,128)(2,1)}, bf16[4,2,128,128]{3,2,1,0:T(8,128)(2,1)S(1)}, u32[]{:S(2)}, u32[]{:S(2)}) collective-permute-start(bf16[4,2,128,128]{3,2,1,0:T(8,128)(2,1)} %get-tuple-element.27), channel_id=1, source_target_pairs={{1,2},{3,4},{5,6},{7,8},{9,10},{11,12},{13,14},{15,16},{17,18},{19... | collective-permute-start | bytes 786440 | tf_op jit(solution)/shard_map/ppermute | solution.py:336
  7.9 26.1 %all-to-all-start = ((f32[256,1,128]{2,1,0:T(1,128)}), f32[256,1,128]{2,1,0:T(1,128)S(1)}, u32[]{:S(2)}, u32[]{:S(2)}) async-start(f32[256,1,128]{2,1,0:T(1,128)} %bitcast.3), calls=%async_computation | async-start | bytes 262144 | tf_op jit(solution)/shard_map/all_to_all | solution.py:337
  23.4 15.2 %collective-permute-start.3 = (bf16[2,2,128,128]{3,2,1,0:T(8,128)(2,1)}, bf16[2,2,128,128]{3,2,1,0:T(8,128)(2,1)S(1)}, u32[]{:S(2)}, u32[]{:S(2)}) collective-permute-start(bf16[2,2,128,128]{3,2,1,0:T(8,128)(2,1)} %get-tuple-element.31), channel_id=1, source_target_pairs={{0,1},{1,0},{2,3},{3,2},{4,5},{5,4},{6,7},{7,6},{8,9},{9,8},{10,11... | collective-permute-start | bytes 393224 | tf_op jit(solution)/shard_map/ppermute | solution.py:343
  25.1 13.4 %collective-permute-start.4 = (bf16[2,2,128,128]{3,2,1,0:T(8,128)(2,1)}, bf16[2,2,128,128]{3,2,1,0:T(8,128)(2,1)S(1)}, u32[]{:S(2)}, u32[]{:S(2)}) collective-permute-start(bf16[2,2,128,128]{3,2,1,0:T(8,128)(2,1)} %get-tuple-element.32), channel_id=1, source_target_pairs={{1,2},{3,4},{5,6},{7,8},{9,10},{11,12},{13,14},{15,16},{17,18},{19... | collective-permute-start | bytes 393224 | tf_op jit(solution)/shard_map/ppermute | solution.py:344
  37.9 23.1 %collective-permute-start.5 = (bf16[2,10,128,128]{3,2,1,0:T(8,128)(2,1)S(1)}, bf16[2,10,128,128]{3,2,1,0:T(8,128)(2,1)S(1)}, u32[]{:S(2)}, u32[]{:S(2)}) collective-permute-start(bf16[2,10,128,128]{3,2,1,0:T(8,128)(2,1)S(1)} %get-tuple-element.36), channel_id=1, source_target_pairs={{0,32},{32,64},{64,96},{96,128},{128,160},{160,192},{192,224},{224... | collective-permute-start | bytes 1966088 | tf_op jit(solution)/shard_map/ppermute | solution.py:352
  38.6 22.4 %copy-start = (bf16[3,3,3,128,128]{4,3,2,1,0:T(8,128)(2,1)S(1)}, bf16[3,3,3,128,128]{4,3,2,1,0:T(8,128)(2,1)}, u32[]{:S(2)}) copy-start(bf16[3,3,3,128,128]{4,3,2,1,0:T(8,128)(2,1)} %param.16) | copy-start | bytes 2654212

commit v10 on v8

--- a/solution.py
+++ b/solution.py
@@ -126,11 +126,9 @@
             put(o, at + r, centre[here, o * 128 : (o + 1) * 128] + left + right)
 
 
-def stats_kernel(x_hbm, *refs):
-    small, (x_ref, pay_ref, z_ref, in_ref, far_ref, small_ref, sems) = refs[:6], refs[6:]
+def stats_kernel(x_hbm, x_ref, pay_ref, z_ref, in_ref, far_ref, sems):
     frames, per = x_ref.shape[:2]
     copies = [pltpu.make_async_copy(x_hbm.at[f], x_ref.at[f], sems.at[f]) for f in range(frames)]
-    copies += [pltpu.make_async_copy(v, small_ref.at[i], sems.at[frames + i]) for i, v in enumerate(small)]
     for copy in copies:
         copy.start()
     odd = (lax.axis_index("space") & 1) == 1
@@ -148,19 +146,21 @@
     sums = shifted_sums(lambda i: load(per + i), (frames - 1) * per, mean)
     mean, spread = joined(mean, spread, cells, *sums, (frames - 1) * cells)
     pay_ref[...] = jnp.broadcast_to(payload(mean, spread)[:1], pay_ref.shape)
-    for copy in copies[frames:]:
-        copy.wait()
-
-
-def pack_kernel(kernel_hbm, z_ref, near_ref, far_ref, kernel_ref, sem):
-    fetch = pltpu.make_async_copy(kernel_hbm, kernel_ref, sem)
-    fetch.start()
+
+
+def pack_kernel(kernel_hbm, *refs):
+    small, (z_ref, near_ref, far_ref, kernel_ref, small_ref, sems) = refs[:6], refs[6:]
+    fetch = [pltpu.make_async_copy(v, small_ref.at[i], sems.at[i]) for i, v in enumerate(small)]
+    fetch.append(pltpu.make_async_copy(kernel_hbm, kernel_ref, sems.at[6]))
+    for copy in fetch:
+        copy.start()
     per = z_ref.shape[1]
     odd = lax.axis_index("space") & 1
     for f in range(2):
         near_ref[f] = z_ref[f, pl.ds((1 - odd) * (per - 2), 2)]
         far_ref[f] = z_ref[f, pl.ds(odd * (per - 2), 2)]
-    fetch.wait()
+    for copy in fetch:
+        copy.wait()
 
 
 def norm_constants(got_ref, small_ref, at, cells):
@@ -314,25 +314,25 @@
     taps_two = kernel_two.reshape(3, 9 * 128, 128)
 
     taps_one = in_hbm(taps_one)
-    x, pay, z_send, in_send, far_send, small = pl.pallas_call(
+    x, pay, z_send, in_send, far_send = pl.pallas_call(
         stats_kernel,
         out_shape=[
             shape((4, 8, 128, 128), BF16), shape((devices, 128), F32), shape((2, 8, 128, 128), BF16),
-            pltpu.HBM((4, 2, 128, 128), BF16), pltpu.HBM((4, 2, 128, 128), BF16), shape((6, 128), F32),
+            pltpu.HBM((4, 2, 128, 128), BF16), pltpu.HBM((4, 2, 128, 128), BF16),
         ],
-        in_specs=[HBM] * 7, out_specs=[VMEM] * 6,
-        scratch_shapes=[DMA((10,))], compiler_params=PARAMS,
+        in_specs=[HBM], out_specs=[VMEM] * 5,
+        scratch_shapes=[DMA((4,))], compiler_params=PARAMS,
         cost_estimate=pl.CostEstimate(flops=1 << 22, bytes_accessed=1 << 20, transcendentals=0), name="stats",
-    )(*map(in_hbm, (features, gain_one, shift_one, bias_one, gain_two, shift_two, bias_two)))
+    )(in_hbm(features))
     z_one = lax.ppermute(z_send, "tm", later)
     near = lax.ppermute(in_send, "space", swap_in)
     far = lax.ppermute(far_send, "space", swap_far)
     got = lax.all_to_all(pay, BOTH, 0, 0)
-    near_send, far_send, taps_one = pl.pallas_call(
-        pack_kernel, out_shape=[pltpu.HBM((2, 2, 128, 128), BF16)] * 2 + [shape((3, 9 * 128, 128), BF16)],
-        in_specs=[HBM, VMEM], out_specs=[VMEM] * 3, scratch_shapes=[DMA], compiler_params=PARAMS,
+    near_send, far_send, taps_one, small = pl.pallas_call(
+        pack_kernel, out_shape=[pltpu.HBM((2, 2, 128, 128), BF16)] * 2 + [shape((3, 9 * 128, 128), BF16), shape((6, 128), F32)],
+        in_specs=[HBM] * 7 + [VMEM], out_specs=[VMEM] * 4, scratch_shapes=[DMA((7,))], compiler_params=PARAMS,
         cost_estimate=pl.CostEstimate(flops=0, bytes_accessed=1 << 19, transcendentals=0), name="pack",
-    )(taps_one, z_one)
+    )(taps_one, *map(in_hbm, (gain_one, shift_one, bias_one, gain_two, shift_two, bias_two)), z_one)
     z_near = lax.ppermute(near_send, "space", swap_in)
     z_far = lax.ppermute(far_send, "space", swap_far)
     inner_a, send, consts = pl.pallas_call(

time: 66.6 us -> 66.4 us (level)
  no operation moved by 1% of the time
where the time goes in v10:
time: 66.4 us; the launch traced here: 66.2 us
  starting transfers between devices  20.9 us (31%)
  blocking collectives  19.1 us (29%)
  Pallas kernels  17.6 us (27%)
  waiting for transfers between devices  8.46 us (13%)
    all_to_all x1, blocking collectives, shards(): got = lax.all_to_all(pay, BOTH, 0, 0)  19.1 us
    all_to_all x1, starting transfers between devices, shards(): got = lax.all_to_all(pay, BOTH, 0, 0)  13.1 us
    all_to_all x1, waiting for transfers between devices, shards(): got = lax.all_to_all(pay, BOTH, 0, 0)  8 us
    pallas_call x1, Pallas kernels, shards(): pl.pallas_call(functools.partial(second_kernel, cells, strips), out_shape...  5.77 us
    pallas_call x1, Pallas kernels, shards(): pl.pallas_call(functools.partial(first_kernel, False, cells, strips), out...  3.82 us
    pallas_call x1, Pallas kernels, shards(): pl.pallas_call(functools.partial(first_kernel, True, cells, strips), out_...  3.35 us
    pallas_call x1, Pallas kernels, shards(): pl.pallas_call(stats_kernel, out_shape=[shape((4, 8, 128, 128), BF16), sh...  2.65 us
    ppermute x1, starting transfers between devices, shards(): z_one = lax.ppermute(z_send, 'tm', later)  2.54 us
  transfers between devices with their start and end apart: 7, of which 2 were waited for; matrix products, arithmetic and copies ran while one was open for 0% of the time, Pallas kernels for 14%

profile of v10, /device:TPU:1, one launch (start us, length us, event | category | flops | bytes accessed | tf_op | source)
XLA Modules:
  0.0 66.2 jit_solution(1324656069544217244)
XLA Ops:
  0.0 2.6 %stats.1 = (bf16[4,8,128,128]{3,2,1,0:T(8,128)(2,1)S(1)}, f32[256,128]{1,0:T(8,128)}, bf16[2,8,128,128]{3,2,1,0:T(8,128)(2,1)S(1)}, bf16[4,2,128,128]{3,2,1,0:T(8,128)(2,1)}, bf16[4,2,128,128]{3,2,1,0:T(8,128)(2,1)}) custom-call(bf16[4,8,128,128]{3,2,1,0:T(8,128)(2,1)} %x_hbm.1), custom_call_target="tpu_custom_call" | custom-call | flops 4194304 | bytes 1048576 | tf_op jit(solution)/shard_map/stats/pallas_call | solution.py:317
  2.7 2.5 %collective-permute-start = (bf16[2,8,128,128]{3,2,1,0:T(8,128)(2,1)S(1)}, bf16[2,8,128,128]{3,2,1,0:T(8,128)(2,1)S(1)}, u32[]{:S(2)}, u32[]{:S(2)}) collective-permute-start(bf16[2,8,128,128]{3,2,1,0:T(8,128)(2,1)S(1)} %get-tuple-element.19), channel_id=1, source_target_pairs={{0,32},{32,64},{64,96},{96,128},{128,160},{160,192},{192,224},{224... | collective-permute-start | bytes 1572872 | tf_op jit(solution)/shard_map/ppermute | solution.py:327
  5.2 1.0 %collective-permute-start.1 = (bf16[4,2,128,128]{3,2,1,0:T(8,128)(2,1)}, bf16[4,2,128,128]{3,2,1,0:T(8,128)(2,1)S(1)}, u32[]{:S(2)}, u32[]{:S(2)}) collective-permute-start(bf16[4,2,128,128]{3,2,1,0:T(8,128)(2,1)} %get-tuple-element.24), channel_id=1, source_target_pairs={{0,1},{1,0},{2,3},{3,2},{4,5},{5,4},{6,7},{7,6},{8,9},{9,8},{10,11... | collective-permute-start | bytes 786440 | tf_op jit(solution)/shard_map/ppermute | solution.py:328
  6.2 1.1 %collective-permute-start.2 = (bf16[4,2,128,128]{3,2,1,0:T(8,128)(2,1)}, bf16[4,2,128,128]{3,2,1,0:T(8,128)(2,1)S(1)}, u32[]{:S(2)}, u32[]{:S(2)}) collective-permute-start(bf16[4,2,128,128]{3,2,1,0:T(8,128)(2,1)} %get-tuple-element.25), channel_id=1, source_target_pairs={{1,2},{3,4},{5,6},{7,8},{9,10},{11,12},{13,14},{15,16},{17,18},{19... | collective-permute-start | bytes 786440 | tf_op jit(solution)/shard_map/ppermute | solution.py:329
  7.3 13.1 %all-to-all-start = ((f32[256,1,128]{2,1,0:T(1,128)}), f32[256,1,128]{2,1,0:T(1,128)S(1)}, u32[]{:S(2)}, u32[]{:S(2)}) async-start(f32[256,1,128]{2,1,0:T(1,128)} %bitcast.3), calls=%async_computation | async-start | bytes 262144 | tf_op jit(solution)/shard_map/all_to_all | solution.py:330
  20.3 0.4 collective-permute-done.refs_6_
  20.8 2.0 %pack.1 = (bf16[2,2,128,128]{3,2,1,0:T(8,128)(2,1)}, bf16[2,2,128,128]{3,2,1,0:T(8,128)(2,1)}, bf16[3,1152,128]{2,1,0:T(8,128)(2,1)S(1)}, f32[6,128]{1,0:T(8,128)S(1)}) custom-call(bf16[3,1152,128]{2,1,0:T(8,128)(2,1)} %bitcast.14, f32[128]{0:T(128)} %refs_0_.1, f32[128]{0:T(128)} %refs_1_.1, f32[128]{0:T(128)} %refs_2_.1, f32[128]{0:T(128)} %refs_3_.1, ...), custom_call_target="tpu_custom_call" | custom-call | bytes 524288 | tf_op jit(solution)/shard_map/pack/pallas_call | solution.py:331
  22.8 1.8 %collective-permute-start.3 = (bf16[2,2,128,128]{3,2,1,0:T(8,128)(2,1)}, bf16[2,2,128,128]{3,2,1,0:T(8,128)(2,1)S(1)}, u32[]{:S(2)}, u32[]{:S(2)}) collective-permute-start(bf16[2,2,128,128]{3,2,1,0:T(8,128)(2,1)} %get-tuple-element.27), channel_id=1, source_target_pairs={{0,1},{1,0},{2,3},{3,2},{4,5},{5,4},{6,7},{7,6},{8,9},{9,8},{10,11... | collective-permute-start | bytes 393224 | tf_op jit(solution)/shard_map/ppermute | solution.py:336
  24.6 0.7 %collective-permute-start.4 = (bf16[2,2,128,128]{3,2,1,0:T(8,128)(2,1)}, bf16[2,2,128,128]{3,2,1,0:T(8,128)(2,1)S(1)}, u32[]{:S(2)}, u32[]{:S(2)}) collective-permute-start(bf16[2,2,128,128]{3,2,1,0:T(8,128)(2,1)} %get-tuple-element.28), channel_id=1, source_target_pairs={{1,2},{3,4},{5,6},{7,8},{9,10},{11,12},{13,14},{15,16},{17,18},{19... | collective-permute-start | bytes 393224 | tf_op jit(solution)/shard_map/ppermute | solution.py:337
  25.3 8.0 %all-to-all-done = f32[256,1,128]{2,1,0:T(1,128)S(1)} async-done(((f32[256,1,128]{2,1,0:T(1,128)}), f32[256,1,128]{2,1,0:T(1,128)S(1)}, u32[]{:S(2)}, u32[]{:S(2)}) %all-to-all-start) | async-done | bytes 131104 | tf_op jit(solution)/shard_map/all_to_all | solution.py:330
  33.3 0.0 collective-permute-done.1.refs_4_
  33.3 0.0 collective-permute-done.2.refs_5_
  33.3 3.8 %first_late.1 = (f32[2,10,128,128]{3,2,1,0:T(8,128)S(1)}, bf16[2,10,128,128]{3,2,1,0:T(8,128)(2,1)S(1)}, f32[8,128]{1,0:T(8,128)S(1)}) custom-call(bf16[3,1152,128]{2,1,0:T(8,128)(2,1)S(1)} %get-tuple-element.20.refs_0_, f32[256,128]{1,0:T(8,128)S(1)} %bitcast.10, f32[6,128]{1,0:T(8,128)S(1)} %get-tuple-element.22.refs_2_.small_ref, ...), custom_call_target="tpu_custom_call" | custom-call | flops 3019898880 | bytes 4194304 | tf_op jit(solution)/shard_map/first_late/pallas_call | solution.py:338
  37.2 0.7 %collective-permute-start.5 = (bf16[2,10,128,128]{3,2,1,0:T(8,128)(2,1)S(1)}, bf16[2,10,128,128]{3,2,1,0:T(8,128)(2,1)S(1)}, u32[]{:S(2)}, u32[]{:S(2)}) collective-permute-start(bf16[2,10,128,128]{3,2,1,0:T(8,128)(2,1)S(1)} %get-tuple-element.32), channel_id=1, source_target_pairs={{0,32},{32,64},{64,96},{96,128},{128,160},{160,192},{192,224},{224... | collective-permute-start | bytes 1966088 | tf_op jit(solution)/shard_map/ppermute | solution.py:344
  37.8 0.0 collective-permute-done.3.refs_7_
  37.8 0.0 collective-permute-done.4.refs_8_
  37.8 0.0 copy-start
  37.9 3.3 %first_early.1 = (f32[2,10,128,128]{3,2,1,0:T(8,128)S(1)}, f32[256,128]{1,0:T(8,128)S(1)}) custom-call(bf16[3,1152,128]{2,1,0:T(8,128)(2,1)S(1)} %get-tuple-element.20.refs_0_, f32[8,128]{1,0:T(8,128)S(1)} %get-tuple-element.26.refs_1_, f32[6,128]{1,0:T(8,128)S(1)} %get-tuple-element.22.refs_2_.small_ref, ...), custom_call_target="tpu_custom_call" | custom-call | flops 3019898880 | bytes 4194304 | tf_op jit(solution)/shard_map/first_early/pallas_call | solution.py:345
  41.2 19.1 %all_to_all.22 = f32[256,1,128]{2,1,0:T(1,128)S(1)} all-to-all(f32[256,1,128]{2,1,0:T(1,128)S(1)} %bitcast.12), channel_id=1, replica_groups=mesh['tm'=8,'space'=32] {'tm','space'}, dimensions={0} | all-to-all | bytes 262144 | tf_op jit(solution)/shard_map/all_to_all | solution.py:351
  60.3 0.0 collective-permute-done.5.z_ref
  60.3 0.0 copy-done
  60.3 5.8 %second.1 = f32[4,8,128,128]{3,2,1,0:T(8,128)} custom-call(bf16[3,1152,128]{2,1,0:T(8,128)(2,1)S(1)} %bitcast.13, f32[256,128]{1,0:T(8,128)S(1)} %bitcast.11, f32[6,128]{1,0:T(8,128)S(1)} %get-tuple-element.22.refs_2_.small_ref, bf16[4,8,128,128]{3,2,1,0:T(8,128)(2,1)S(1)} %get-tuple-element.23.refs_3_.feat_ref, ...), custom_call_target="tpu_custom_call" | custom-call | flops 4831838208 | bytes 4194304 | tf_op jit(solution)/shard_map/second/pallas_call | solution.py:352
Async XLA Ops:
  2.7 18.1 %collective-permute-start = (bf16[2,8,128,128]{3,2,1,0:T(8,128)(2,1)S(1)}, bf16[2,8,128,128]{3,2,1,0:T(8,128)(2,1)S(1)}, u32[]{:S(2)}, u32[]{:S(2)}) collective-permute-start(bf16[2,8,128,128]{3,2,1,0:T(8,128)(2,1)S(1)} %get-tuple-element.19), channel_id=1, source_target_pairs={{0,32},{32,64},{64,96},{96,128},{128,160},{160,192},{192,224},{224... | collective-permute-start | bytes 1572872 | tf_op jit(solution)/shard_map/ppermute | solution.py:327
  5.2 28.1 %collective-permute-start.1 = (bf16[4,2,128,128]{3,2,1,0:T(8,128)(2,1)}, bf16[4,2,128,128]{3,2,1,0:T(8,128)(2,1)S(1)}, u32[]{:S(2)}, u32[]{:S(2)}) collective-permute-start(bf16[4,2,128,128]{3,2,1,0:T(8,128)(2,1)} %get-tuple-element.24), channel_id=1, source_target_pairs={{0,1},{1,0},{2,3},{3,2},{4,5},{5,4},{6,7},{7,6},{8,9},{9,8},{10,11... | collective-permute-start | bytes 786440 | tf_op jit(solution)/shard_map/ppermute | solution.py:328
  6.2 27.2 %collective-permute-start.2 = (bf16[4,2,128,128]{3,2,1,0:T(8,128)(2,1)}, bf16[4,2,128,128]{3,2,1,0:T(8,128)(2,1)S(1)}, u32[]{:S(2)}, u32[]{:S(2)}) collective-permute-start(bf16[4,2,128,128]{3,2,1,0:T(8,128)(2,1)} %get-tuple-element.25), channel_id=1, source_target_pairs={{1,2},{3,4},{5,6},{7,8},{9,10},{11,12},{13,14},{15,16},{17,18},{19... | collective-permute-start | bytes 786440 | tf_op jit(solution)/shard_map/ppermute | solution.py:329
  7.3 26.1 %all-to-all-start = ((f32[256,1,128]{2,1,0:T(1,128)}), f32[256,1,128]{2,1,0:T(1,128)S(1)}, u32[]{:S(2)}, u32[]{:S(2)}) async-start(f32[256,1,128]{2,1,0:T(1,128)} %bitcast.3), calls=%async_computation | async-start | bytes 262144 | tf_op jit(solution)/shard_map/all_to_all | solution.py:330
  22.8 15.0 %collective-permute-start.3 = (bf16[2,2,128,128]{3,2,1,0:T(8,128)(2,1)}, bf16[2,2,128,128]{3,2,1,0:T(8,128)(2,1)S(1)}, u32[]{:S(2)}, u32[]{:S(2)}) collective-permute-start(bf16[2,2,128,128]{3,2,1,0:T(8,128)(2,1)} %get-tuple-element.27), channel_id=1, source_target_pairs={{0,1},{1,0},{2,3},{3,2},{4,5},{5,4},{6,7},{7,6},{8,9},{9,8},{10,11... | collective-permute-start | bytes 393224 | tf_op jit(solution)/shard_map/ppermute | solution.py:336
  24.6 13.2 %collective-permute-start.4 = (bf16[2,2,128,128]{3,2,1,0:T(8,128)(2,1)}, bf16[2,2,128,128]{3,2,1,0:T(8,128)(2,1)S(1)}, u32[]{:S(2)}, u32[]{:S(2)}) collective-permute-start(bf16[2,2,128,128]{3,2,1,0:T(8,128)(2,1)} %get-tuple-element.28), channel_id=1, source_target_pairs={{1,2},{3,4},{5,6},{7,8},{9,10},{11,12},{13,14},{15,16},{17,18},{19... | collective-permute-start | bytes 393224 | tf_op jit(solution)/shard_map/ppermute | solution.py:337
  37.2 23.1 %collective-permute-start.5 = (bf16[2,10,128,128]{3,2,1,0:T(8,128)(2,1)S(1)}, bf16[2,10,128,128]{3,2,1,0:T(8,128)(2,1)S(1)}, u32[]{:S(2)}, u32[]{:S(2)}) collective-permute-start(bf16[2,10,128,128]{3,2,1,0:T(8,128)(2,1)S(1)} %get-tuple-element.32), channel_id=1, source_target_pairs={{0,32},{32,64},{64,96},{96,128},{128,160},{160,192},{192,224},{224... | collective-permute-start | bytes 1966088 | tf_op jit(solution)/shard_map/ppermute | solution.py:344
  37.8 22.4 %copy-start = (bf16[3,3,3,128,128]{4,3,2,1,0:T(8,128)(2,1)S(1)}, bf16[3,3,3,128,128]{4,3,2,1,0:T(8,128)(2,1)}, u32[]{:S(2)}) copy-start(bf16[3,3,3,128,128]{4,3,2,1,0:T(8,128)(2,1)} %param.16) | copy-start | bytes 2654212
